TPU v7x, 512 devices: a whole 4x4x16 slice. The times are simulated.
512 devices in a mesh: tp: 8 (over y, core), ad: 64 (over z, x).
Axes of the slice: x: 4, y: 4, z: 16, core: 2. Of those that a mesh axis runs over, the one named last changes fastest.
Arguments:
- tokens: bfloat16 [16384, 4096], P('ad', 'tp'), may hold values from -6 to 6
- key_value_weight: bfloat16 [4096, 2048], P('tp'), may hold values from -0.09375 to 0.09375
- adapter_down_weight: bfloat16 [512, 32, 4096], P('ad', None, 'tp'), may hold values from -0.09375 to 0.09375
- adapter_up_weight: bfloat16 [512, 16, 2048], P('ad', None, 'tp'), may hold values from -1.5 to 1.5
- request_adapter_index: int32 [4096], P('ad'), may hold values from 0 to 511, as said below
- lengths: int32 [64, 64], P('ad'), may hold values from 1 to 8, 256 in all within a row
Outputs:
- mixed: bfloat16 [16384, 2048], P('ad', 'tp')
Inputs may be any that keep to these rules, and one draw needn't show every extreme that they name: `request_adapter_index`: owner o stores adapters o * 8 to (o+1) * 8 - 1. Among the 64 requests of one token group, the adapters of exactly one owner are named by exactly 2 requests and those of every other owner by at most one.
All inputs are finite; a program needn't handle non-finite values.
Results may differ from a plain program's by a relative error of at most 0.018.
Values may be sent and summed in bfloat16 or wider, within the bound.
No kernel may reach another device: no remote copies, remote signals or barrier semaphores. Data moves between devices by JAX's collectives and lax.ppermute only.
A program may use at most 64 MiB of HBM per device.

v0:
```python
import jax
import jax.numpy as jnp
from jax import lax
from jax.sharding import PartitionSpec as P

OWNER_SLOTS = 2


ADAPTER_SCALE = 2.0


def local(
    tokens, key_value_weight, adapter_down_weight, adapter_up_weight, request_adapter_index, lengths
):
    tok_rows, width = tokens.shape
    n_ad = lax.axis_size("ad")
    n_tp = lax.axis_size("tp")
    stored_factors = adapter_down_weight.shape[0]
    doubled_rank = adapter_down_weight.shape[1]
    rank_rows = adapter_up_weight.shape[1]
    column_range = adapter_up_weight.shape[2]
    half_cols = column_range * n_tp // 2
    requests = request_adapter_index.shape[0]
    slots = n_ad * OWNER_SLOTS
    longest = 2 * tok_rows // n_ad
    lens = lengths[0]
    ends = jnp.cumsum(lens)
    starts = ends - lens
    owner = request_adapter_index // stored_factors
    inside = request_adapter_index % stored_factors
    order = jnp.arange(requests, dtype=jnp.int32)
    earlier = (owner[:, None] == owner[None, :]) & (order[None, :] < order[:, None])
    slot_of = owner * OWNER_SLOTS + jnp.sum(earlier.astype(jnp.int32), axis=1)
    hits = slot_of[None, :] == jnp.arange(slots, dtype=jnp.int32)[:, None]
    slot_used = jnp.any(hits, axis=1)
    slot_req = jnp.sum(jnp.where(hits, order[None, :], 0), axis=1)
    slot_ids = jnp.sum(jnp.where(hits, inside[None, :], 0), axis=1)
    offsets = jnp.arange(longest, dtype=jnp.int32)
    live = slot_used[:, None] & (offsets[None, :] < lens[slot_req][:, None])
    take = jnp.where(live, starts[slot_req][:, None] + offsets[None, :], 0)
    slot_rows = jnp.where(live[:, :, None], tokens[take], jnp.zeros((), tokens.dtype))
    positions = jnp.arange(tok_rows, dtype=jnp.int32)
    request_of = jnp.sum((positions[:, None] >= ends[None, :]).astype(jnp.int32), axis=1)
    back = slot_of[request_of] * longest + positions - starts[request_of]
    wanted_rows = lax.all_to_all(
        slot_ids.reshape(n_ad, OWNER_SLOTS), "ad", split_axis=0, concat_axis=0, tiled=True
    )
    selected_up_factor = adapter_up_weight[wanted_rows]
    down_got, up_got = (
        lax.all_to_all(
            adapter_down_weight[wanted_rows], "ad", split_axis=0, concat_axis=0, tiled=True
        ),
        lax.all_to_all(selected_up_factor, "ad", split_axis=0, concat_axis=0, tiled=True),
    )
    low_slots = jnp.einsum(
        "smd,scd->smc",
        slot_rows,
        down_got.reshape(slots, doubled_rank, width),
        preferred_element_type=jnp.float32,
    )
    partial_value = jnp.dot(tokens, key_value_weight, preferred_element_type=jnp.float32)
    base_output = lax.psum_scatter(
        partial_value.astype(jnp.bfloat16), "tp", scatter_dimension=1, tiled=True
    ).astype(jnp.float32)
    low_tokens = low_slots.reshape(slots * longest, doubled_rank)[back]
    low = lax.psum(low_tokens.astype(jnp.bfloat16), "tp").astype(jnp.float32)
    half = lax.axis_index("tp") * column_range // half_cols
    low_half = lax.dynamic_slice_in_dim(low, half * rank_rows, rank_rows, 1)
    low_padded = jnp.where(live[:, :, None], low_half[take], jnp.float32(0.0))
    up_float = up_got.reshape(slots, rank_rows, column_range).astype(jnp.float32)
    delta_slots = jnp.einsum("smc,sck->smk", low_padded, up_float, precision=lax.Precision.HIGHEST)
    adapter_delta = delta_slots.reshape(slots * longest, column_range)[back]
    return (base_output + ADAPTER_SCALE * adapter_delta).astype(jnp.bfloat16)


def solution(mesh):
    return jax.shard_map(
        local,
        mesh=mesh,
        in_specs=(
            P("ad", "tp"),
            P("tp", None),
            P("ad", None, "tp"),
            P("ad", None, "tp"),
            P("ad"),
            P("ad", None),
        ),
        out_specs=P("ad", "tp"),
        check_vma=False,
    )
```

profile of v0, /device:TPU:6, one launch (start us, length us, event | category | flops | bytes accessed | tf_op | source)
XLA Modules:
  0.0 312.2 jit_solution(7859275561999897293)
XLA Ops:
  6.5 0.0 copy-start
  6.5 0.8 and_select_fusion
  7.4 0.2 convert_reduce_fusion.1
  7.5 0.1 select_reduce_fusion.1
  7.6 0.1 all_to_all.14
  7.8 31.0 %all_to_all.22 = s32[64,1,2]{2,1,0:T(1,128)S(1)} all-to-all(s32[64,1,2]{2,1,0:T(1,128)S(1)} %bitcast.41), channel_id=1, replica_groups=mesh['tp'=8,'ad'=64] {'ad'}, dimensions={0} | all-to-all | bytes 1024 | tf_op jit(solution)/shard_map/all_to_all | solution.py:45
  38.8 0.1 copy.19
  38.8 0.1 copy.20
  38.9 0.1 reshape.291
  39.1 3.7 %gather_fusion.3 = bf16[128,32,512]{2,1,0:T(8,128)(2,1)} fusion(bf16[8,32,512]{2,1,0:T(8,128)(2,1)} %param.8, s32[1024]{0:T(1024)S(1)} %pad_clamp_fusion.2), kind=kCustom, calls=%fused_computation.3 | custom fusion | bytes 8389120 | tf_op jit(solution)/shard_map/gather | solution.py:51
  42.8 0.0 copy-start.3
  42.8 7.6 %all-to-all-start.1 = ((bf16[64,2,32,512]{3,2,1,0:T(8,128)(2,1)}), bf16[64,2,32,512]{3,2,1,0:T(8,128)(2,1)}, u32[]{:S(2)}, u32[]{:S(2)}) async-start(bf16[64,2,32,512]{3,2,1,0:T(8,128)(2,1)} %bitcast.39), calls=%async_computation.2 | async-start | bytes 8388608 | tf_op jit(solution)/shard_map/all_to_all | solution.py:50
  50.5 0.0 copy-done.3
  50.5 0.0 copy-start.2
  50.5 0.0 copy-start.1
  50.5 1.7 gather_fusion.8
  52.2 187.1 %all-to-all-done.1 = bf16[64,2,32,512]{3,2,1,0:T(8,128)(2,1)} async-done(((bf16[64,2,32,512]{3,2,1,0:T(8,128)(2,1)}), bf16[64,2,32,512]{3,2,1,0:T(8,128)(2,1)}, u32[]{:S(2)}, u32[]{:S(2)}) %all-to-all-start.1) | async-done | bytes 4194336 | tf_op jit(solution)/shard_map/all_to_all | solution.py:50
  239.4 5.9 %all-to-all-start.2 = ((bf16[64,2,16,256]{3,2,1,0:T(8,128)(2,1)}), bf16[64,2,16,256]{3,2,1,0:T(8,128)(2,1)S(1)}, u32[]{:S(2)}, u32[]{:S(2)}) async-start(bf16[64,2,16,256]{3,2,1,0:T(8,128)(2,1)} %bitcast.16), calls=%async_computation.3 | async-start | bytes 2097152 | tf_op jit(solution)/shard_map/all_to_all | solution.py:53
  245.3 0.0 reduce-scatter.2.cloned.1.call-start
  245.4 0.0 copy-done
  245.4 0.0 copy-done.2
  245.4 1.7 convolution_convert_fusion
  247.1 0.0 reduce-scatter.2.cloned.1.call-update
  247.1 0.0 copy-done.1
  247.1 0.1 copy.17
  247.2 0.1 reduce-window.8
  247.3 0.1 reduce
  247.5 0.1 convert_reduce_fusion
  247.6 1.9 gather_fusion.4
  249.5 1.9 gather_fusion.5
  251.4 1.2 gather_fusion.1
  252.6 1.2 gather_fusion
  253.8 0.1 fusion.6
  253.9 0.1 compare_select_fusion
  254.1 0.1 reshape.283
  254.2 5.1 %gather_fusion.2 = bf16[1024,512]{1,0:T(8,128)(2,1)} fusion(bf16[256,512]{1,0:T(8,128)(2,1)S(1)} %copy-done.2, s32[1024]{0:T(1024)S(1)} %broadcast_clamp_fusion), kind=kCustom, calls=%fused_computation.2 | custom fusion | bytes 2101248 | tf_op jit(solution)/shard_map/gather | solution.py:41
  259.3 0.1 fusion.4
  259.4 3.8 %convolution_bitcast_fusion.1 = bf16[1024,32]{1,0:T(8,128)(2,1)S(1)} fusion(bf16[128,32,512]{2,1,0:T(8,128)(2,1)} %bitcast.8, bf16[1024,512]{1,0:T(8,128)(2,1)} %gather_fusion.2, pred[128,8]{1,0:T(8,128)(4,1)S(1)} %fusion.4), kind=kOutput, calls=%fused_computation.12 | convolution fusion | flops 34078720 | bytes 5309440 | tf_op jit(solution)/shard_map/smd,scd->smc/dot_general | solution.py:55
  263.1 0.9 gather_fusion.6
  264.0 26.2 %psum.7 = bf16[256,32]{1,0:T(8,128)(2,1)S(1)} all-reduce(bf16[256,32]{1,0:T(8,128)(2,1)S(1)} %gather_fusion.6), channel_id=1, replica_groups=mesh['tp'=8,'ad'=64] {'tp'}, use_global_device_ids=true, to_apply=%region_7.8 | all-reduce | flops 8192 | bytes 32768 | tf_op jit(solution)/shard_map/psum | solution.py:66
  290.2 0.1 dynamic-slice_convert_fusion
  290.3 4.0 %gather_fusion.7 = f32[1024,16]{1,0:T(8,128)} fusion(f32[256,16]{1,0:T(8,128)S(1)} %dynamic-slice_convert_fusion, s32[1024]{0:T(1024)S(1)} %broadcast_clamp_fusion), kind=kCustom, calls=%fused_computation.7 | custom fusion | bytes 135168 | tf_op jit(solution)/shard_map/gather | solution.py:69
  294.3 5.4 %all-to-all-done.2 = bf16[64,2,16,256]{3,2,1,0:T(8,128)(2,1)S(1)} async-done(((bf16[64,2,16,256]{3,2,1,0:T(8,128)(2,1)}), bf16[64,2,16,256]{3,2,1,0:T(8,128)(2,1)S(1)}, u32[]{:S(2)}, u32[]{:S(2)}) %all-to-all-start.2) | async-done | bytes 1048608 | tf_op jit(solution)/shard_map/all_to_all | solution.py:53
  299.7 0.0 copy-start.4
  299.7 1.0 copy-done.4
  300.7 2.0 convolution_bitcast_fusion
  302.7 1.0 gather_fusion.9
  303.7 0.0 reduce-scatter.2.cloned.1.call-done
  303.7 1.6 add_convert_fusion
  (12 shorter events, 0.1 us)
Async XLA Ops:
  6.5 238.8 %copy-start = (bf16[512,2048]{1,0:T(8,128)(2,1)S(1)}, bf16[512,2048]{1,0:T(8,128)(2,1)}, u32[]{:S(2)}) copy-start(bf16[512,2048]{1,0:T(8,128)(2,1)} %param.7) | copy-start | bytes 6291460
  42.8 7.7 %copy-start.3 = (bf16[8,16,256]{2,1,0:T(8,128)(2,1)S(1)}, bf16[8,16,256]{2,1,0:T(8,128)(2,1)}, u32[]{:S(2)}) copy-start(bf16[8,16,256]{2,1,0:T(8,128)(2,1)} %param.9) | copy-start | bytes 196612
  42.8 196.5 %all-to-all-start.1 = ((bf16[64,2,32,512]{3,2,1,0:T(8,128)(2,1)}), bf16[64,2,32,512]{3,2,1,0:T(8,128)(2,1)}, u32[]{:S(2)}, u32[]{:S(2)}) async-start(bf16[64,2,32,512]{3,2,1,0:T(8,128)(2,1)} %bitcast.39), calls=%async_computation.2 | async-start | bytes 8388608 | tf_op jit(solution)/shard_map/all_to_all | solution.py:50
  50.5 194.9 %copy-start.2 = (bf16[256,512]{1,0:T(8,128)(2,1)S(1)}, bf16[256,512]{1,0:T(8,128)(2,1)}, u32[]{:S(2)}) copy-start(bf16[256,512]{1,0:T(8,128)(2,1)} %param.6) | copy-start | bytes 786436
  50.5 196.6 %copy-start.1 = (s32[1,64]{1,0:T(1,128)S(1)}, s32[1,64]{1,0:T(1,128)}, u32[]{:S(2)}) copy-start(s32[1,64]{1,0:T(1,128)} %param.11) | copy-start | bytes 772
  239.4 60.3 %all-to-all-start.2 = ((bf16[64,2,16,256]{3,2,1,0:T(8,128)(2,1)}), bf16[64,2,16,256]{3,2,1,0:T(8,128)(2,1)S(1)}, u32[]{:S(2)}, u32[]{:S(2)}) async-start(bf16[64,2,16,256]{3,2,1,0:T(8,128)(2,1)} %bitcast.16), calls=%async_computation.3 | async-start | bytes 2097152 | tf_op jit(solution)/shard_map/all_to_all | solution.py:53
  245.3 58.4 %reduce-scatter.2.cloned.1.call-start = ((), (), s32[]{:S(2)}) async-start(), calls=%async_computation.4 | async-start | bytes 1179648 | tf_op jit(solution)/shard_map/reduce_scatter | solution.py:62
  299.7 1.0 copy-start.4
Sparse Core Ops, SparseCore 0:
  249.0 41.1 reduce-scatter.1
where the time goes:
time: 313 us; the launch traced here: 312 us
  waiting for transfers between devices  193 us (62%)
  blocking collectives  57.2 us (18%)
  local copies, waits for them, and re-layouts  24.2 us (8%)
  starting transfers between devices  13.6 us (4%)
  between operations  13.6 us (4%)
  matrix products  7.52 us (2%)
  other arithmetic  3.46 us (1%)
    all_to_all x1, waiting for transfers between devices, local(): lax.all_to_all(adapter_down_weight[wanted_rows], 'ad', split_axis=0, conc...  187 us
    all_to_all x1, blocking collectives, local(): lax.all_to_all(slot_ids.reshape(n_ad, OWNER_SLOTS), 'ad', split_axis=0, c...  31 us
    psum x1, blocking collectives, local(): low = lax.psum(low_tokens.astype(jnp.bfloat16), 'tp').astype(jnp.float32)  26.2 us
    all_to_all x1, starting transfers between devices, local(): lax.all_to_all(adapter_down_weight[wanted_rows], 'ad', split_axis=0, conc...  7.64 us
  transfers between devices with their start and end apart: 3, of which 2 were waited for; matrix products, arithmetic and copies ran while one was open for 9% of the time, Pallas kernels for 0%

commit v1 on v0

v1 whole, which is shorter than its diff:
```python
import jax
import jax.numpy as jnp
from jax import lax
from jax.experimental import pallas as pl
from jax.experimental.pallas import tpu as pltpu
from jax.sharding import PartitionSpec as P

ADAPTER_SCALE = 2.0
N_X = 4
MAXLEN = 8

F32 = jnp.float32
BF16 = jnp.bfloat16
NT = (((1,), (1,)), ((), ()))
TN = (((0,), (0,)), ((), ()))
VMEM_LIMIT = 48 * 1024 * 1024


def iota(shape, dimension):
    return lax.broadcasted_iota(jnp.int32, shape, dimension)


def pack_kernel(planes, cap, per_plane, lens_ref, index_ref, tokens_ref, send_ref, ids_ref, place_ref):
    requests = lens_ref.shape[1]
    rows = tokens_ref.shape[0]
    lens = lens_ref[...].astype(F32)
    index = index_ref[...].astype(F32)
    r0, r1 = iota((requests, requests), 0), iota((requests, requests), 1)
    ends = jnp.sum(jnp.where(r1 <= r0, lens, 0.0), axis=1, keepdims=True)
    starts = jnp.sum(jnp.where(r1 < r0, lens, 0.0), axis=1, keepdims=True)
    index_col = jnp.sum(jnp.where(r1 == r0, index, 0.0), axis=1, keepdims=True)
    t = iota((requests, rows), 1).astype(F32)
    inside = (t >= starts) & (t < ends)
    adapter = jnp.sum(jnp.where(inside, index_col, 0.0), axis=0, keepdims=True)
    plane = jnp.floor(adapter * (1.0 / per_plane))
    local = adapter - plane * per_plane
    member = iota((planes, rows), 0).astype(F32) == plane
    before = (iota((rows, rows), 0) < iota((rows, rows), 1)).astype(F32).astype(BF16)
    counts = jnp.dot(member.astype(F32).astype(BF16), before, preferred_element_type=F32)
    rank = jnp.sum(jnp.where(member, counts, 0.0), axis=0, keepdims=True)
    place = (plane * cap + rank).astype(jnp.int32)
    select = (iota((planes * cap, rows), 0) == place).astype(F32).astype(BF16)
    send_ref[...] = jnp.dot(select, tokens_ref[...], preferred_element_type=F32).astype(BF16)
    at_rank = (iota((ids_ref.shape[1], rows), 0).astype(F32) == rank).astype(F32).astype(BF16)
    ids_ref[...] = lax.dot_general(
        jnp.where(member, local, 0.0).astype(BF16), at_rank, NT, preferred_element_type=F32
    )
    place_ref[...] = jnp.broadcast_to(place, place_ref.shape)


def low_kernel(planes, cap, recv_ref, ids_ref, down_ref, out_ref, lane_ids_ref):
    rows = recv_ref.shape[0]
    doubled_rank = down_ref.shape[1]
    slot = ids_ref.shape[1]
    source = iota((planes, rows), 0)
    p = iota((planes, rows), 1)
    mine = (p >= source * cap) & (p < source * cap + cap)
    offset = jnp.sum(jnp.where(mine, p - source * cap, 0).astype(F32), axis=0, keepdims=True)
    spread = (iota((slot, rows), 0).astype(F32) == offset).astype(F32).astype(BF16)
    ids = jnp.dot(ids_ref[...].astype(BF16), spread, preferred_element_type=F32)
    ids = jnp.sum(jnp.where(mine, ids, 0.0), axis=0, keepdims=True)
    lane_ids_ref[...] = jnp.broadcast_to(ids, lane_ids_ref.shape)
    recv = recv_ref[...]
    adapters = down_ref.shape[0]
    step = 8
    low = jnp.zeros((doubled_rank, rows), F32)
    for first in range(0, adapters, step):
        block = down_ref[first : first + step].reshape(step * doubled_rank, -1)
        values = lax.dot_general(block, recv, NT, preferred_element_type=F32)
        for a in range(step):
            low = jnp.where(
                ids == float(first + a), values[a * doubled_rank : (a + 1) * doubled_rank], low
            )
    low = low.astype(BF16)
    n = out_ref.shape[0]
    rank = doubled_rank // 2
    for j in range(n):
        half = j * 2 // n
        out_ref[j] = low[half * rank : (half + 1) * rank]


def delta_kernel(parts_ref, lane_ids_ref, up_ref, out_ref):
    low = parts_ref[0].astype(F32)
    for j in range(1, parts_ref.shape[0]):
        low = low + parts_ref[j].astype(F32)
    ids = lane_ids_ref[0:1, :]
    adapters = up_ref.shape[0]
    spread = jnp.concatenate(
        [jnp.where(ids == float(a), low, 0.0).astype(BF16) for a in range(adapters)], axis=0
    )
    up = up_ref[...].reshape(spread.shape[0], -1)
    out_ref[...] = lax.dot_general(spread, up, TN, preferred_element_type=F32).astype(BF16)


def mix_kernel(place_ref, back_ref, base_ref, out_ref):
    rows = base_ref.shape[0]
    place = place_ref[0:1, :]
    select = (iota((back_ref.shape[0], rows), 0) == place).astype(F32).astype(BF16)
    delta = lax.dot_general(select, back_ref[...], TN, preferred_element_type=F32)
    out_ref[...] = (base_ref[...].astype(F32) + ADAPTER_SCALE * delta).astype(BF16)


def call(kernel, out_shape, *args):
    return pl.pallas_call(
        kernel,
        out_shape=out_shape,
        compiler_params=pltpu.CompilerParams(vmem_limit_bytes=VMEM_LIMIT),
    )(*args)


def local(
    tokens, key_value_weight, adapter_down_weight, adapter_up_weight, request_adapter_index, lengths
):
    tok_rows, width = tokens.shape
    n_ad = lax.axis_size("ad")
    n_tp = lax.axis_size("tp")
    n_z = n_ad // N_X
    stored, doubled_rank, _ = adapter_down_weight.shape
    columns = adapter_up_weight.shape[2]
    per_plane = stored * N_X
    cap = (N_X + 1) * MAXLEN
    rows = n_z * cap
    along_x = [[z * N_X + x for x in range(N_X)] for z in range(n_z)]
    along_z = [[z * N_X + x for z in range(n_z)] for x in range(N_X)]

    def pack(*refs):
        pack_kernel(n_z, cap, per_plane, *refs)

    def project(*refs):
        low_kernel(n_z, cap, *refs)

    down = lax.all_gather(adapter_down_weight, "ad", axis_index_groups=along_x, tiled=True)
    up = lax.all_gather(adapter_up_weight, "ad", axis_index_groups=along_x, tiled=True)
    send, ids, place = call(
        pack,
        (
            jax.ShapeDtypeStruct((rows, width), BF16),
            jax.ShapeDtypeStruct((n_z, 128), F32),
            jax.ShapeDtypeStruct((8, tok_rows), jnp.int32),
        ),
        lengths,
        request_adapter_index.reshape(1, -1),
        tokens,
    )
    ids = lax.all_to_all(ids, "ad", 0, 0, axis_index_groups=along_z, tiled=True)
    recv = lax.all_to_all(
        send.reshape(n_z, cap, width), "ad", 0, 0, axis_index_groups=along_z, tiled=True
    )
    partial_value = jnp.dot(tokens, key_value_weight, preferred_element_type=F32)
    base = lax.psum_scatter(partial_value.astype(BF16), "tp", scatter_dimension=1, tiled=True)
    parts, lane_ids = call(
        project,
        (
            jax.ShapeDtypeStruct((n_tp, doubled_rank // 2, rows), BF16),
            jax.ShapeDtypeStruct((8, rows), F32),
        ),
        recv.reshape(rows, width),
        ids,
        down,
    )
    parts = lax.all_to_all(parts, "tp", 0, 0, tiled=True)
    delta = call(delta_kernel, jax.ShapeDtypeStruct((rows, columns), BF16), parts, lane_ids, up)
    back = lax.all_to_all(
        delta.reshape(n_z, cap, columns), "ad", 0, 0, axis_index_groups=along_z, tiled=True
    )
    return call(
        mix_kernel,
        jax.ShapeDtypeStruct((tok_rows, columns), BF16),
        place,
        back.reshape(rows, columns),
        base,
    )


def solution(mesh):
    return jax.shard_map(
        local,
        mesh=mesh,
        in_specs=(
            P("ad", "tp"),
            P("tp", None),
            P("ad", None, "tp"),
            P("ad", None, "tp"),
            P("ad"),
            P("ad", None),
        ),
        out_specs=P("ad", "tp"),
        check_vma=False,
    )
```

time: 313 us -> 140 us (0.45)
  waiting for transfers between devices: 193 us -> 50.6 us
  local copies, waits for them, and re-layouts: 24.2 us -> 4.55 us
  blocking collectives: 57.2 us -> 39.7 us
  starting transfers between devices: 13.6 us -> 20.3 us
  Pallas kernels: 0 us -> 5.23 us
  matrix products: 7.52 us -> 2.65 us
  other arithmetic: 3.46 us -> 0 us
    all_to_all x2 -> x3, waiting for transfers between devices: 193 us -> 18.8 us  [the longest x1 18.8 us: local(): lax.all_to_all(delta.reshape(n_z, cap, columns), 'ad', 0, 0, axis_index_g...]
    all_gather x0 -> x1, waiting for transfers between devices: none -> 31 us  [local(): lax.all_gather(adapter_down_weight, 'ad', axis_index_groups=along_x, tile...]
    psum x1 -> x0, blocking collectives: 26.2 us -> none  [local(): low = lax.psum(low_tokens.astype(jnp.bfloat16), 'tp').astype(jnp.float32)]
    gather x10 -> x0, local copies, waits for them, and re-layouts: 22.5 us -> none  [the longest x1 5.07 us: local(): tokens[take]]
    all_gather x0 -> x1, blocking collectives: none -> 12.3 us  [local(): lax.all_gather(adapter_up_weight, 'ad', axis_index_groups=along_x, tiled=...]
    all_to_all x2 -> x3, starting transfers between devices: 13.6 us -> 20.2 us  [the longest x1 12.3 us: local(): lax.all_to_all(delta.reshape(n_z, cap, columns), 'ad', 0, 0, axis_index_g...]
    pallas_call x0 -> x4, Pallas kernels: none -> 5.23 us  [call(): pl.pallas_call(kernel, out_shape=out_shape, compiler_params=pltpu.Compile...]
    dot_general x3 -> x1, matrix products: 7.52 us -> 2.65 us  [local(): jnp.dot(tokens, key_value_weight, preferred_element_type=F32)]
  transfers between devices with their start and end apart: 3 -> 5, of which waited for: 2 -> 2; matrix products, arithmetic and copies ran while one was open for 9% -> 2% of each run, Pallas kernels for 0% -> 2%
where the time goes in v1:
time: 140 us; the launch traced here: 138 us
  waiting for transfers between devices  50.6 us (36%)
  blocking collectives  39.7 us (28%)
  starting transfers between devices  20.3 us (14%)
  between operations  14.9 us (11%)
  Pallas kernels  5.23 us (4%)
  local copies, waits for them, and re-layouts  4.55 us (3%)
  matrix products  2.65 us (2%)
    all_gather x1, waiting for transfers between devices, local(): lax.all_gather(adapter_down_weight, 'ad', axis_index_groups=along_x, tile...  31 us
    all_to_all x1, blocking collectives, local(): ids = lax.all_to_all(ids, 'ad', 0, 0, axis_index_groups=along_z, tiled=True)  27.4 us
    all_to_all x1, waiting for transfers between devices, local(): lax.all_to_all(delta.reshape(n_z, cap, columns), 'ad', 0, 0, axis_index_g...  18.8 us
    all_to_all x1, starting transfers between devices, local(): lax.all_to_all(delta.reshape(n_z, cap, columns), 'ad', 0, 0, axis_index_g...  12.3 us
    all_gather x1, blocking collectives, local(): lax.all_gather(adapter_up_weight, 'ad', axis_index_groups=along_x, tiled=...  12.3 us
    pallas_call x4, Pallas kernels, call(): pl.pallas_call(kernel, out_shape=out_shape, compiler_params=pltpu.Compile...  5.23 us
    unnamed x14, local copies, waits for them, and re-layouts  4.55 us
    all_to_all x1, starting transfers between devices, local(): parts = lax.all_to_all(parts, 'tp', 0, 0, tiled=True)  4.29 us
  transfers between devices with their start and end apart: 5, of which 2 were waited for; matrix products, arithmetic and copies ran while one was open for 2% of the time, Pallas kernels for 2%

profile of v1, /device:TPU:6, one launch (start us, length us, event | category | flops | bytes accessed | tf_op | source)
XLA Modules:
  0.0 137.8 jit_solution(17589387031314122835)
XLA Ops:
  7.4 0.0 copy-start
  7.4 0.0 copy-start.2
  7.4 1.1 copy-done.2
  8.5 0.0 copy-start.4
  8.5 0.7 copy-done.4
  9.1 0.0 copy-start.5
  9.1 0.7 copy-done.5
  9.8 1.4 %shard_map.64 = (bf16[640,512]{1,0:T(8,128)(2,1)}, f32[16,128]{1,0:T(8,128)S(1)}, s32[8,256]{1,0:T(8,128)S(1)}) custom-call(s32[1,64]{1,0:T(1,128)S(1)} %copy-done.4, s32[1,64]{1,0:T(1,128)S(1)} %bitcast.15, bf16[256,512]{1,0:T(8,128)(2,1)S(1)} %copy-done.2), custom_call_target="tpu_custom_call" | custom-call | tf_op jit(solution)/shard_map/pallas_call | solution.py:104
  11.2 27.4 %all_to_all.26 = f32[16,1,128]{2,1,0:T(1,128)S(1)} all-to-all(f32[16,1,128]{2,1,0:T(1,128)S(1)} %bitcast.14), channel_id=1, replica_groups={{0,4,8,12,16,20,24,28,32,36,40,44,48,52,56,60},{1,5,9,13,17,21,25,29,33..., dimensions={0} | all-to-all | bytes 16384 | tf_op jit(solution)/shard_map/all_to_all | solution.py:145
  38.6 3.6 %all-to-all-start = ((bf16[16,40,512]{2,1,0:T(8,128)(2,1)}), bf16[16,40,512]{2,1,0:T(8,128)(2,1)S(1)}, u32[]{:S(2)}, u32[]{:S(2)}) async-start(bf16[16,40,512]{2,1,0:T(8,128)(2,1)} %bitcast.1), calls=%async_computation | async-start | bytes 1310720 | tf_op jit(solution)/shard_map/all_to_all | solution.py:146
  42.2 0.0 all-gather.2.cloned.1.call-start
  42.2 0.7 all-gather.2.cloned.1.call-update
  42.9 0.0 reduce-scatter.2.cloned.1.call-start
  43.0 0.0 copy-done
  43.0 2.6 %convolution_convert_fusion = bf16[256,2048]{1,0:T(8,128)(2,1)} fusion(bf16[256,512]{1,0:T(8,128)(2,1)} %refs_2_.1, bf16[512,2048]{1,0:T(8,128)(2,1)S(1)} %copy-done), kind=kOutput, calls=%fused_computation | convolution fusion | flops 537395200 | bytes 3407872 | tf_op jit(solution)/shard_map/dot_general | solution.py:149
  45.6 0.0 copy-start.6
  45.6 0.0 reduce-scatter.2.cloned.1.call-update
  45.7 31.0 %all-gather.2.cloned.1.call-done.refs_2_ = bf16[32,32,512]{2,1,0:T(8,128)(2,1)} async-done(((bf16[8,32,512]{2,1,0:T(8,128)(2,1)}), bf16[32,32,512]{2,1,0:T(8,128)(2,1)}) %all-gather.2.cloned.1.call-update) | async-done | bytes 1048592 | tf_op jit(solution)/shard_map/all_gather | solution.py:132
  76.7 0.0 all-to-all-done
  76.7 0.0 copy-start.1
  76.7 1.2 copy-done.1
  77.9 1.7 %shard_map.65 = (bf16[8,16,640]{2,1,0:T(8,128)(2,1)}, f32[8,640]{1,0:T(8,128)S(1)}) custom-call(bf16[640,512]{1,0:T(8,128)(2,1)S(1)} %bitcast.11, f32[16,128]{1,0:T(8,128)S(1)} %bitcast.13, bf16[32,32,512]{2,1,0:T(8,128)(2,1)S(1)} %copy-done.1), custom_call_target="tpu_custom_call" | custom-call | tf_op jit(solution)/shard_map/pallas_call | solution.py:104
  79.7 4.3 %all-to-all-start.2 = ((bf16[8,16,640]{2,1,0:T(8,128)(2,1)}), bf16[8,16,640]{2,1,0:T(8,128)(2,1)S(1)}, u32[]{:S(2)}, u32[]{:S(2)}) async-start(bf16[8,16,640]{2,1,0:T(8,128)(2,1)} %get-tuple-element.13), calls=%async_computation.2 | async-start | bytes 327680 | tf_op jit(solution)/shard_map/all_to_all | solution.py:161
  84.0 0.0 copy-done.6
  84.0 12.3 %all_gather.7.up_ref = bf16[32,16,256]{2,1,0:T(8,128)(2,1)S(1)} all-gather(bf16[8,16,256]{2,1,0:T(8,128)(2,1)S(1)} %copy-done.6), channel_id=1, replica_groups={{0,1,2,3},{4,5,6,7},{8,9,10,11},{12,13,14,15},{16,17,18,19},{20,21,22,2..., dimensions={0}, use_global_device_ids=true | all-gather | bytes 327680 | tf_op jit(solution)/shard_map/all_gather | solution.py:133
  96.2 0.0 all-to-all-done.2.parts_ref
  96.2 1.1 shard_map.66
  97.3 12.3 %all-to-all-start.3 = ((bf16[16,40,256]{2,1,0:T(8,128)(2,1)}), bf16[16,40,256]{2,1,0:T(8,128)(2,1)S(1)}, u32[]{:S(2)}, u32[]{:S(2)}) async-start(bf16[16,40,256]{2,1,0:T(8,128)(2,1)} %bitcast.6), calls=%async_computation.3 | async-start | bytes 655360 | tf_op jit(solution)/shard_map/all_to_all | solution.py:163
  109.6 0.0 reduce-scatter.2.cloned.1.call-done.base_ref
  109.7 18.8 %all-to-all-done.3 = bf16[16,40,256]{2,1,0:T(8,128)(2,1)S(1)} async-done(((bf16[16,40,256]{2,1,0:T(8,128)(2,1)}), bf16[16,40,256]{2,1,0:T(8,128)(2,1)S(1)}, u32[]{:S(2)}, u32[]{:S(2)}) %all-to-all-start.3) | async-done | bytes 327712 | tf_op jit(solution)/shard_map/all_to_all | solution.py:163
  128.5 0.0 copy-start.3
  128.5 0.9 copy-done.3
  129.4 1.0 shard_map.67
Async XLA Ops:
  7.4 35.6 %copy-start = (bf16[512,2048]{1,0:T(8,128)(2,1)S(1)}, bf16[512,2048]{1,0:T(8,128)(2,1)}, u32[]{:S(2)}) copy-start(bf16[512,2048]{1,0:T(8,128)(2,1)} %param.7) | copy-start | bytes 6291460
  7.4 1.1 copy-start.2
  8.5 0.7 copy-start.4
  9.1 0.7 copy-start.5
  38.6 38.1 %all-to-all-start = ((bf16[16,40,512]{2,1,0:T(8,128)(2,1)}), bf16[16,40,512]{2,1,0:T(8,128)(2,1)S(1)}, u32[]{:S(2)}, u32[]{:S(2)}) async-start(bf16[16,40,512]{2,1,0:T(8,128)(2,1)} %bitcast.1), calls=%async_computation | async-start | bytes 1310720 | tf_op jit(solution)/shard_map/all_to_all | solution.py:146
  42.2 34.5 %all-gather.2.cloned.1.call-start = ((), (), s32[]{:S(2)}) async-start(), calls=%async_computation.5 | async-start | bytes 1310720 | tf_op jit(solution)/shard_map/all_gather | solution.py:132
  42.9 66.8 %reduce-scatter.2.cloned.1.call-start = ((), (), s32[]{:S(2)}) async-start(), calls=%async_computation.6 | async-start | bytes 1179648 | tf_op jit(solution)/shard_map/reduce_scatter | solution.py:150
  45.6 38.3 %copy-start.6 = (bf16[8,16,256]{2,1,0:T(8,128)(2,1)S(1)}, bf16[8,16,256]{2,1,0:T(8,128)(2,1)}, u32[]{:S(2)}) copy-start(bf16[8,16,256]{2,1,0:T(8,128)(2,1)} %param.9) | copy-start | bytes 196612
  76.7 1.2 copy-start.1
  79.7 16.6 %all-to-all-start.2 = ((bf16[8,16,640]{2,1,0:T(8,128)(2,1)}), bf16[8,16,640]{2,1,0:T(8,128)(2,1)S(1)}, u32[]{:S(2)}, u32[]{:S(2)}) async-start(bf16[8,16,640]{2,1,0:T(8,128)(2,1)} %get-tuple-element.13), calls=%async_computation.2 | async-start | bytes 327680 | tf_op jit(solution)/shard_map/all_to_all | solution.py:161
  97.3 31.2 %all-to-all-start.3 = ((bf16[16,40,256]{2,1,0:T(8,128)(2,1)}), bf16[16,40,256]{2,1,0:T(8,128)(2,1)S(1)}, u32[]{:S(2)}, u32[]{:S(2)}) async-start(bf16[16,40,256]{2,1,0:T(8,128)(2,1)} %bitcast.6), calls=%async_computation.3 | async-start | bytes 655360 | tf_op jit(solution)/shard_map/all_to_all | solution.py:163
  128.5 0.9 copy-start.3
Sparse Core Ops, SparseCore 0:
  45.1 31.5 all-gather.1
Sparse Core Ops, SparseCore 1:
  46.2 41.1 reduce-scatter.1

commit v2 on v1

v2 whole, which is shorter than its diff:
```python
import jax
import jax.numpy as jnp
from jax import lax
from jax.experimental import pallas as pl
from jax.experimental.pallas import tpu as pltpu
from jax.sharding import PartitionSpec as P

ADAPTER_SCALE = 2.0
N_X = 4
MAXLEN = 8

F32 = jnp.float32
BF16 = jnp.bfloat16
NT = (((1,), (1,)), ((), ()))
TN = (((0,), (0,)), ((), ()))
LANES = 128
VMEM_LIMIT = 48 * 1024 * 1024


def iota(shape, dimension):
    return lax.broadcasted_iota(jnp.int32, shape, dimension)


def pack_kernel(
    planes, cap, per_plane,
    lens_ref, index_ref, tokens_ref, down_ref, up_ref,
    send_ref, place_ref, factors_ref,
):
    requests = lens_ref.shape[1]
    rows, width = tokens_ref.shape
    rank, columns = up_ref.shape[1:]
    doubled = down_ref.shape[1]
    factors_ref[:, :doubled, :] = down_ref[...]
    for half in range(2):
        factors_ref[:, doubled:, half * columns : (half + 1) * columns] = up_ref[
            :, half * rank // 2 : (half + 1) * rank // 2, :
        ]
    lens = lens_ref[...].astype(F32)
    index = index_ref[...].astype(F32)
    r0, r1 = iota((requests, requests), 0), iota((requests, requests), 1)
    ends = jnp.sum(jnp.where(r1 <= r0, lens, 0.0), axis=1, keepdims=True)
    starts = jnp.sum(jnp.where(r1 < r0, lens, 0.0), axis=1, keepdims=True)
    index_col = jnp.sum(jnp.where(r1 == r0, index, 0.0), axis=1, keepdims=True)
    t = iota((requests, rows), 1).astype(F32)
    inside = (t >= starts) & (t < ends)
    adapter = jnp.sum(jnp.where(inside, index_col, 0.0), axis=0, keepdims=True)
    plane = jnp.floor(adapter * (1.0 / per_plane))
    local = adapter - plane * per_plane
    member = iota((planes, rows), 0).astype(F32) == plane
    before = (iota((rows, rows), 0) < iota((rows, rows), 1)).astype(F32).astype(BF16)
    counts = jnp.dot(member.astype(F32).astype(BF16), before, preferred_element_type=F32)
    rank_in = jnp.sum(jnp.where(member, counts, 0.0), axis=0, keepdims=True)
    place = (plane * cap + rank_in).astype(jnp.int32)
    place_ref[...] = jnp.broadcast_to(place, place_ref.shape)
    select = (iota((planes * cap, rows), 0) == place).astype(F32).astype(BF16)
    packed = jnp.dot(select, tokens_ref[...], preferred_element_type=F32)
    blocks = width // LANES
    for c in range(blocks):
        block = packed[:, c * LANES : (c + 1) * LANES].reshape(planes, cap, LANES)
        send_ref[:, c * cap : (c + 1) * cap, :] = block.astype(BF16)
    at_rank = (iota((LANES, rows), 0).astype(F32) == rank_in).astype(F32).astype(BF16)
    ids = lax.dot_general(
        jnp.where(member, local, 0.0).astype(BF16), at_rank, NT, preferred_element_type=F32
    )
    ids = jnp.broadcast_to(ids.reshape(planes, 1, LANES), (planes, 8, LANES))
    send_ref[:, blocks * cap :, :] = ids.astype(BF16)


def low_kernel(planes, cap, recv_ref, factors_ref, out_ref, lane_ids_ref):
    rows = planes * cap
    blocks = recv_ref.shape[1] // cap
    source = iota((planes, rows), 0)
    p = iota((planes, rows), 1)
    mine = (p >= source * cap) & (p < source * cap + cap)
    offset = jnp.sum(jnp.where(mine, p - source * cap, 0).astype(F32), axis=0, keepdims=True)
    spread = (iota((LANES, rows), 0).astype(F32) == offset).astype(F32).astype(BF16)
    ids = recv_ref[:, blocks * cap :, :].astype(F32)[:, 0, :].astype(BF16)
    ids = jnp.dot(ids, spread, preferred_element_type=F32)
    ids = jnp.sum(jnp.where(mine, ids, 0.0), axis=0, keepdims=True)
    lane_ids_ref[...] = jnp.broadcast_to(ids, lane_ids_ref.shape)
    recv = jnp.concatenate(
        [
            recv_ref[:, c * cap : (c + 1) * cap, :].astype(F32).reshape(rows, LANES).astype(BF16)
            for c in range(blocks)
        ],
        axis=1,
    )
    adapters = factors_ref.shape[0]
    n, rank = out_ref.shape[:2]
    doubled = 2 * rank
    step = 8
    low = jnp.zeros((doubled, rows), F32)
    for first in range(0, adapters, step):
        block = factors_ref[first : first + step, :doubled, :].reshape(step * doubled, -1)
        values = lax.dot_general(block, recv, NT, preferred_element_type=F32)
        for a in range(step):
            low = jnp.where(
                ids == float(first + a), values[a * doubled : (a + 1) * doubled], low
            )
    low = low.astype(BF16)
    for j in range(n):
        half = j * 2 // n
        out_ref[j] = low[half * rank : (half + 1) * rank]


def delta_kernel(parts_ref, lane_ids_ref, factors_ref, out_ref):
    low = parts_ref[0].astype(F32)
    for j in range(1, parts_ref.shape[0]):
        low = low + parts_ref[j].astype(F32)
    rank = low.shape[0]
    columns = out_ref.shape[1]
    ids = lane_ids_ref[0:1, :]
    adapters = factors_ref.shape[0]
    total = None
    for half in range(2):
        part = low[half * rank // 2 : (half + 1) * rank // 2]
        spread = jnp.concatenate(
            [jnp.where(ids == float(a), part, 0.0) for a in range(adapters)], axis=0
        ).astype(BF16)
        up = factors_ref[:, 2 * rank :, half * columns : (half + 1) * columns].astype(F32)
        up = up.reshape(spread.shape[0], columns).astype(BF16)
        product = lax.dot_general(spread, up, TN, preferred_element_type=F32)
        total = product if total is None else total + product
    out_ref[...] = total.astype(BF16)


def mix_kernel(place_ref, back_ref, base_ref, out_ref):
    rows = base_ref.shape[0]
    place = place_ref[0:1, :]
    select = (iota((back_ref.shape[0], rows), 0) == place).astype(F32).astype(BF16)
    delta = lax.dot_general(select, back_ref[...], TN, preferred_element_type=F32)
    out_ref[...] = (base_ref[...].astype(F32) + ADAPTER_SCALE * delta).astype(BF16)


def call(kernel, out_shape, *args):
    return pl.pallas_call(
        kernel,
        out_shape=out_shape,
        compiler_params=pltpu.CompilerParams(vmem_limit_bytes=VMEM_LIMIT),
    )(*args)


def local(
    tokens, key_value_weight, adapter_down_weight, adapter_up_weight, request_adapter_index, lengths
):
    tok_rows, width = tokens.shape
    n_ad = lax.axis_size("ad")
    n_tp = lax.axis_size("tp")
    n_z = n_ad // N_X
    stored, doubled_rank, _ = adapter_down_weight.shape
    columns = adapter_up_weight.shape[2]
    per_plane = stored * N_X
    cap = (N_X + 1) * MAXLEN
    rows = n_z * cap
    along_x = [[z * N_X + x for x in range(N_X)] for z in range(n_z)]
    along_z = [[z * N_X + x for z in range(n_z)] for x in range(N_X)]

    def pack(*refs):
        pack_kernel(n_z, cap, per_plane, *refs)

    def project(*refs):
        low_kernel(n_z, cap, *refs)

    send, place, factors = call(
        pack,
        (
            jax.ShapeDtypeStruct((n_z, width // LANES * cap + 8, LANES), BF16),
            jax.ShapeDtypeStruct((8, tok_rows), jnp.int32),
            jax.ShapeDtypeStruct((stored, doubled_rank + 8, width), BF16),
        ),
        lengths,
        request_adapter_index.reshape(1, -1),
        tokens,
        adapter_down_weight,
        adapter_up_weight,
    )
    factors = lax.all_gather(factors, "ad", axis_index_groups=along_x, tiled=True)
    recv = lax.all_to_all(send, "ad", 0, 0, axis_index_groups=along_z, tiled=True)
    partial_value = jnp.dot(tokens, key_value_weight, preferred_element_type=F32)
    base = lax.psum_scatter(partial_value.astype(BF16), "tp", scatter_dimension=1, tiled=True)
    parts, lane_ids = call(
        project,
        (
            jax.ShapeDtypeStruct((n_tp, doubled_rank // 2, rows), BF16),
            jax.ShapeDtypeStruct((8, rows), F32),
        ),
        recv,
        factors,
    )
    parts = lax.all_to_all(parts, "tp", 0, 0, tiled=True)
    delta = call(delta_kernel, jax.ShapeDtypeStruct((rows, columns), BF16), parts, lane_ids, factors)
    back = lax.all_to_all(
        delta.reshape(n_z, cap, columns), "ad", 0, 0, axis_index_groups=along_z, tiled=True
    )
    return call(
        mix_kernel,
        jax.ShapeDtypeStruct((tok_rows, columns), BF16),
        place,
        back.reshape(rows, columns),
        base,
    )


def solution(mesh):
    return jax.shard_map(
        local,
        mesh=mesh,
        in_specs=(
            P("ad", "tp"),
            P("tp", None),
            P("ad", None, "tp"),
            P("ad", None, "tp"),
            P("ad"),
            P("ad", None),
        ),
        out_specs=P("ad", "tp"),
        check_vma=False,
    )
```

time: 140 us -> 116 us (0.83); the launches traced: 138 us -> 115 us
  blocking collectives: 39.7 us -> 10.7 us
  waiting for transfers between devices: 50.6 us -> 53.6 us
  local copies, waits for them, and re-layouts: 4.55 us -> 7.29 us
  starting transfers between devices: 20.3 us -> 22.8 us
    all_to_all x1, blocking collectives: 27.4 us -> 10.7 us  [local(): parts = lax.all_to_all(parts, 'tp', 0, 0, tiled=True)]
    all_to_all x2 -> x1, waiting for transfers between devices: 0.01 us -> 14 us  [local(): lax.all_to_all(send, 'ad', 0, 0, axis_index_groups=along_z, tiled=True)]
    all_gather x1 -> x0, blocking collectives: 12.3 us -> none  [local(): lax.all_gather(adapter_up_weight, 'ad', axis_index_groups=along_x, tiled=...]
    all_gather x1, waiting for transfers between devices: 31 us -> 19.2 us  [local(): lax.all_gather(factors, 'ad', axis_index_groups=along_x, tiled=True)]
    all_to_all x2 -> x1, starting transfers between devices: 7.88 us -> 15.2 us  [local(): lax.all_to_all(send, 'ad', 0, 0, axis_index_groups=along_z, tiled=True)]
    all_to_all x1, starting transfers between devices: 12.3 us -> 7.6 us  [local(): lax.all_to_all(delta.reshape(n_z, cap, columns), 'ad', 0, 0, axis_index_g...]
    unnamed x14 -> x22, local copies, waits for them, and re-layouts: 4.55 us -> 7.29 us
    all_to_all x1, waiting for transfers between devices: 18.8 us -> 20.3 us  [local(): lax.all_to_all(delta.reshape(n_z, cap, columns), 'ad', 0, 0, axis_index_g...]
  transfers between devices with their start and end apart: 5 -> 4, of which waited for: 2 -> 3; matrix products, arithmetic and copies ran while one was open for 2% -> 1% of each run, Pallas kernels for 2% -> 2%
where the time goes in v2:
time: 116 us; the launch traced here: 115 us
  waiting for transfers between devices  53.6 us (46%)
  starting transfers between devices  22.8 us (20%)
  between operations  14.9 us (13%)
  blocking collectives  10.7 us (9%)
  local copies, waits for them, and re-layouts  7.29 us (6%)
  Pallas kernels  4.39 us (4%)
  matrix products  1.67 us (1%)
    all_to_all x1, waiting for transfers between devices, local(): lax.all_to_all(delta.reshape(n_z, cap, columns), 'ad', 0, 0, axis_index_g...  20.3 us
    all_gather x1, waiting for transfers between devices, local(): lax.all_gather(factors, 'ad', axis_index_groups=along_x, tiled=True)  19.2 us
    all_to_all x1, starting transfers between devices, local(): lax.all_to_all(send, 'ad', 0, 0, axis_index_groups=along_z, tiled=True)  15.2 us
    all_to_all x1, waiting for transfers between devices, local(): lax.all_to_all(send, 'ad', 0, 0, axis_index_groups=along_z, tiled=True)  14 us
    all_to_all x1, blocking collectives, local(): parts = lax.all_to_all(parts, 'tp', 0, 0, tiled=True)  10.7 us
    all_to_all x1, starting transfers between devices, local(): lax.all_to_all(delta.reshape(n_z, cap, columns), 'ad', 0, 0, axis_index_g...  7.6 us
    unnamed x22, local copies, waits for them, and re-layouts  7.29 us
    pallas_call x4, Pallas kernels, call(): pl.pallas_call(kernel, out_shape=out_shape, compiler_params=pltpu.Compile...  4.39 us
  transfers between devices with their start and end apart: 4, of which 3 were waited for; matrix products, arithmetic and copies ran while one was open for 1% of the time, Pallas kernels for 2%

profile of v2, /device:TPU:6, one launch (start us, length us, event | category | flops | bytes accessed | tf_op | source)
XLA Modules:
  0.0 115.4 jit_solution(1186602445457704996)
XLA Ops:
  7.4 0.0 copy-start
  7.4 0.0 all-gather.2.cloned.1.call-start
  7.4 0.0 copy-start.3
  7.4 1.1 copy-done.3
  8.5 0.0 copy-start.6
  8.5 0.9 copy-done.6
  9.4 0.0 copy-start.8
  9.4 0.8 copy-done.8
  10.3 0.0 copy-start.9
  10.3 0.7 copy-done.9
  10.9 0.0 copy-start.10
  10.9 0.7 copy-done.10
  11.6 0.0 copy-start.4
  11.6 1.2 %shard_map.64 = (bf16[16,168,128]{2,1,0:T(8,128)(2,1)S(1)}, s32[8,256]{1,0:T(8,128)S(1)}, bf16[8,40,512]{2,1,0:T(8,128)(2,1)}) custom-call(s32[1,64]{1,0:T(1,128)S(1)} %copy-done.9, s32[1,64]{1,0:T(1,128)S(1)} %bitcast.6, bf16[256,512]{1,0:T(8,128)(2,1)S(1)} %copy-done.3, bf16[8,32,512]{2,1,0:T(8,128)(2,1)S(1)} %copy-done.6, bf16[8,16,256]{2,1,0:T(8,128)(2,1)S(1)} %copy-done.8), custom_call_target="tpu_custom_call" | custom-call | tf_op jit(solution)/shard_map/pallas_call | solution.py:136
  12.8 0.0 copy-start.5
  12.8 0.9 copy-done.5
  13.7 0.0 all-gather.2.cloned.1.call-update
  13.7 15.2 %all-to-all-start = ((bf16[16,168,128]{2,1,0:T(8,128)(2,1)}), bf16[16,168,128]{2,1,0:T(8,128)(2,1)S(1)}, u32[]{:S(2)}, u32[]{:S(2)}) async-start(bf16[16,168,128]{2,1,0:T(8,128)(2,1)} %copy-done.5), calls=%async_computation | async-start | bytes 1376256 | tf_op jit(solution)/shard_map/all_to_all | solution.py:178
  28.9 0.0 reduce-scatter.2.cloned.1.call-start
  29.0 0.0 copy-done
  29.0 0.0 copy-done.4
  29.0 1.7 %convolution_convert_fusion = bf16[256,2048]{1,0:T(8,128)(2,1)} fusion(bf16[256,512]{1,0:T(8,128)(2,1)S(1)} %copy-done.4, bf16[512,2048]{1,0:T(8,128)(2,1)S(1)} %copy-done), kind=kOutput, calls=%fused_computation | convolution fusion | flops 537395200 | bytes 3407872 | tf_op jit(solution)/shard_map/dot_general | solution.py:179
  30.6 0.0 reduce-scatter.2.cloned.1.call-update
  30.7 19.2 %all-gather.2.cloned.1.call-done.refs_1_.factors_ref = bf16[32,40,512]{2,1,0:T(8,128)(2,1)} async-done(((bf16[8,40,512]{2,1,0:T(8,128)(2,1)}), bf16[32,40,512]{2,1,0:T(8,128)(2,1)}) %all-gather.2.cloned.1.call-update) | async-done | bytes 1310736 | tf_op jit(solution)/shard_map/all_gather | solution.py:177
  49.9 14.0 %all-to-all-done.refs_0_ = bf16[16,168,128]{2,1,0:T(8,128)(2,1)S(1)} async-done(((bf16[16,168,128]{2,1,0:T(8,128)(2,1)}), bf16[16,168,128]{2,1,0:T(8,128)(2,1)S(1)}, u32[]{:S(2)}, u32[]{:S(2)}) %all-to-all-start) | async-done | bytes 688160 | tf_op jit(solution)/shard_map/all_to_all | solution.py:178
  63.9 0.0 copy-start.1
  63.9 1.3 %copy-done.1 = bf16[32,40,512]{2,1,0:T(8,128)(2,1)S(1)} copy-done((bf16[32,40,512]{2,1,0:T(8,128)(2,1)S(1)}, bf16[32,40,512]{2,1,0:T(8,128)(2,1)}, u32[]{:S(2)}) %copy-start.1) | copy-done | bytes 1310744
  65.2 0.0 copy-start.2
  65.2 1.1 shard_map.65
  66.3 10.7 %all_to_all.15.parts_ref = bf16[8,16,640]{2,1,0:T(8,128)(2,1)S(1)} all-to-all(bf16[8,16,640]{2,1,0:T(8,128)(2,1)S(1)} %get-tuple-element.13), channel_id=1, replica_groups=mesh['tp'=8,'ad'=64] {'tp'}, dimensions={0} | all-to-all | bytes 327680 | tf_op jit(solution)/shard_map/all_to_all | solution.py:190
  77.0 0.0 copy-done.2
  77.0 1.1 shard_map.66
  78.1 7.6 %all-to-all-start.2 = ((bf16[16,40,256]{2,1,0:T(8,128)(2,1)}), bf16[16,40,256]{2,1,0:T(8,128)(2,1)S(1)}, u32[]{:S(2)}, u32[]{:S(2)}) async-start(bf16[16,40,256]{2,1,0:T(8,128)(2,1)} %bitcast.1), calls=%async_computation.2 | async-start | bytes 655360 | tf_op jit(solution)/shard_map/all_to_all | solution.py:192
  85.7 0.0 reduce-scatter.2.cloned.1.call-done.base_ref
  85.8 20.3 %all-to-all-done.2 = bf16[16,40,256]{2,1,0:T(8,128)(2,1)S(1)} async-done(((bf16[16,40,256]{2,1,0:T(8,128)(2,1)}), bf16[16,40,256]{2,1,0:T(8,128)(2,1)S(1)}, u32[]{:S(2)}, u32[]{:S(2)}) %all-to-all-start.2) | async-done | bytes 327712 | tf_op jit(solution)/shard_map/all_to_all | solution.py:192
  106.1 0.0 copy-start.7
  106.1 0.9 copy-done.7
  107.0 1.0 shard_map.67
Async XLA Ops:
  7.4 21.6 %copy-start = (bf16[512,2048]{1,0:T(8,128)(2,1)S(1)}, bf16[512,2048]{1,0:T(8,128)(2,1)}, u32[]{:S(2)}) copy-start(bf16[512,2048]{1,0:T(8,128)(2,1)} %param.7) | copy-start | bytes 6291460
  7.4 42.5 %all-gather.2.cloned.1.call-start = ((), (), s32[]{:S(2)}) async-start(), calls=%async_computation.4 | async-start | bytes 1638400 | tf_op jit(solution)/shard_map/all_gather | solution.py:177
  7.4 1.1 copy-start.3
  8.5 0.9 copy-start.6
  9.4 0.8 copy-start.8
  10.3 0.7 copy-start.9
  10.9 0.7 copy-start.10
  11.6 17.4 %copy-start.4 = (bf16[256,512]{1,0:T(8,128)(2,1)S(1)}, bf16[256,512]{1,0:T(8,128)(2,1)}, u32[]{:S(2)}) copy-start(bf16[256,512]{1,0:T(8,128)(2,1)} %refs_2_.1) | copy-start | bytes 786436
  12.8 0.9 copy-start.5
  13.7 50.2 %all-to-all-start = ((bf16[16,168,128]{2,1,0:T(8,128)(2,1)}), bf16[16,168,128]{2,1,0:T(8,128)(2,1)S(1)}, u32[]{:S(2)}, u32[]{:S(2)}) async-start(bf16[16,168,128]{2,1,0:T(8,128)(2,1)} %copy-done.5), calls=%async_computation | async-start | bytes 1376256 | tf_op jit(solution)/shard_map/all_to_all | solution.py:178
  28.9 56.9 %reduce-scatter.2.cloned.1.call-start = ((), (), s32[]{:S(2)}) async-start(), calls=%async_computation.5 | async-start | bytes 1179648 | tf_op jit(solution)/shard_map/reduce_scatter | solution.py:180
  63.9 1.3 %copy-start.1 = (bf16[32,40,512]{2,1,0:T(8,128)(2,1)S(1)}, bf16[32,40,512]{2,1,0:T(8,128)(2,1)}, u32[]{:S(2)}) copy-start(bf16[32,40,512]{2,1,0:T(8,128)(2,1)} %all-gather.2.cloned.1.call-done.refs_1_.factors_ref) | copy-start | bytes 3932164
  65.2 11.8 %copy-start.2 = (bf16[32,40,512]{2,1,0:T(8,128)(2,1)S(1)}, bf16[32,40,512]{2,1,0:T(8,128)(2,1)}, u32[]{:S(2)}) copy-start(bf16[32,40,512]{2,1,0:T(8,128)(2,1)} %all-gather.2.cloned.1.call-done.refs_1_.factors_ref) | copy-start | bytes 3932164
  78.1 27.9 %all-to-all-start.2 = ((bf16[16,40,256]{2,1,0:T(8,128)(2,1)}), bf16[16,40,256]{2,1,0:T(8,128)(2,1)S(1)}, u32[]{:S(2)}, u32[]{:S(2)}) async-start(bf16[16,40,256]{2,1,0:T(8,128)(2,1)} %bitcast.1), calls=%async_computation.2 | async-start | bytes 655360 | tf_op jit(solution)/shard_map/all_to_all | solution.py:192
  106.1 0.9 copy-start.7
Sparse Core Ops, SparseCore 0:
  13.8 36.0 all-gather.1
Sparse Core Ops, SparseCore 1:
  32.2 41.1 reduce-scatter.1

commit v3 on v2

--- a/solution.py
+++ b/solution.py
@@ -23,18 +23,28 @@
 
 def pack_kernel(
     planes, cap, per_plane,
-    lens_ref, index_ref, tokens_ref, down_ref, up_ref,
-    send_ref, place_ref, factors_ref,
+    lens_hbm, index_hbm, tokens_hbm, down_hbm, up_hbm,
+    send_ref, place_ref, factors_hbm,
+    lens_ref, index_ref, tokens_ref, block_ref, up_ref, sems,
 ):
     requests = lens_ref.shape[1]
     rows, width = tokens_ref.shape
-    rank, columns = up_ref.shape[1:]
-    doubled = down_ref.shape[1]
-    factors_ref[:, :doubled, :] = down_ref[...]
-    for half in range(2):
-        factors_ref[:, doubled:, half * columns : (half + 1) * columns] = up_ref[
-            :, half * rank // 2 : (half + 1) * rank // 2, :
-        ]
+    adapters, rank, columns = up_ref.shape
+    down_rows = down_hbm.shape[0]
+
+    def copy(source, target, k):
+        made = pltpu.make_async_copy(source, target, sems.at[k])
+        made.start()
+        return made
+
+    get_lens = copy(lens_hbm, lens_ref, 0)
+    get_index = copy(index_hbm, index_ref, 1)
+    get_tokens = copy(tokens_hbm, tokens_ref, 2)
+    get_down = copy(down_hbm, block_ref.at[pl.ds(0, down_rows)], 3)
+    get_up = copy(up_hbm, up_ref, 4)
+
+    get_lens.wait()
+    get_index.wait()
     lens = lens_ref[...].astype(F32)
     index = index_ref[...].astype(F32)
     r0, r1 = iota((requests, requests), 0), iota((requests, requests), 1)
@@ -45,7 +55,9 @@
     inside = (t >= starts) & (t < ends)
     adapter = jnp.sum(jnp.where(inside, index_col, 0.0), axis=0, keepdims=True)
     plane = jnp.floor(adapter * (1.0 / per_plane))
-    local = adapter - plane * per_plane
+    local = (adapter - plane * per_plane).astype(jnp.int32)
+    my_x = lax.axis_index("ad") % N_X
+    local = (local ^ (my_x * (per_plane // N_X))).astype(F32)
     member = iota((planes, rows), 0).astype(F32) == plane
     before = (iota((rows, rows), 0) < iota((rows, rows), 1)).astype(F32).astype(BF16)
     counts = jnp.dot(member.astype(F32).astype(BF16), before, preferred_element_type=F32)
@@ -53,6 +65,18 @@
     place = (plane * cap + rank_in).astype(jnp.int32)
     place_ref[...] = jnp.broadcast_to(place, place_ref.shape)
     select = (iota((planes * cap, rows), 0) == place).astype(F32).astype(BF16)
+
+    get_up.wait()
+    for a in range(adapters):
+        pair, side = a // 2, a % 2
+        block_ref[
+            down_rows + pair * rank : down_rows + (pair + 1) * rank,
+            side * columns : (side + 1) * columns,
+        ] = up_ref[a]
+    get_down.wait()
+    put = copy(block_ref, factors_hbm, 5)
+
+    get_tokens.wait()
     packed = jnp.dot(select, tokens_ref[...], preferred_element_type=F32)
     blocks = width // LANES
     for c in range(blocks):
@@ -64,9 +88,36 @@
     )
     ids = jnp.broadcast_to(ids.reshape(planes, 1, LANES), (planes, 8, LANES))
     send_ref[:, blocks * cap :, :] = ids.astype(BF16)
-
-
-def low_kernel(planes, cap, recv_ref, factors_ref, out_ref, lane_ids_ref):
+    put.wait()
+
+
+def base_kernel(place_ref, tokens_ref, weight_ref, keep_ref, send_ref):
+    del place_ref
+    columns = keep_ref.shape[2]
+    me = lax.axis_index("tp")
+
+    def block(relative):
+        first = pl.multiple_of((me ^ relative) * columns, columns)
+        return jnp.dot(
+            tokens_ref[...], weight_ref[:, pl.ds(first, columns)], preferred_element_type=F32
+        ).astype(BF16)
+
+    for k, relative in enumerate((0, 6, 2, 4)):
+        send_ref[k] = block(relative ^ 1)
+        keep_ref[k] = block(relative)
+
+
+def halve_kernel(keep_ref, recv_ref, kept_ref, send_ref):
+    half = kept_ref.shape[0]
+    for k in range(half):
+        kept_ref[k] = keep_ref[k].astype(F32) + recv_ref[k].astype(F32)
+        send_ref[k] = (keep_ref[half + k].astype(F32) + recv_ref[half + k].astype(F32)).astype(BF16)
+
+
+def low_kernel(
+    planes, cap, stored, recv_ref, f0_ref, f1_ref, f2_ref, f3_ref, kept_ref, out_ref, lane_ids_ref
+):
+    del kept_ref
     rows = planes * cap
     blocks = recv_ref.shape[1] // cap
     source = iota((planes, rows), 0)
@@ -85,17 +136,15 @@
         ],
         axis=1,
     )
-    adapters = factors_ref.shape[0]
     n, rank = out_ref.shape[:2]
     doubled = 2 * rank
-    step = 8
     low = jnp.zeros((doubled, rows), F32)
-    for first in range(0, adapters, step):
-        block = factors_ref[first : first + step, :doubled, :].reshape(step * doubled, -1)
+    for x, factors_ref in enumerate((f0_ref, f1_ref, f2_ref, f3_ref)):
+        block = factors_ref[: stored * doubled, :]
         values = lax.dot_general(block, recv, NT, preferred_element_type=F32)
-        for a in range(step):
+        for a in range(stored):
             low = jnp.where(
-                ids == float(first + a), values[a * doubled : (a + 1) * doubled], low
+                ids == float(x * stored + a), values[a * doubled : (a + 1) * doubled], low
             )
     low = low.astype(BF16)
     for j in range(n):
@@ -103,33 +152,35 @@
         out_ref[j] = low[half * rank : (half + 1) * rank]
 
 
-def delta_kernel(parts_ref, lane_ids_ref, factors_ref, out_ref):
+def delta_kernel(
+    stored, parts_ref, lane_ids_ref, f0_ref, f1_ref, f2_ref, f3_ref, out_ref
+):
     low = parts_ref[0].astype(F32)
     for j in range(1, parts_ref.shape[0]):
         low = low + parts_ref[j].astype(F32)
     rank = low.shape[0]
     columns = out_ref.shape[1]
     ids = lane_ids_ref[0:1, :]
-    adapters = factors_ref.shape[0]
-    total = None
-    for half in range(2):
-        part = low[half * rank // 2 : (half + 1) * rank // 2]
-        spread = jnp.concatenate(
-            [jnp.where(ids == float(a), part, 0.0) for a in range(adapters)], axis=0
-        ).astype(BF16)
-        up = factors_ref[:, 2 * rank :, half * columns : (half + 1) * columns].astype(F32)
-        up = up.reshape(spread.shape[0], columns).astype(BF16)
-        product = lax.dot_general(spread, up, TN, preferred_element_type=F32)
-        total = product if total is None else total + product
-    out_ref[...] = total.astype(BF16)
-
-
-def mix_kernel(place_ref, back_ref, base_ref, out_ref):
-    rows = base_ref.shape[0]
+    spread, up = [], []
+    for x, factors_ref in enumerate((f0_ref, f1_ref, f2_ref, f3_ref)):
+        for side in range(2):
+            up.append(factors_ref[stored * 2 * rank :, side * columns : (side + 1) * columns])
+            for pair in range(stored // 2):
+                a = float(x * stored + 2 * pair + side)
+                spread.append(jnp.where(ids == a, low, 0.0).astype(BF16))
+    product = lax.dot_general(
+        jnp.concatenate(spread, axis=0), jnp.concatenate(up, axis=0), TN, preferred_element_type=F32
+    )
+    out_ref[...] = product.astype(BF16)
+
+
+def mix_kernel(place_ref, back_ref, kept_ref, recv_ref, out_ref):
+    rows = out_ref.shape[0]
     place = place_ref[0:1, :]
     select = (iota((back_ref.shape[0], rows), 0) == place).astype(F32).astype(BF16)
     delta = lax.dot_general(select, back_ref[...], TN, preferred_element_type=F32)
-    out_ref[...] = (base_ref[...].astype(F32) + ADAPTER_SCALE * delta).astype(BF16)
+    base = kept_ref[0] + recv_ref[0].astype(F32)
+    out_ref[...] = (base + ADAPTER_SCALE * delta).astype(BF16)
 
 
 def call(kernel, out_shape, *args):
@@ -148,7 +199,7 @@
     n_tp = lax.axis_size("tp")
     n_z = n_ad // N_X
     stored, doubled_rank, _ = adapter_down_weight.shape
-    columns = adapter_up_weight.shape[2]
+    rank, columns = adapter_up_weight.shape[1:]
     per_plane = stored * N_X
     cap = (N_X + 1) * MAXLEN
     rows = n_z * cap
@@ -159,25 +210,57 @@
         pack_kernel(n_z, cap, per_plane, *refs)
 
     def project(*refs):
-        low_kernel(n_z, cap, *refs)
-
-    send, place, factors = call(
+        low_kernel(n_z, cap, stored, *refs)
+
+    def apply_up(*refs):
+        delta_kernel(stored, *refs)
+
+    hbm = pl.BlockSpec(memory_space=pltpu.HBM)
+    vmem = pl.BlockSpec(memory_space=pltpu.VMEM)
+    block_rows = stored * doubled_rank + stored // 2 * rank
+    send, place, factors = pl.pallas_call(
         pack,
-        (
+        out_shape=(
             jax.ShapeDtypeStruct((n_z, width // LANES * cap + 8, LANES), BF16),
             jax.ShapeDtypeStruct((8, tok_rows), jnp.int32),
-            jax.ShapeDtypeStruct((stored, doubled_rank + 8, width), BF16),
+            jax.ShapeDtypeStruct((block_rows, width), BF16),
         ),
+        in_specs=[hbm] * 5,
+        out_specs=(vmem, vmem, hbm),
+        scratch_shapes=[
+            pltpu.VMEM((1, lengths.shape[1]), jnp.int32),
+            pltpu.VMEM((1, lengths.shape[1]), jnp.int32),
+            pltpu.VMEM((tok_rows, width), BF16),
+            pltpu.VMEM((block_rows, width), BF16),
+            pltpu.VMEM((stored, rank, columns), BF16),
+            pltpu.SemaphoreType.DMA((6,)),
+        ],
+        compiler_params=pltpu.CompilerParams(vmem_limit_bytes=VMEM_LIMIT),
+    )(
         lengths,
         request_adapter_index.reshape(1, -1),
         tokens,
-        adapter_down_weight,
+        adapter_down_weight.reshape(stored * doubled_rank, width),
         adapter_up_weight,
     )
-    factors = lax.all_gather(factors, "ad", axis_index_groups=along_x, tiled=True)
     recv = lax.all_to_all(send, "ad", 0, 0, axis_index_groups=along_z, tiled=True)
-    partial_value = jnp.dot(tokens, key_value_weight, preferred_element_type=F32)
-    base = lax.psum_scatter(partial_value.astype(BF16), "tp", scatter_dimension=1, tiled=True)
+    factors = [factors] + [
+        lax.ppermute(
+            factors, "ad", [(z * N_X + x, z * N_X + (x ^ s)) for z in range(n_z) for x in range(N_X)]
+        )
+        for s in range(1, N_X)
+    ]
+
+    def swap(array, mask):
+        return lax.ppermute(array, "tp", [(j, j ^ mask) for j in range(n_tp)])
+
+    def blocks(count, kind):
+        return jax.ShapeDtypeStruct((count, tok_rows, columns), kind)
+
+    keep, out = call(base_kernel, (blocks(4, BF16), blocks(4, BF16)), place, tokens, key_value_weight)
+    keep, out = call(halve_kernel, (blocks(2, F32), blocks(2, BF16)), keep, swap(out, 1))
+    keep, out = call(halve_kernel, (blocks(1, F32), blocks(1, BF16)), keep, swap(out, 2))
+    base_recv = swap(out, 6)
     parts, lane_ids = call(
         project,
         (
@@ -185,10 +268,11 @@
             jax.ShapeDtypeStruct((8, rows), F32),
         ),
         recv,
-        factors,
+        *factors,
+        base_recv,
     )
     parts = lax.all_to_all(parts, "tp", 0, 0, tiled=True)
-    delta = call(delta_kernel, jax.ShapeDtypeStruct((rows, columns), BF16), parts, lane_ids, factors)
+    delta = call(apply_up, jax.ShapeDtypeStruct((rows, columns), BF16), parts, lane_ids, *factors)
     back = lax.all_to_all(
         delta.reshape(n_z, cap, columns), "ad", 0, 0, axis_index_groups=along_z, tiled=True
     )
@@ -197,7 +281,8 @@
         jax.ShapeDtypeStruct((tok_rows, columns), BF16),
         place,
         back.reshape(rows, columns),
-        base,
+        keep,
+        base_recv,
     )
 
 

time: 116 us -> 103 us (0.89)
  the two profiles are of different devices: /device:TPU:6 before, /device:TPU:64 now
where the time goes in v3:
time: 103 us; the launch traced here: 102 us
  blocking collectives  42.8 us (42%)
  starting transfers between devices  34.7 us (34%)
  waiting for transfers between devices  14 us (14%)
  local copies, waits for them, and re-layouts  5.64 us (5%)
  Pallas kernels  5.12 us (5%)
    all_to_all x1, blocking collectives, local(): lax.all_to_all(delta.reshape(n_z, cap, columns), 'ad', 0, 0, axis_index_g...  32.3 us
    all_to_all x1, starting transfers between devices, local(): lax.all_to_all(send, 'ad', 0, 0, axis_index_groups=along_z, tiled=True)  14.8 us
    ppermute x3, waiting for transfers between devices, local(): lax.ppermute(factors, 'ad', [(z * N_X + x, z * N_X + (x ^ s)) for z in ra...  12.2 us
    all_to_all x1, blocking collectives, local(): parts = lax.all_to_all(parts, 'tp', 0, 0, tiled=True)  10.5 us
    ppermute x3, starting transfers between devices, local(): lax.ppermute(factors, 'ad', [(z * N_X + x, z * N_X + (x ^ s)) for z in ra...  10.4 us
    ppermute x3, starting transfers between devices, swap(): return lax.ppermute(array, 'tp', [(j, j ^ mask) for j in range(n_tp)])  9.5 us
    unnamed x14, local copies, waits for them, and re-layouts  5.64 us
    pallas_call x6, Pallas kernels, call(): pl.pallas_call(kernel, out_shape=out_shape, compiler_params=pltpu.Compile...  3.31 us
  transfers between devices with their start and end apart: 7, of which 3 were waited for; matrix products, arithmetic and copies ran while one was open for 0% of the time, Pallas kernels for 1%

profile of v3, /device:TPU:64, one launch (start us, length us, event | category | flops | bytes accessed | tf_op | source)
XLA Modules:
  0.0 102.4 jit_solution(3826615036160813615)
XLA Ops:
  0.0 0.0 copy-start.1
  0.0 0.9 copy-done.1
  1.0 0.0 copy-start.3
  1.0 0.9 copy-done.3
  1.9 0.0 copy-start.4
  1.9 0.8 copy-done.4
  2.7 0.0 copy-start.5
  2.7 0.7 copy-done.5
  3.4 0.0 copy-start.6
  3.4 0.7 copy-done.6
  4.1 0.0 copy-start.2
  4.1 1.8 %shard_map.64 = (bf16[16,168,128]{2,1,0:T(8,128)(2,1)}, s32[8,256]{1,0:T(8,128)S(1)}, bf16[320,512]{1,0:T(8,128)(2,1)S(1)}) custom-call(s32[1,64]{1,0:T(1,128)S(1)} %copy-done.5, s32[1,64]{1,0:T(1,128)S(1)} %bitcast.7, bf16[256,512]{1,0:T(8,128)(2,1)S(1)} %copy-done.1, bf16[256,512]{1,0:T(8,128)(2,1)S(1)} %bitcast.6, bf16[8,16,256]{2,1,0:T(8,128)(2,1)S(1)} %copy-done.4), custom_call_target="tpu_custom_call" | custom-call | tf_op jit(solution)/shard_map/pallas_call | solution.py:221
  5.9 14.8 %all-to-all-start = ((bf16[16,168,128]{2,1,0:T(8,128)(2,1)}), bf16[16,168,128]{2,1,0:T(8,128)(2,1)S(1)}, u32[]{:S(2)}, u32[]{:S(2)}) async-start(bf16[16,168,128]{2,1,0:T(8,128)(2,1)} %get-tuple-element.17), calls=%async_computation | async-start | bytes 1376256 | tf_op jit(solution)/shard_map/all_to_all | solution.py:246
  20.6 0.0 copy-done.2
  20.6 0.0 copy-start
  20.7 1.6 %copy-done = bf16[512,2048]{1,0:T(8,128)(2,1)S(1)} copy-done((bf16[512,2048]{1,0:T(8,128)(2,1)S(1)}, bf16[512,2048]{1,0:T(8,128)(2,1)}, u32[]{:S(2)}) %copy-start) | copy-done | bytes 2097176
  22.2 0.7 shard_map.65
  23.0 1.9 %collective-permute-start.3 = (bf16[4,256,256]{2,1,0:T(8,128)(2,1)S(1)}, bf16[4,256,256]{2,1,0:T(8,128)(2,1)S(1)}, u32[]{:S(2)}, u32[]{:S(2)}) collective-permute-start(bf16[4,256,256]{2,1,0:T(8,128)(2,1)S(1)} %get-tuple-element.20), channel_id=1, source_target_pairs={{0,64},{64,0},{128,192},{192,128},{256,320},{320,256},{384,448},{4... | collective-permute-start | bytes 1572872 | tf_op jit(solution)/shard_map/ppermute | solution.py:255
  24.9 1.9 %collective-permute-done.3.recv_ref = bf16[4,256,256]{2,1,0:T(8,128)(2,1)S(1)} collective-permute-done((bf16[4,256,256]{2,1,0:T(8,128)(2,1)S(1)}, bf16[4,256,256]{2,1,0:T(8,128)(2,1)S(1)}, u32[]{:S(2)}, u32[]{:S(2)}) %collective-permute-start.3) | collective-permute-done | bytes 524320 | tf_op jit(solution)/shard_map/ppermute | solution.py:255
  26.8 0.1 shard_map.66
  26.9 3.5 %collective-permute-start.4 = (bf16[2,256,256]{2,1,0:T(8,128)(2,1)S(1)}, bf16[2,256,256]{2,1,0:T(8,128)(2,1)S(1)}, u32[]{:S(2)}, u32[]{:S(2)}) collective-permute-start(bf16[2,256,256]{2,1,0:T(8,128)(2,1)S(1)} %get-tuple-element.22), channel_id=1, source_target_pairs={{0,128},{64,192},{128,0},{192,64},{256,384},{320,448},{384,256},{4... | collective-permute-start | bytes 786440 | tf_op jit(solution)/shard_map/ppermute | solution.py:255
  30.4 3.4 %collective-permute-start = (bf16[320,512]{1,0:T(8,128)(2,1)S(1)}, bf16[320,512]{1,0:T(8,128)(2,1)S(1)}, u32[]{:S(2)}, u32[]{:S(2)}) collective-permute-start(bf16[320,512]{1,0:T(8,128)(2,1)S(1)} %get-tuple-element.18.refs_1_.refs_2_), channel_id=1, source_target_pairs={{0,1},{1,0},{2,3},{3,2},{4,5},{5,4},{6,7},{7,6},{8,9},{9,8},{10,11... | collective-permute-start | bytes 983048 | tf_op jit(solution)/shard_map/ppermute | solution.py:248
  33.8 4.6 %collective-permute-start.1 = (bf16[320,512]{1,0:T(8,128)(2,1)S(1)}, bf16[320,512]{1,0:T(8,128)(2,1)S(1)}, u32[]{:S(2)}, u32[]{:S(2)}) collective-permute-start(bf16[320,512]{1,0:T(8,128)(2,1)S(1)} %get-tuple-element.18.refs_1_.refs_2_), channel_id=1, source_target_pairs={{0,2},{1,3},{2,0},{3,1},{4,6},{5,7},{6,4},{7,5},{8,10},{9,11},{10,... | collective-permute-start | bytes 983048 | tf_op jit(solution)/shard_map/ppermute | solution.py:248
  38.5 2.4 %collective-permute-start.2 = (bf16[320,512]{1,0:T(8,128)(2,1)S(1)}, bf16[320,512]{1,0:T(8,128)(2,1)S(1)}, u32[]{:S(2)}, u32[]{:S(2)}) collective-permute-start(bf16[320,512]{1,0:T(8,128)(2,1)S(1)} %get-tuple-element.18.refs_1_.refs_2_), channel_id=1, source_target_pairs={{0,3},{1,2},{2,1},{3,0},{4,7},{5,6},{6,5},{7,4},{8,11},{9,10},{10,... | collective-permute-start | bytes 983048 | tf_op jit(solution)/shard_map/ppermute | solution.py:248
  40.8 0.0 collective-permute-done.4.recv_ref
  40.9 4.1 %collective-permute-start.5 = (bf16[1,256,256]{2,1,0:T(8,128)(2,1)S(1)}, bf16[1,256,256]{2,1,0:T(8,128)(2,1)S(1)}, u32[]{:S(2)}, u32[]{:S(2)}) collective-permute-start(bf16[1,256,256]{2,1,0:T(8,128)(2,1)S(1)} %get-tuple-element.23), channel_id=1, source_target_pairs={{0,384},{64,448},{128,256},{192,320},{256,128},{320,192},{384,0},{... | collective-permute-start | bytes 393224 | tf_op jit(solution)/shard_map/ppermute | solution.py:255
  45.0 0.0 collective-permute-done.refs_2_.refs_3_
  45.0 6.1 %collective-permute-done.1.refs_3_.refs_4_ = bf16[320,512]{1,0:T(8,128)(2,1)S(1)} collective-permute-done((bf16[320,512]{1,0:T(8,128)(2,1)S(1)}, bf16[320,512]{1,0:T(8,128)(2,1)S(1)}, u32[]{:S(2)}, u32[]{:S(2)}) %collective-permute-start.1) | collective-permute-done | bytes 327712 | tf_op jit(solution)/shard_map/ppermute | solution.py:248
  51.1 6.1 %collective-permute-done.2.refs_4_.refs_5_ = bf16[320,512]{1,0:T(8,128)(2,1)S(1)} collective-permute-done((bf16[320,512]{1,0:T(8,128)(2,1)S(1)}, bf16[320,512]{1,0:T(8,128)(2,1)S(1)}, u32[]{:S(2)}, u32[]{:S(2)}) %collective-permute-start.2) | collective-permute-done | bytes 327712 | tf_op jit(solution)/shard_map/ppermute | solution.py:248
  57.2 0.0 collective-permute-done.5.refs_5_.recv_ref
  57.2 0.0 all-to-all-done.refs_0_
  57.2 1.1 %shard_map.68 = (bf16[8,16,640]{2,1,0:T(8,128)(2,1)S(1)}, f32[8,640]{1,0:T(8,128)S(1)}) custom-call(bf16[16,168,128]{2,1,0:T(8,128)(2,1)S(1)} %all-to-all-done.refs_0_, bf16[320,512]{1,0:T(8,128)(2,1)S(1)} %get-tuple-element.18.refs_1_.refs_2_, bf16[320,512]{1,0:T(8,128)(2,1)S(1)} %collective-permute-done.refs_2_.refs_3_, ...), custom_call_target="tpu_custom_call" | custom-call | tf_op jit(solution)/shard_map/pallas_call | solution.py:187
  58.3 10.5 %all_to_all.15.refs_0_ = bf16[8,16,640]{2,1,0:T(8,128)(2,1)S(1)} all-to-all(bf16[8,16,640]{2,1,0:T(8,128)(2,1)S(1)} %get-tuple-element.24), channel_id=1, replica_groups=mesh['tp'=8,'ad'=64] {'tp'}, dimensions={0} | all-to-all | bytes 327680 | tf_op jit(solution)/shard_map/all_to_all | solution.py:274
  68.7 0.4 shard_map.69
  69.1 32.3 %all_to_all.16 = bf16[16,40,256]{2,1,0:T(8,128)(2,1)S(1)} all-to-all(bf16[16,40,256]{2,1,0:T(8,128)(2,1)S(1)} %bitcast.4), channel_id=1, replica_groups={{0,4,8,12,16,20,24,28,32,36,40,44,48,52,56,60},{1,5,9,13,17,21,25,29,33..., dimensions={0} | all-to-all | bytes 655360 | tf_op jit(solution)/shard_map/all_to_all | solution.py:276
  101.4 1.0 shard_map.70
  (1 shorter events, 0.0 us)
Async XLA Ops:
  0.0 0.9 copy-start.1
  1.0 0.9 copy-start.3
  1.9 0.8 copy-start.4
  2.7 0.7 copy-start.5
  3.4 0.7 copy-start.6
  4.1 16.6 %copy-start.2 = (bf16[256,512]{1,0:T(8,128)(2,1)S(1)}, bf16[256,512]{1,0:T(8,128)(2,1)}, u32[]{:S(2)}) copy-start(bf16[256,512]{1,0:T(8,128)(2,1)} %tokens_ref.1) | copy-start | bytes 786436
  5.9 51.3 %all-to-all-start = ((bf16[16,168,128]{2,1,0:T(8,128)(2,1)}), bf16[16,168,128]{2,1,0:T(8,128)(2,1)S(1)}, u32[]{:S(2)}, u32[]{:S(2)}) async-start(bf16[16,168,128]{2,1,0:T(8,128)(2,1)} %get-tuple-element.17), calls=%async_computation | async-start | bytes 1376256 | tf_op jit(solution)/shard_map/all_to_all | solution.py:246
  20.6 1.6 %copy-start = (bf16[512,2048]{1,0:T(8,128)(2,1)S(1)}, bf16[512,2048]{1,0:T(8,128)(2,1)}, u32[]{:S(2)}) copy-start(bf16[512,2048]{1,0:T(8,128)(2,1)} %weight_ref.1) | copy-start | bytes 6291460
  23.0 3.8 %collective-permute-start.3 = (bf16[4,256,256]{2,1,0:T(8,128)(2,1)S(1)}, bf16[4,256,256]{2,1,0:T(8,128)(2,1)S(1)}, u32[]{:S(2)}, u32[]{:S(2)}) collective-permute-start(bf16[4,256,256]{2,1,0:T(8,128)(2,1)S(1)} %get-tuple-element.20), channel_id=1, source_target_pairs={{0,64},{64,0},{128,192},{192,128},{256,320},{320,256},{384,448},{4... | collective-permute-start | bytes 1572872 | tf_op jit(solution)/shard_map/ppermute | solution.py:255
  26.9 13.9 %collective-permute-start.4 = (bf16[2,256,256]{2,1,0:T(8,128)(2,1)S(1)}, bf16[2,256,256]{2,1,0:T(8,128)(2,1)S(1)}, u32[]{:S(2)}, u32[]{:S(2)}) collective-permute-start(bf16[2,256,256]{2,1,0:T(8,128)(2,1)S(1)} %get-tuple-element.22), channel_id=1, source_target_pairs={{0,128},{64,192},{128,0},{192,64},{256,384},{320,448},{384,256},{4... | collective-permute-start | bytes 786440 | tf_op jit(solution)/shard_map/ppermute | solution.py:255
  30.4 14.6 %collective-permute-start = (bf16[320,512]{1,0:T(8,128)(2,1)S(1)}, bf16[320,512]{1,0:T(8,128)(2,1)S(1)}, u32[]{:S(2)}, u32[]{:S(2)}) collective-permute-start(bf16[320,512]{1,0:T(8,128)(2,1)S(1)} %get-tuple-element.18.refs_1_.refs_2_), channel_id=1, source_target_pairs={{0,1},{1,0},{2,3},{3,2},{4,5},{5,4},{6,7},{7,6},{8,9},{9,8},{10,11... | collective-permute-start | bytes 983048 | tf_op jit(solution)/shard_map/ppermute | solution.py:248
  33.8 17.3 %collective-permute-start.1 = (bf16[320,512]{1,0:T(8,128)(2,1)S(1)}, bf16[320,512]{1,0:T(8,128)(2,1)S(1)}, u32[]{:S(2)}, u32[]{:S(2)}) collective-permute-start(bf16[320,512]{1,0:T(8,128)(2,1)S(1)} %get-tuple-element.18.refs_1_.refs_2_), channel_id=1, source_target_pairs={{0,2},{1,3},{2,0},{3,1},{4,6},{5,7},{6,4},{7,5},{8,10},{9,11},{10,... | collective-permute-start | bytes 983048 | tf_op jit(solution)/shard_map/ppermute | solution.py:248
  38.5 18.7 %collective-permute-start.2 = (bf16[320,512]{1,0:T(8,128)(2,1)S(1)}, bf16[320,512]{1,0:T(8,128)(2,1)S(1)}, u32[]{:S(2)}, u32[]{:S(2)}) collective-permute-start(bf16[320,512]{1,0:T(8,128)(2,1)S(1)} %get-tuple-element.18.refs_1_.refs_2_), channel_id=1, source_target_pairs={{0,3},{1,2},{2,1},{3,0},{4,7},{5,6},{6,5},{7,4},{8,11},{9,10},{10,... | collective-permute-start | bytes 983048 | tf_op jit(solution)/shard_map/ppermute | solution.py:248
  40.9 16.3 %collective-permute-start.5 = (bf16[1,256,256]{2,1,0:T(8,128)(2,1)S(1)}, bf16[1,256,256]{2,1,0:T(8,128)(2,1)S(1)}, u32[]{:S(2)}, u32[]{:S(2)}) collective-permute-start(bf16[1,256,256]{2,1,0:T(8,128)(2,1)S(1)} %get-tuple-element.23), channel_id=1, source_target_pairs={{0,384},{64,448},{128,256},{192,320},{256,128},{320,192},{384,0},{... | collective-permute-start | bytes 393224 | tf_op jit(solution)/shard_map/ppermute | solution.py:255

commit v4 on v3

--- a/solution.py
+++ b/solution.py
@@ -107,7 +107,8 @@
         keep_ref[k] = block(relative)
 
 
-def halve_kernel(keep_ref, recv_ref, kept_ref, send_ref):
+def halve_kernel(after_ref, keep_ref, recv_ref, kept_ref, send_ref):
+    del after_ref
     half = kept_ref.shape[0]
     for k in range(half):
         kept_ref[k] = keep_ref[k].astype(F32) + recv_ref[k].astype(F32)
@@ -153,7 +154,7 @@
 
 
 def delta_kernel(
-    stored, parts_ref, lane_ids_ref, f0_ref, f1_ref, f2_ref, f3_ref, out_ref
+    stored, parts_ref, lane_ids_ref, f0_ref, f1_ref, f2_ref, f3_ref, out_ref, mark_ref
 ):
     low = parts_ref[0].astype(F32)
     for j in range(1, parts_ref.shape[0]):
@@ -172,6 +173,7 @@
         jnp.concatenate(spread, axis=0), jnp.concatenate(up, axis=0), TN, preferred_element_type=F32
     )
     out_ref[...] = product.astype(BF16)
+    mark_ref[...] = jnp.zeros(mark_ref.shape, F32)
 
 
 def mix_kernel(place_ref, back_ref, kept_ref, recv_ref, out_ref):
@@ -237,11 +239,16 @@
         ],
         compiler_params=pltpu.CompilerParams(vmem_limit_bytes=VMEM_LIMIT),
     )(
-        lengths,
-        request_adapter_index.reshape(1, -1),
-        tokens,
-        adapter_down_weight.reshape(stored * doubled_rank, width),
-        adapter_up_weight,
+        *(
+            pltpu.with_memory_space_constraint(array, pltpu.HBM)
+            for array in (
+                lengths,
+                request_adapter_index.reshape(1, -1),
+                tokens,
+                adapter_down_weight.reshape(stored * doubled_rank, width),
+                adapter_up_weight,
+            )
+        )
     )
     recv = lax.all_to_all(send, "ad", 0, 0, axis_index_groups=along_z, tiled=True)
     factors = [factors] + [
@@ -258,9 +265,7 @@
         return jax.ShapeDtypeStruct((count, tok_rows, columns), kind)
 
     keep, out = call(base_kernel, (blocks(4, BF16), blocks(4, BF16)), place, tokens, key_value_weight)
-    keep, out = call(halve_kernel, (blocks(2, F32), blocks(2, BF16)), keep, swap(out, 1))
-    keep, out = call(halve_kernel, (blocks(1, F32), blocks(1, BF16)), keep, swap(out, 2))
-    base_recv = swap(out, 6)
+    out_recv = swap(out, 1)
     parts, lane_ids = call(
         project,
         (
@@ -269,10 +274,22 @@
         ),
         recv,
         *factors,
-        base_recv,
+        out_recv,
     )
     parts = lax.all_to_all(parts, "tp", 0, 0, tiled=True)
-    delta = call(apply_up, jax.ShapeDtypeStruct((rows, columns), BF16), parts, lane_ids, *factors)
+    delta, mark = call(
+        apply_up,
+        (
+            jax.ShapeDtypeStruct((rows, columns), BF16),
+            jax.ShapeDtypeStruct((8, LANES), F32),
+        ),
+        parts,
+        lane_ids,
+        *factors,
+    )
+    keep, out = call(halve_kernel, (blocks(2, F32), blocks(2, BF16)), mark, keep, out_recv)
+    keep, out = call(halve_kernel, (blocks(1, F32), blocks(1, BF16)), mark, keep, swap(out, 2))
+    base_recv = swap(out, 6)
     back = lax.all_to_all(
         delta.reshape(n_z, cap, columns), "ad", 0, 0, axis_index_groups=along_z, tiled=True
     )

time: 103 us -> 94.9 us (0.921)
  the two profiles are of different devices: /device:TPU:64 before, /device:TPU:6 now
where the time goes in v4:
time: 94.9 us; the launch traced here: 94.4 us
  starting transfers between devices  39.9 us (42%)
  waiting for transfers between devices  35.5 us (37%)
  blocking collectives  10.8 us (11%)
  Pallas kernels  6.5 us (7%)
  local copies, waits for them, and re-layouts  1.59 us (2%)
    all_to_all x1, starting transfers between devices, local(): lax.all_to_all(send, 'ad', 0, 0, axis_index_groups=along_z, tiled=True)  15.2 us
    ppermute x3, waiting for transfers between devices, local(): lax.ppermute(factors, 'ad', [(z * N_X + x, z * N_X + (x ^ s)) for z in ra...  12.9 us
    ppermute x3, waiting for transfers between devices, swap(): return lax.ppermute(array, 'tp', [(j, j ^ mask) for j in range(n_tp)])  11.9 us
    all_to_all x1, blocking collectives, local(): parts = lax.all_to_all(parts, 'tp', 0, 0, tiled=True)  10.8 us
    ppermute x3, starting transfers between devices, local(): lax.ppermute(factors, 'ad', [(z * N_X + x, z * N_X + (x ^ s)) for z in ra...  9.82 us
    all_to_all x1, waiting for transfers between devices, local(): lax.all_to_all(send, 'ad', 0, 0, axis_index_groups=along_z, tiled=True)  7.92 us
    ppermute x3, starting transfers between devices, swap(): return lax.ppermute(array, 'tp', [(j, j ^ mask) for j in range(n_tp)])  7.47 us
    all_to_all x1, starting transfers between devices, local(): lax.all_to_all(delta.reshape(n_z, cap, columns), 'ad', 0, 0, axis_index_g...  7.44 us
  transfers between devices with their start and end apart: 8, of which 6 were waited for; matrix products, arithmetic and copies ran while one was open for 0% of the time, Pallas kernels for 1%

profile of v4, /device:TPU:6, one launch (start us, length us, event | category | flops | bytes accessed | tf_op | source)
XLA Modules:
  0.0 94.4 jit_solution(2037142274598540156)
XLA Ops:
  0.0 0.0 copy-start.1
  0.0 2.5 %shard_map.64 = (bf16[16,168,128]{2,1,0:T(8,128)(2,1)}, s32[8,256]{1,0:T(8,128)S(1)}, bf16[320,512]{1,0:T(8,128)(2,1)S(1)}) custom-call(s32[1,64]{1,0:T(1,128)} %refs_0_.1, s32[1,64]{1,0:T(1,128)} %bitcast.6, bf16[256,512]{1,0:T(8,128)(2,1)} %tokens_ref.1, bf16[256,512]{1,0:T(8,128)(2,1)} %bitcast.5, bf16[8,16,256]{2,1,0:T(8,128)(2,1)} %refs_4_.1), custom_call_target="tpu_custom_call" | custom-call | tf_op jit(solution)/shard_map/pallas_call | solution.py:223
  2.5 15.2 %all-to-all-start = ((bf16[16,168,128]{2,1,0:T(8,128)(2,1)}), bf16[16,168,128]{2,1,0:T(8,128)(2,1)S(1)}, u32[]{:S(2)}, u32[]{:S(2)}) async-start(bf16[16,168,128]{2,1,0:T(8,128)(2,1)} %get-tuple-element.19), calls=%async_computation | async-start | bytes 1376256 | tf_op jit(solution)/shard_map/all_to_all | solution.py:253
  17.7 0.0 copy-done.1
  17.7 0.0 copy-start
  17.7 1.6 %copy-done = bf16[512,2048]{1,0:T(8,128)(2,1)S(1)} copy-done((bf16[512,2048]{1,0:T(8,128)(2,1)S(1)}, bf16[512,2048]{1,0:T(8,128)(2,1)}, u32[]{:S(2)}) %copy-start) | copy-done | bytes 2097176
  19.3 0.7 shard_map.65
  20.0 1.9 %collective-permute-start.3 = (bf16[4,256,256]{2,1,0:T(8,128)(2,1)S(1)}, bf16[4,256,256]{2,1,0:T(8,128)(2,1)S(1)}, u32[]{:S(2)}, u32[]{:S(2)}) collective-permute-start(bf16[4,256,256]{2,1,0:T(8,128)(2,1)S(1)} %get-tuple-element.21), channel_id=1, source_target_pairs={{0,64},{64,0},{128,192},{192,128},{256,320},{320,256},{384,448},{4... | collective-permute-start | bytes 1572872 | tf_op jit(solution)/shard_map/ppermute | solution.py:262
  22.0 2.4 %collective-permute-start.2 = (bf16[320,512]{1,0:T(8,128)(2,1)S(1)}, bf16[320,512]{1,0:T(8,128)(2,1)S(1)}, u32[]{:S(2)}, u32[]{:S(2)}) collective-permute-start(bf16[320,512]{1,0:T(8,128)(2,1)S(1)} %get-tuple-element.20.refs_1_.refs_2_), channel_id=1, source_target_pairs={{0,3},{1,2},{2,1},{3,0},{4,7},{5,6},{6,5},{7,4},{8,11},{9,10},{10,... | collective-permute-start | bytes 983048 | tf_op jit(solution)/shard_map/ppermute | solution.py:255
  24.4 4.3 %collective-permute-start.1 = (bf16[320,512]{1,0:T(8,128)(2,1)S(1)}, bf16[320,512]{1,0:T(8,128)(2,1)S(1)}, u32[]{:S(2)}, u32[]{:S(2)}) collective-permute-start(bf16[320,512]{1,0:T(8,128)(2,1)S(1)} %get-tuple-element.20.refs_1_.refs_2_), channel_id=1, source_target_pairs={{0,2},{1,3},{2,0},{3,1},{4,6},{5,7},{6,4},{7,5},{8,10},{9,11},{10,... | collective-permute-start | bytes 983048 | tf_op jit(solution)/shard_map/ppermute | solution.py:255
  28.7 3.1 %collective-permute-start = (bf16[320,512]{1,0:T(8,128)(2,1)S(1)}, bf16[320,512]{1,0:T(8,128)(2,1)S(1)}, u32[]{:S(2)}, u32[]{:S(2)}) collective-permute-start(bf16[320,512]{1,0:T(8,128)(2,1)S(1)} %get-tuple-element.20.refs_1_.refs_2_), channel_id=1, source_target_pairs={{0,1},{1,0},{2,3},{3,2},{4,5},{5,4},{6,7},{7,6},{8,9},{9,8},{10,11... | collective-permute-start | bytes 983048 | tf_op jit(solution)/shard_map/ppermute | solution.py:255
  31.8 10.4 %collective-permute-done.2.refs_4_.refs_5_ = bf16[320,512]{1,0:T(8,128)(2,1)S(1)} collective-permute-done((bf16[320,512]{1,0:T(8,128)(2,1)S(1)}, bf16[320,512]{1,0:T(8,128)(2,1)S(1)}, u32[]{:S(2)}, u32[]{:S(2)}) %collective-permute-start.2) | collective-permute-done | bytes 327712 | tf_op jit(solution)/shard_map/ppermute | solution.py:255
  42.2 0.0 collective-permute-done.1.refs_3_.refs_4_
  42.2 2.5 %collective-permute-done.refs_2_.refs_3_ = bf16[320,512]{1,0:T(8,128)(2,1)S(1)} collective-permute-done((bf16[320,512]{1,0:T(8,128)(2,1)S(1)}, bf16[320,512]{1,0:T(8,128)(2,1)S(1)}, u32[]{:S(2)}, u32[]{:S(2)}) %collective-permute-start) | collective-permute-done | bytes 327712 | tf_op jit(solution)/shard_map/ppermute | solution.py:255
  44.7 0.0 collective-permute-done.3.refs_5_.recv_ref
  44.7 7.9 %all-to-all-done.refs_0_ = bf16[16,168,128]{2,1,0:T(8,128)(2,1)S(1)} async-done(((bf16[16,168,128]{2,1,0:T(8,128)(2,1)}), bf16[16,168,128]{2,1,0:T(8,128)(2,1)S(1)}, u32[]{:S(2)}, u32[]{:S(2)}) %all-to-all-start) | async-done | bytes 688160 | tf_op jit(solution)/shard_map/all_to_all | solution.py:253
  52.7 1.1 %shard_map.66 = (bf16[8,16,640]{2,1,0:T(8,128)(2,1)S(1)}, f32[8,640]{1,0:T(8,128)S(1)}) custom-call(bf16[16,168,128]{2,1,0:T(8,128)(2,1)S(1)} %all-to-all-done.refs_0_, bf16[320,512]{1,0:T(8,128)(2,1)S(1)} %get-tuple-element.20.refs_1_.refs_2_, bf16[320,512]{1,0:T(8,128)(2,1)S(1)} %collective-permute-done.refs_2_.refs_3_, ...), custom_call_target="tpu_custom_call" | custom-call | tf_op jit(solution)/shard_map/pallas_call | solution.py:189
  53.7 10.8 %all_to_all.15.refs_0_ = bf16[8,16,640]{2,1,0:T(8,128)(2,1)S(1)} all-to-all(bf16[8,16,640]{2,1,0:T(8,128)(2,1)S(1)} %get-tuple-element.22), channel_id=1, replica_groups=mesh['tp'=8,'ad'=64] {'tp'}, dimensions={0} | all-to-all | bytes 327680 | tf_op jit(solution)/shard_map/all_to_all | solution.py:279
  64.5 1.1 %shard_map.67 = (bf16[640,256]{1,0:T(8,128)(2,1)}, f32[8,128]{1,0:T(8,128)S(1)}) custom-call(bf16[8,16,640]{2,1,0:T(8,128)(2,1)S(1)} %all_to_all.15.refs_0_, f32[8,640]{1,0:T(8,128)S(1)} %get-tuple-element.23.refs_1_, bf16[320,512]{1,0:T(8,128)(2,1)S(1)} %get-tuple-element.20.refs_1_.refs_2_, bf16[320,512]{1,0:T(8,128)(2,1)S(1)} %collective-permute-done.refs_2_.refs_3_, ...), custom_call_target="tpu_custom_call" | custom-call | tf_op jit(solution)/shard_map/pallas_call | solution.py:189
  65.6 7.4 %all-to-all-start.2 = ((bf16[16,40,256]{2,1,0:T(8,128)(2,1)}), bf16[16,40,256]{2,1,0:T(8,128)(2,1)S(1)}, u32[]{:S(2)}, u32[]{:S(2)}) async-start(bf16[16,40,256]{2,1,0:T(8,128)(2,1)} %bitcast.2), calls=%async_computation.2 | async-start | bytes 655360 | tf_op jit(solution)/shard_map/all_to_all | solution.py:293
  73.0 0.1 shard_map.68
  73.2 2.5 %collective-permute-start.4 = (bf16[2,256,256]{2,1,0:T(8,128)(2,1)S(1)}, bf16[2,256,256]{2,1,0:T(8,128)(2,1)S(1)}, u32[]{:S(2)}, u32[]{:S(2)}) collective-permute-start(bf16[2,256,256]{2,1,0:T(8,128)(2,1)S(1)} %get-tuple-element.28), channel_id=1, source_target_pairs={{0,128},{64,192},{128,0},{192,64},{256,384},{320,448},{384,256},{4... | collective-permute-start | bytes 786440 | tf_op jit(solution)/shard_map/ppermute | solution.py:262
  75.7 6.9 %collective-permute-done.4.recv_ref = bf16[2,256,256]{2,1,0:T(8,128)(2,1)S(1)} collective-permute-done((bf16[2,256,256]{2,1,0:T(8,128)(2,1)S(1)}, bf16[2,256,256]{2,1,0:T(8,128)(2,1)S(1)}, u32[]{:S(2)}, u32[]{:S(2)}) %collective-permute-start.4) | collective-permute-done | bytes 262176 | tf_op jit(solution)/shard_map/ppermute | solution.py:262
  82.6 3.1 %collective-permute-start.5 = (bf16[1,256,256]{2,1,0:T(8,128)(2,1)S(1)}, bf16[1,256,256]{2,1,0:T(8,128)(2,1)S(1)}, u32[]{:S(2)}, u32[]{:S(2)}) collective-permute-start(bf16[1,256,256]{2,1,0:T(8,128)(2,1)S(1)} %get-tuple-element.30), channel_id=1, source_target_pairs={{0,384},{64,448},{128,256},{192,320},{256,128},{320,192},{384,0},{... | collective-permute-start | bytes 393224 | tf_op jit(solution)/shard_map/ppermute | solution.py:262
  85.7 5.0 %collective-permute-done.5.recv_ref = bf16[1,256,256]{2,1,0:T(8,128)(2,1)S(1)} collective-permute-done((bf16[1,256,256]{2,1,0:T(8,128)(2,1)S(1)}, bf16[1,256,256]{2,1,0:T(8,128)(2,1)S(1)}, u32[]{:S(2)}, u32[]{:S(2)}) %collective-permute-start.5) | collective-permute-done | bytes 131104 | tf_op jit(solution)/shard_map/ppermute | solution.py:262
  90.7 2.7 %all-to-all-done.2 = bf16[16,40,256]{2,1,0:T(8,128)(2,1)S(1)} async-done(((bf16[16,40,256]{2,1,0:T(8,128)(2,1)}), bf16[16,40,256]{2,1,0:T(8,128)(2,1)S(1)}, u32[]{:S(2)}, u32[]{:S(2)}) %all-to-all-start.2) | async-done | bytes 327712 | tf_op jit(solution)/shard_map/all_to_all | solution.py:293
  93.4 1.0 %shard_map.70 = bf16[256,256]{1,0:T(8,128)(2,1)} custom-call(s32[8,256]{1,0:T(8,128)S(1)} %get-tuple-element.18.place_ref, bf16[640,256]{1,0:T(8,128)(2,1)S(1)} %bitcast.4, f32[1,256,256]{2,1,0:T(8,128)S(1)} %get-tuple-element.29.kept_ref, bf16[1,256,256]{2,1,0:T(8,128)(2,1)S(1)} %collective-permute-done.5.recv_ref), custom_call_target="tpu_custom_call" | custom-call | tf_op jit(solution)/shard_map/pallas_call | solution.py:189
  (1 shorter events, 0.0 us)
Async XLA Ops:
  0.0 17.7 %copy-start.1 = (bf16[256,512]{1,0:T(8,128)(2,1)S(1)}, bf16[256,512]{1,0:T(8,128)(2,1)}, u32[]{:S(2)}) copy-start(bf16[256,512]{1,0:T(8,128)(2,1)} %tokens_ref.1) | copy-start | bytes 786436
  2.5 50.2 %all-to-all-start = ((bf16[16,168,128]{2,1,0:T(8,128)(2,1)}), bf16[16,168,128]{2,1,0:T(8,128)(2,1)S(1)}, u32[]{:S(2)}, u32[]{:S(2)}) async-start(bf16[16,168,128]{2,1,0:T(8,128)(2,1)} %get-tuple-element.19), calls=%async_computation | async-start | bytes 1376256 | tf_op jit(solution)/shard_map/all_to_all | solution.py:253
  17.7 1.6 %copy-start = (bf16[512,2048]{1,0:T(8,128)(2,1)S(1)}, bf16[512,2048]{1,0:T(8,128)(2,1)}, u32[]{:S(2)}) copy-start(bf16[512,2048]{1,0:T(8,128)(2,1)} %weight_ref.1) | copy-start | bytes 6291460
  20.0 24.7 %collective-permute-start.3 = (bf16[4,256,256]{2,1,0:T(8,128)(2,1)S(1)}, bf16[4,256,256]{2,1,0:T(8,128)(2,1)S(1)}, u32[]{:S(2)}, u32[]{:S(2)}) collective-permute-start(bf16[4,256,256]{2,1,0:T(8,128)(2,1)S(1)} %get-tuple-element.21), channel_id=1, source_target_pairs={{0,64},{64,0},{128,192},{192,128},{256,320},{320,256},{384,448},{4... | collective-permute-start | bytes 1572872 | tf_op jit(solution)/shard_map/ppermute | solution.py:262
  22.0 20.2 %collective-permute-start.2 = (bf16[320,512]{1,0:T(8,128)(2,1)S(1)}, bf16[320,512]{1,0:T(8,128)(2,1)S(1)}, u32[]{:S(2)}, u32[]{:S(2)}) collective-permute-start(bf16[320,512]{1,0:T(8,128)(2,1)S(1)} %get-tuple-element.20.refs_1_.refs_2_), channel_id=1, source_target_pairs={{0,3},{1,2},{2,1},{3,0},{4,7},{5,6},{6,5},{7,4},{8,11},{9,10},{10,... | collective-permute-start | bytes 983048 | tf_op jit(solution)/shard_map/ppermute | solution.py:255
  24.4 17.8 %collective-permute-start.1 = (bf16[320,512]{1,0:T(8,128)(2,1)S(1)}, bf16[320,512]{1,0:T(8,128)(2,1)S(1)}, u32[]{:S(2)}, u32[]{:S(2)}) collective-permute-start(bf16[320,512]{1,0:T(8,128)(2,1)S(1)} %get-tuple-element.20.refs_1_.refs_2_), channel_id=1, source_target_pairs={{0,2},{1,3},{2,0},{3,1},{4,6},{5,7},{6,4},{7,5},{8,10},{9,11},{10,... | collective-permute-start | bytes 983048 | tf_op jit(solution)/shard_map/ppermute | solution.py:255
  28.7 16.0 %collective-permute-start = (bf16[320,512]{1,0:T(8,128)(2,1)S(1)}, bf16[320,512]{1,0:T(8,128)(2,1)S(1)}, u32[]{:S(2)}, u32[]{:S(2)}) collective-permute-start(bf16[320,512]{1,0:T(8,128)(2,1)S(1)} %get-tuple-element.20.refs_1_.refs_2_), channel_id=1, source_target_pairs={{0,1},{1,0},{2,3},{3,2},{4,5},{5,4},{6,7},{7,6},{8,9},{9,8},{10,11... | collective-permute-start | bytes 983048 | tf_op jit(solution)/shard_map/ppermute | solution.py:255
  65.6 27.8 %all-to-all-start.2 = ((bf16[16,40,256]{2,1,0:T(8,128)(2,1)}), bf16[16,40,256]{2,1,0:T(8,128)(2,1)S(1)}, u32[]{:S(2)}, u32[]{:S(2)}) async-start(bf16[16,40,256]{2,1,0:T(8,128)(2,1)} %bitcast.2), calls=%async_computation.2 | async-start | bytes 655360 | tf_op jit(solution)/shard_map/all_to_all | solution.py:293
  73.2 9.4 %collective-permute-start.4 = (bf16[2,256,256]{2,1,0:T(8,128)(2,1)S(1)}, bf16[2,256,256]{2,1,0:T(8,128)(2,1)S(1)}, u32[]{:S(2)}, u32[]{:S(2)}) collective-permute-start(bf16[2,256,256]{2,1,0:T(8,128)(2,1)S(1)} %get-tuple-element.28), channel_id=1, source_target_pairs={{0,128},{64,192},{128,0},{192,64},{256,384},{320,448},{384,256},{4... | collective-permute-start | bytes 786440 | tf_op jit(solution)/shard_map/ppermute | solution.py:262
  82.6 8.1 %collective-permute-start.5 = (bf16[1,256,256]{2,1,0:T(8,128)(2,1)S(1)}, bf16[1,256,256]{2,1,0:T(8,128)(2,1)S(1)}, u32[]{:S(2)}, u32[]{:S(2)}) collective-permute-start(bf16[1,256,256]{2,1,0:T(8,128)(2,1)S(1)} %get-tuple-element.30), channel_id=1, source_target_pairs={{0,384},{64,448},{128,256},{192,320},{256,128},{320,192},{384,0},{... | collective-permute-start | bytes 393224 | tf_op jit(solution)/shard_map/ppermute | solution.py:262

commit v5 on v4

--- a/solution.py
+++ b/solution.py
@@ -8,6 +8,7 @@
 ADAPTER_SCALE = 2.0
 N_X = 4
 MAXLEN = 8
+CHAIN = 1
 
 F32 = jnp.float32
 BF16 = jnp.bfloat16
@@ -22,7 +23,7 @@
 
 
 def pack_kernel(
-    planes, cap, per_plane,
+    planes, cap, stored,
     lens_hbm, index_hbm, tokens_hbm, down_hbm, up_hbm,
     send_ref, place_ref, factors_hbm,
     lens_ref, index_ref, tokens_ref, block_ref, up_ref, sems,
@@ -51,17 +52,38 @@
     ends = jnp.sum(jnp.where(r1 <= r0, lens, 0.0), axis=1, keepdims=True)
     starts = jnp.sum(jnp.where(r1 < r0, lens, 0.0), axis=1, keepdims=True)
     index_col = jnp.sum(jnp.where(r1 == r0, index, 0.0), axis=1, keepdims=True)
+    owner = jnp.floor(index_col * (1.0 / stored))
+    same_earlier = (owner == jnp.floor(index * (1.0 / stored))) & (r1 < r0)
+    first = jnp.sum(jnp.where(same_earlier, 1.0, 0.0), axis=1, keepdims=True) == 0.0
+    within = index_col - owner * stored
+    home = jnp.floor(owner * (1.0 / N_X))
+    column = owner - home * N_X
+    lane = iota((requests, planes), 1).astype(F32)
+    counts = jnp.sum(jnp.where(home == lane, 1.0, 0.0), axis=0, keepdims=True)
+    number = lane[0:1]
+    over = jnp.sum(jnp.where(counts > N_X, number, 0.0), axis=1, keepdims=True)
+    under = jnp.sum(jnp.where(counts < N_X, number, 0.0), axis=1, keepdims=True)
+
+    def ahead(steps):
+        steps = steps * CHAIN
+        return jnp.where(steps < 0.0, steps + planes, steps)
+
+    my_x = lax.axis_index("ad") % N_X
+    relative = (column.astype(jnp.int32) ^ my_x).astype(F32)
+    in_chain = ahead(home - over) < ahead(under - over)
+    handed = in_chain & first & (relative == 0.0)
+    target = jnp.where(handed, home + CHAIN, home)
+    target = jnp.where(target < 0.0, target + planes, target)
+    target = jnp.where(target >= planes, target - planes, target)
+    block = jnp.where(handed, float(N_X), relative) * stored + within
     t = iota((requests, rows), 1).astype(F32)
     inside = (t >= starts) & (t < ends)
-    adapter = jnp.sum(jnp.where(inside, index_col, 0.0), axis=0, keepdims=True)
-    plane = jnp.floor(adapter * (1.0 / per_plane))
-    local = (adapter - plane * per_plane).astype(jnp.int32)
-    my_x = lax.axis_index("ad") % N_X
-    local = (local ^ (my_x * (per_plane // N_X))).astype(F32)
+    plane = jnp.sum(jnp.where(inside, target, 0.0), axis=0, keepdims=True)
+    local = jnp.sum(jnp.where(inside, block, 0.0), axis=0, keepdims=True)
     member = iota((planes, rows), 0).astype(F32) == plane
     before = (iota((rows, rows), 0) < iota((rows, rows), 1)).astype(F32).astype(BF16)
-    counts = jnp.dot(member.astype(F32).astype(BF16), before, preferred_element_type=F32)
-    rank_in = jnp.sum(jnp.where(member, counts, 0.0), axis=0, keepdims=True)
+    earlier = jnp.dot(member.astype(F32).astype(BF16), before, preferred_element_type=F32)
+    rank_in = jnp.sum(jnp.where(member, earlier, 0.0), axis=0, keepdims=True)
     place = (plane * cap + rank_in).astype(jnp.int32)
     place_ref[...] = jnp.broadcast_to(place, place_ref.shape)
     select = (iota((planes * cap, rows), 0) == place).astype(F32).astype(BF16)
@@ -116,7 +138,8 @@
 
 
 def low_kernel(
-    planes, cap, stored, recv_ref, f0_ref, f1_ref, f2_ref, f3_ref, kept_ref, out_ref, lane_ids_ref
+    planes, cap, stored, recv_ref, f0_ref, f1_ref, f2_ref, f3_ref,
+    handed_ref, kept_ref, out_ref, lane_ids_ref
 ):
     del kept_ref
     rows = planes * cap
@@ -140,7 +163,7 @@
     n, rank = out_ref.shape[:2]
     doubled = 2 * rank
     low = jnp.zeros((doubled, rows), F32)
-    for x, factors_ref in enumerate((f0_ref, f1_ref, f2_ref, f3_ref)):
+    for x, factors_ref in enumerate((f0_ref, f1_ref, f2_ref, f3_ref, handed_ref)):
         block = factors_ref[: stored * doubled, :]
         values = lax.dot_general(block, recv, NT, preferred_element_type=F32)
         for a in range(stored):
@@ -154,7 +177,8 @@
 
 
 def delta_kernel(
-    stored, parts_ref, lane_ids_ref, f0_ref, f1_ref, f2_ref, f3_ref, out_ref, mark_ref
+    stored, parts_ref, lane_ids_ref, f0_ref, f1_ref, f2_ref, f3_ref,
+    handed_ref, out_ref, mark_ref
 ):
     low = parts_ref[0].astype(F32)
     for j in range(1, parts_ref.shape[0]):
@@ -163,7 +187,7 @@
     columns = out_ref.shape[1]
     ids = lane_ids_ref[0:1, :]
     spread, up = [], []
-    for x, factors_ref in enumerate((f0_ref, f1_ref, f2_ref, f3_ref)):
+    for x, factors_ref in enumerate((f0_ref, f1_ref, f2_ref, f3_ref, handed_ref)):
         for side in range(2):
             up.append(factors_ref[stored * 2 * rank :, side * columns : (side + 1) * columns])
             for pair in range(stored // 2):
@@ -185,12 +209,17 @@
     out_ref[...] = (base + ADAPTER_SCALE * delta).astype(BF16)
 
 
-def call(kernel, out_shape, *args):
+def call(kernel, out_shape, *args, cost=None):
     return pl.pallas_call(
         kernel,
         out_shape=out_shape,
         compiler_params=pltpu.CompilerParams(vmem_limit_bytes=VMEM_LIMIT),
+        cost_estimate=cost,
     )(*args)
+
+
+def in_hbm(array):
+    return pltpu.with_memory_space_constraint(array, pltpu.HBM)
 
 
 def local(
@@ -202,14 +231,13 @@
     n_z = n_ad // N_X
     stored, doubled_rank, _ = adapter_down_weight.shape
     rank, columns = adapter_up_weight.shape[1:]
-    per_plane = stored * N_X
-    cap = (N_X + 1) * MAXLEN
+    cap = N_X * MAXLEN
     rows = n_z * cap
     along_x = [[z * N_X + x for x in range(N_X)] for z in range(n_z)]
     along_z = [[z * N_X + x for z in range(n_z)] for x in range(N_X)]
 
     def pack(*refs):
-        pack_kernel(n_z, cap, per_plane, *refs)
+        pack_kernel(n_z, cap, stored, *refs)
 
     def project(*refs):
         low_kernel(n_z, cap, stored, *refs)
@@ -258,13 +286,20 @@
         for s in range(1, N_X)
     ]
 
+    handed = lax.ppermute(
+        factors[0],
+        "ad",
+        [(z * N_X + x, (z + CHAIN) % n_z * N_X + x) for z in range(n_z) for x in range(N_X)],
+    )
+
     def swap(array, mask):
         return lax.ppermute(array, "tp", [(j, j ^ mask) for j in range(n_tp)])
 
     def blocks(count, kind):
         return jax.ShapeDtypeStruct((count, tok_rows, columns), kind)
 
-    keep, out = call(base_kernel, (blocks(4, BF16), blocks(4, BF16)), place, tokens, key_value_weight)
+    much = pl.CostEstimate(flops=4 * 10**10, bytes_accessed=tokens.size, transcendentals=0)
+    keep, out = call(base_kernel, (blocks(4, BF16), blocks(4, BF16)), handed, in_hbm(tokens), in_hbm(key_value_weight), cost=much)
     out_recv = swap(out, 1)
     parts, lane_ids = call(
         project,
@@ -274,6 +309,7 @@
         ),
         recv,
         *factors,
+        handed,
         out_recv,
     )
     parts = lax.all_to_all(parts, "tp", 0, 0, tiled=True)
@@ -286,6 +322,7 @@
         parts,
         lane_ids,
         *factors,
+        handed,
     )
     keep, out = call(halve_kernel, (blocks(2, F32), blocks(2, BF16)), mark, keep, out_recv)
     keep, out = call(halve_kernel, (blocks(1, F32), blocks(1, BF16)), mark, keep, swap(out, 2))

time: 94.9 us -> 92 us (0.969)
  waiting for transfers between devices: 35.5 us -> 28 us
  starting transfers between devices: 39.9 us -> 45 us
  local copies, waits for them, and re-layouts: 1.59 us -> 0 us
  Pallas kernels: 6.5 us -> 7.94 us
    all_to_all x1, waiting for transfers between devices: 7.92 us -> 1.52 us  [local(): lax.all_to_all(send, 'ad', 0, 0, axis_index_groups=along_z, tiled=True)]
    ppermute x0 -> x1, starting transfers between devices: none -> 3.82 us  [local(): lax.ppermute(factors[0], 'ad', [(z * N_X + x, (z + CHAIN) % n_z * N_X + x...]
    all_to_all x1, starting transfers between devices: 7.44 us -> 9.55 us  [local(): lax.all_to_all(delta.reshape(n_z, cap, columns), 'ad', 0, 0, axis_index_g...]
    all_to_all x1, waiting for transfers between devices: 2.71 us -> 0.63 us  [local(): lax.all_to_all(delta.reshape(n_z, cap, columns), 'ad', 0, 0, axis_index_g...]
    unnamed x4 -> x0, local copies, waits for them, and re-layouts: 1.59 us -> none
    pallas_call x6, Pallas kernels: 4.03 us -> 5.57 us  [call(): pl.pallas_call(kernel, out_shape=out_shape, compiler_params=pltpu.Compile...]
    ppermute x0 -> x1, waiting for transfers between devices: none -> 0.96 us  [local(): lax.ppermute(factors[0], 'ad', [(z * N_X + x, (z + CHAIN) % n_z * N_X + x...]
  transfers between devices with their start and end apart: 8 -> 9, of which waited for: 6 -> 7; matrix products, arithmetic and copies ran while one was open for 0% -> 0% of each run, Pallas kernels for 1% -> 3%
where the time goes in v5:
time: 92 us; the launch traced here: 91.4 us
  starting transfers between devices  45 us (49%)
  waiting for transfers between devices  28 us (30%)
  blocking collectives  10.4 us (11%)
  Pallas kernels  7.94 us (9%)
    all_to_all x1, starting transfers between devices, local(): lax.all_to_all(send, 'ad', 0, 0, axis_index_groups=along_z, tiled=True)  14.3 us
    ppermute x3, waiting for transfers between devices, local(): lax.ppermute(factors, 'ad', [(z * N_X + x, z * N_X + (x ^ s)) for z in ra...  12.9 us
    ppermute x3, waiting for transfers between devices, swap(): return lax.ppermute(array, 'tp', [(j, j ^ mask) for j in range(n_tp)])  12 us
    all_to_all x1, blocking collectives, local(): parts = lax.all_to_all(parts, 'tp', 0, 0, tiled=True)  10.4 us
    ppermute x3, starting transfers between devices, local(): lax.ppermute(factors, 'ad', [(z * N_X + x, z * N_X + (x ^ s)) for z in ra...  9.82 us
    all_to_all x1, starting transfers between devices, local(): lax.all_to_all(delta.reshape(n_z, cap, columns), 'ad', 0, 0, axis_index_g...  9.55 us
    ppermute x3, starting transfers between devices, swap(): return lax.ppermute(array, 'tp', [(j, j ^ mask) for j in range(n_tp)])  7.47 us
    pallas_call x6, Pallas kernels, call(): pl.pallas_call(kernel, out_shape=out_shape, compiler_params=pltpu.Compile...  5.57 us
  transfers between devices with their start and end apart: 9, of which 7 were waited for; matrix products, arithmetic and copies ran while one was open for 0% of the time, Pallas kernels for 3%

profile of v5, /device:TPU:6, one launch (start us, length us, event | category | flops | bytes accessed | tf_op | source)
XLA Modules:
  0.0 91.4 jit_solution(16158623221671171910)
XLA Ops:
  0.0 2.4 %shard_map.64 = (bf16[16,136,128]{2,1,0:T(8,128)(2,1)}, s32[8,256]{1,0:T(8,128)S(1)}, bf16[320,512]{1,0:T(8,128)(2,1)S(1)}) custom-call(s32[1,64]{1,0:T(1,128)} %refs_0_.1, s32[1,64]{1,0:T(1,128)} %bitcast.6, bf16[256,512]{1,0:T(8,128)(2,1)} %tokens_ref.1, bf16[256,512]{1,0:T(8,128)(2,1)} %bitcast.5, bf16[8,16,256]{2,1,0:T(8,128)(2,1)} %refs_4_.1), custom_call_target="tpu_custom_call" | custom-call | tf_op jit(solution)/shard_map/pallas_call | solution.py:251
  2.4 3.8 %collective-permute-start.3 = (bf16[320,512]{1,0:T(8,128)(2,1)S(1)}, bf16[320,512]{1,0:T(8,128)(2,1)S(1)}, u32[]{:S(2)}, u32[]{:S(2)}) collective-permute-start(bf16[320,512]{1,0:T(8,128)(2,1)S(1)} %get-tuple-element.20.refs_1_.refs_2_), channel_id=1, source_target_pairs={{0,4},{1,5},{2,6},{3,7},{4,8},{5,9},{6,10},{7,11},{8,12},{9,13},{1... | collective-permute-start | bytes 983048 | tf_op jit(solution)/shard_map/ppermute | solution.py:289
  6.2 14.3 %all-to-all-start = ((bf16[16,136,128]{2,1,0:T(8,128)(2,1)}), bf16[16,136,128]{2,1,0:T(8,128)(2,1)S(1)}, u32[]{:S(2)}, u32[]{:S(2)}) async-start(bf16[16,136,128]{2,1,0:T(8,128)(2,1)} %get-tuple-element.19), calls=%async_computation | async-start | bytes 1114112 | tf_op jit(solution)/shard_map/all_to_all | solution.py:281
  20.5 1.0 %collective-permute-done.3.place_ref.refs_5_.refs_6_ = bf16[320,512]{1,0:T(8,128)(2,1)S(1)} collective-permute-done((bf16[320,512]{1,0:T(8,128)(2,1)S(1)}, bf16[320,512]{1,0:T(8,128)(2,1)S(1)}, u32[]{:S(2)}, u32[]{:S(2)}) %collective-permute-start.3) | collective-permute-done | bytes 327712 | tf_op jit(solution)/shard_map/ppermute | solution.py:289
  21.5 2.4 %shard_map.65 = (bf16[4,256,256]{2,1,0:T(8,128)(2,1)S(1)}, bf16[4,256,256]{2,1,0:T(8,128)(2,1)S(1)}) custom-call(bf16[320,512]{1,0:T(8,128)(2,1)S(1)} %collective-permute-done.3.place_ref.refs_5_.refs_6_, bf16[256,512]{1,0:T(8,128)(2,1)} %tokens_ref.1, bf16[512,2048]{1,0:T(8,128)(2,1)} %weight_ref.1), custom_call_target="tpu_custom_call" | custom-call | flops 40000000000 | bytes 131072 | tf_op jit(solution)/shard_map/pallas_call | solution.py:213
  23.9 1.9 %collective-permute-start.4 = (bf16[4,256,256]{2,1,0:T(8,128)(2,1)S(1)}, bf16[4,256,256]{2,1,0:T(8,128)(2,1)S(1)}, u32[]{:S(2)}, u32[]{:S(2)}) collective-permute-start(bf16[4,256,256]{2,1,0:T(8,128)(2,1)S(1)} %get-tuple-element.21), channel_id=1, source_target_pairs={{0,64},{64,0},{128,192},{192,128},{256,320},{320,256},{384,448},{4... | collective-permute-start | bytes 1572872 | tf_op jit(solution)/shard_map/ppermute | solution.py:296
  25.8 2.4 %collective-permute-start.2 = (bf16[320,512]{1,0:T(8,128)(2,1)S(1)}, bf16[320,512]{1,0:T(8,128)(2,1)S(1)}, u32[]{:S(2)}, u32[]{:S(2)}) collective-permute-start(bf16[320,512]{1,0:T(8,128)(2,1)S(1)} %get-tuple-element.20.refs_1_.refs_2_), channel_id=1, source_target_pairs={{0,3},{1,2},{2,1},{3,0},{4,7},{5,6},{6,5},{7,4},{8,11},{9,10},{10,... | collective-permute-start | bytes 983048 | tf_op jit(solution)/shard_map/ppermute | solution.py:283
  28.2 4.3 %collective-permute-start.1 = (bf16[320,512]{1,0:T(8,128)(2,1)S(1)}, bf16[320,512]{1,0:T(8,128)(2,1)S(1)}, u32[]{:S(2)}, u32[]{:S(2)}) collective-permute-start(bf16[320,512]{1,0:T(8,128)(2,1)S(1)} %get-tuple-element.20.refs_1_.refs_2_), channel_id=1, source_target_pairs={{0,2},{1,3},{2,0},{3,1},{4,6},{5,7},{6,4},{7,5},{8,10},{9,11},{10,... | collective-permute-start | bytes 983048 | tf_op jit(solution)/shard_map/ppermute | solution.py:283
  32.6 3.1 %collective-permute-start = (bf16[320,512]{1,0:T(8,128)(2,1)S(1)}, bf16[320,512]{1,0:T(8,128)(2,1)S(1)}, u32[]{:S(2)}, u32[]{:S(2)}) collective-permute-start(bf16[320,512]{1,0:T(8,128)(2,1)S(1)} %get-tuple-element.20.refs_1_.refs_2_), channel_id=1, source_target_pairs={{0,1},{1,0},{2,3},{3,2},{4,5},{5,4},{6,7},{7,6},{8,9},{9,8},{10,11... | collective-permute-start | bytes 983048 | tf_op jit(solution)/shard_map/ppermute | solution.py:283
  35.7 10.4 %collective-permute-done.2.refs_4_.refs_5_ = bf16[320,512]{1,0:T(8,128)(2,1)S(1)} collective-permute-done((bf16[320,512]{1,0:T(8,128)(2,1)S(1)}, bf16[320,512]{1,0:T(8,128)(2,1)S(1)}, u32[]{:S(2)}, u32[]{:S(2)}) %collective-permute-start.2) | collective-permute-done | bytes 327712 | tf_op jit(solution)/shard_map/ppermute | solution.py:283
  46.1 0.0 collective-permute-done.1.refs_3_.refs_4_
  46.1 2.5 %collective-permute-done.refs_2_.refs_3_ = bf16[320,512]{1,0:T(8,128)(2,1)S(1)} collective-permute-done((bf16[320,512]{1,0:T(8,128)(2,1)S(1)}, bf16[320,512]{1,0:T(8,128)(2,1)S(1)}, u32[]{:S(2)}, u32[]{:S(2)}) %collective-permute-start) | collective-permute-done | bytes 327712 | tf_op jit(solution)/shard_map/ppermute | solution.py:283
  48.6 0.0 collective-permute-done.4.refs_6_.recv_ref
  48.6 1.5 %all-to-all-done.refs_0_ = bf16[16,136,128]{2,1,0:T(8,128)(2,1)S(1)} async-done(((bf16[16,136,128]{2,1,0:T(8,128)(2,1)}), bf16[16,136,128]{2,1,0:T(8,128)(2,1)S(1)}, u32[]{:S(2)}, u32[]{:S(2)}) %all-to-all-start) | async-done | bytes 557088 | tf_op jit(solution)/shard_map/all_to_all | solution.py:281
  50.1 0.9 %shard_map.66 = (bf16[8,16,512]{2,1,0:T(8,128)(2,1)S(1)}, f32[8,512]{1,0:T(8,128)S(1)}) custom-call(bf16[16,136,128]{2,1,0:T(8,128)(2,1)S(1)} %all-to-all-done.refs_0_, bf16[320,512]{1,0:T(8,128)(2,1)S(1)} %get-tuple-element.20.refs_1_.refs_2_, bf16[320,512]{1,0:T(8,128)(2,1)S(1)} %collective-permute-done.refs_2_.refs_3_, ...), custom_call_target="tpu_custom_call" | custom-call | tf_op jit(solution)/shard_map/pallas_call | solution.py:213
  51.1 10.4 %all_to_all.15.refs_0_ = bf16[8,16,512]{2,1,0:T(8,128)(2,1)S(1)} all-to-all(bf16[8,16,512]{2,1,0:T(8,128)(2,1)S(1)} %get-tuple-element.22), channel_id=1, replica_groups=mesh['tp'=8,'ad'=64] {'tp'}, dimensions={0} | all-to-all | bytes 262144 | tf_op jit(solution)/shard_map/all_to_all | solution.py:315
  61.5 1.1 %shard_map.67 = (bf16[512,256]{1,0:T(8,128)(2,1)}, f32[8,128]{1,0:T(8,128)S(1)}) custom-call(bf16[8,16,512]{2,1,0:T(8,128)(2,1)S(1)} %all_to_all.15.refs_0_, f32[8,512]{1,0:T(8,128)S(1)} %get-tuple-element.23.refs_1_, bf16[320,512]{1,0:T(8,128)(2,1)S(1)} %get-tuple-element.20.refs_1_.refs_2_, bf16[320,512]{1,0:T(8,128)(2,1)S(1)} %collective-permute-done.refs_2_.refs_3_, ...), custom_call_target="tpu_custom_call" | custom-call | tf_op jit(solution)/shard_map/pallas_call | solution.py:213
  62.6 9.6 %all-to-all-start.2 = ((bf16[16,32,256]{2,1,0:T(8,128)(2,1)}), bf16[16,32,256]{2,1,0:T(8,128)(2,1)S(1)}, u32[]{:S(2)}, u32[]{:S(2)}) async-start(bf16[16,32,256]{2,1,0:T(8,128)(2,1)} %bitcast.2), calls=%async_computation.2 | async-start | bytes 524288 | tf_op jit(solution)/shard_map/all_to_all | solution.py:330
  72.2 0.1 shard_map.68
  72.3 2.5 %collective-permute-start.5 = (bf16[2,256,256]{2,1,0:T(8,128)(2,1)S(1)}, bf16[2,256,256]{2,1,0:T(8,128)(2,1)S(1)}, u32[]{:S(2)}, u32[]{:S(2)}) collective-permute-start(bf16[2,256,256]{2,1,0:T(8,128)(2,1)S(1)} %get-tuple-element.28), channel_id=1, source_target_pairs={{0,128},{64,192},{128,0},{192,64},{256,384},{320,448},{384,256},{4... | collective-permute-start | bytes 786440 | tf_op jit(solution)/shard_map/ppermute | solution.py:296
  74.8 7.0 %collective-permute-done.5.recv_ref = bf16[2,256,256]{2,1,0:T(8,128)(2,1)S(1)} collective-permute-done((bf16[2,256,256]{2,1,0:T(8,128)(2,1)S(1)}, bf16[2,256,256]{2,1,0:T(8,128)(2,1)S(1)}, u32[]{:S(2)}, u32[]{:S(2)}) %collective-permute-start.5) | collective-permute-done | bytes 262176 | tf_op jit(solution)/shard_map/ppermute | solution.py:296
  81.8 3.1 %collective-permute-start.6 = (bf16[1,256,256]{2,1,0:T(8,128)(2,1)S(1)}, bf16[1,256,256]{2,1,0:T(8,128)(2,1)S(1)}, u32[]{:S(2)}, u32[]{:S(2)}) collective-permute-start(bf16[1,256,256]{2,1,0:T(8,128)(2,1)S(1)} %get-tuple-element.30), channel_id=1, source_target_pairs={{0,384},{64,448},{128,256},{192,320},{256,128},{320,192},{384,0},{... | collective-permute-start | bytes 393224 | tf_op jit(solution)/shard_map/ppermute | solution.py:296
  84.9 5.0 %collective-permute-done.6.recv_ref = bf16[1,256,256]{2,1,0:T(8,128)(2,1)S(1)} collective-permute-done((bf16[1,256,256]{2,1,0:T(8,128)(2,1)S(1)}, bf16[1,256,256]{2,1,0:T(8,128)(2,1)S(1)}, u32[]{:S(2)}, u32[]{:S(2)}) %collective-permute-start.6) | collective-permute-done | bytes 131104 | tf_op jit(solution)/shard_map/ppermute | solution.py:296
  89.9 0.6 all-to-all-done.2
  90.5 0.9 %shard_map.70 = bf16[256,256]{1,0:T(8,128)(2,1)} custom-call(s32[8,256]{1,0:T(8,128)S(1)} %get-tuple-element.18.place_ref, bf16[512,256]{1,0:T(8,128)(2,1)S(1)} %bitcast.4, f32[1,256,256]{2,1,0:T(8,128)S(1)} %get-tuple-element.29.kept_ref, bf16[1,256,256]{2,1,0:T(8,128)(2,1)S(1)} %collective-permute-done.6.recv_ref), custom_call_target="tpu_custom_call" | custom-call | tf_op jit(solution)/shard_map/pallas_call | solution.py:213
  (1 shorter events, 0.0 us)
Async XLA Ops:
  2.4 19.1 %collective-permute-start.3 = (bf16[320,512]{1,0:T(8,128)(2,1)S(1)}, bf16[320,512]{1,0:T(8,128)(2,1)S(1)}, u32[]{:S(2)}, u32[]{:S(2)}) collective-permute-start(bf16[320,512]{1,0:T(8,128)(2,1)S(1)} %get-tuple-element.20.refs_1_.refs_2_), channel_id=1, source_target_pairs={{0,4},{1,5},{2,6},{3,7},{4,8},{5,9},{6,10},{7,11},{8,12},{9,13},{1... | collective-permute-start | bytes 983048 | tf_op jit(solution)/shard_map/ppermute | solution.py:289
  6.2 43.9 %all-to-all-start = ((bf16[16,136,128]{2,1,0:T(8,128)(2,1)}), bf16[16,136,128]{2,1,0:T(8,128)(2,1)S(1)}, u32[]{:S(2)}, u32[]{:S(2)}) async-start(bf16[16,136,128]{2,1,0:T(8,128)(2,1)} %get-tuple-element.19), calls=%async_computation | async-start | bytes 1114112 | tf_op jit(solution)/shard_map/all_to_all | solution.py:281
  23.9 24.7 %collective-permute-start.4 = (bf16[4,256,256]{2,1,0:T(8,128)(2,1)S(1)}, bf16[4,256,256]{2,1,0:T(8,128)(2,1)S(1)}, u32[]{:S(2)}, u32[]{:S(2)}) collective-permute-start(bf16[4,256,256]{2,1,0:T(8,128)(2,1)S(1)} %get-tuple-element.21), channel_id=1, source_target_pairs={{0,64},{64,0},{128,192},{192,128},{256,320},{320,256},{384,448},{4... | collective-permute-start | bytes 1572872 | tf_op jit(solution)/shard_map/ppermute | solution.py:296
  25.8 20.2 %collective-permute-start.2 = (bf16[320,512]{1,0:T(8,128)(2,1)S(1)}, bf16[320,512]{1,0:T(8,128)(2,1)S(1)}, u32[]{:S(2)}, u32[]{:S(2)}) collective-permute-start(bf16[320,512]{1,0:T(8,128)(2,1)S(1)} %get-tuple-element.20.refs_1_.refs_2_), channel_id=1, source_target_pairs={{0,3},{1,2},{2,1},{3,0},{4,7},{5,6},{6,5},{7,4},{8,11},{9,10},{10,... | collective-permute-start | bytes 983048 | tf_op jit(solution)/shard_map/ppermute | solution.py:283
  28.2 17.9 %collective-permute-start.1 = (bf16[320,512]{1,0:T(8,128)(2,1)S(1)}, bf16[320,512]{1,0:T(8,128)(2,1)S(1)}, u32[]{:S(2)}, u32[]{:S(2)}) collective-permute-start(bf16[320,512]{1,0:T(8,128)(2,1)S(1)} %get-tuple-element.20.refs_1_.refs_2_), channel_id=1, source_target_pairs={{0,2},{1,3},{2,0},{3,1},{4,6},{5,7},{6,4},{7,5},{8,10},{9,11},{10,... | collective-permute-start | bytes 983048 | tf_op jit(solution)/shard_map/ppermute | solution.py:283
  32.6 16.0 %collective-permute-start = (bf16[320,512]{1,0:T(8,128)(2,1)S(1)}, bf16[320,512]{1,0:T(8,128)(2,1)S(1)}, u32[]{:S(2)}, u32[]{:S(2)}) collective-permute-start(bf16[320,512]{1,0:T(8,128)(2,1)S(1)} %get-tuple-element.20.refs_1_.refs_2_), channel_id=1, source_target_pairs={{0,1},{1,0},{2,3},{3,2},{4,5},{5,4},{6,7},{7,6},{8,9},{9,8},{10,11... | collective-permute-start | bytes 983048 | tf_op jit(solution)/shard_map/ppermute | solution.py:283
  62.6 27.9 %all-to-all-start.2 = ((bf16[16,32,256]{2,1,0:T(8,128)(2,1)}), bf16[16,32,256]{2,1,0:T(8,128)(2,1)S(1)}, u32[]{:S(2)}, u32[]{:S(2)}) async-start(bf16[16,32,256]{2,1,0:T(8,128)(2,1)} %bitcast.2), calls=%async_computation.2 | async-start | bytes 524288 | tf_op jit(solution)/shard_map/all_to_all | solution.py:330
  72.3 9.5 %collective-permute-start.5 = (bf16[2,256,256]{2,1,0:T(8,128)(2,1)S(1)}, bf16[2,256,256]{2,1,0:T(8,128)(2,1)S(1)}, u32[]{:S(2)}, u32[]{:S(2)}) collective-permute-start(bf16[2,256,256]{2,1,0:T(8,128)(2,1)S(1)} %get-tuple-element.28), channel_id=1, source_target_pairs={{0,128},{64,192},{128,0},{192,64},{256,384},{320,448},{384,256},{4... | collective-permute-start | bytes 786440 | tf_op jit(solution)/shard_map/ppermute | solution.py:296
  81.8 8.1 %collective-permute-start.6 = (bf16[1,256,256]{2,1,0:T(8,128)(2,1)S(1)}, bf16[1,256,256]{2,1,0:T(8,128)(2,1)S(1)}, u32[]{:S(2)}, u32[]{:S(2)}) collective-permute-start(bf16[1,256,256]{2,1,0:T(8,128)(2,1)S(1)} %get-tuple-element.30), channel_id=1, source_target_pairs={{0,384},{64,448},{128,256},{192,320},{256,128},{320,192},{384,0},{... | collective-permute-start | bytes 393224 | tf_op jit(solution)/shard_map/ppermute | solution.py:296

commit v6 on v5

--- a/solution.py
+++ b/solution.py
@@ -129,12 +129,11 @@
         keep_ref[k] = block(relative)
 
 
-def halve_kernel(after_ref, keep_ref, recv_ref, kept_ref, send_ref):
+def pair_kernel(after_ref, keep_ref, recv_ref, kept_ref, *send_refs):
     del after_ref
-    half = kept_ref.shape[0]
-    for k in range(half):
-        kept_ref[k] = keep_ref[k].astype(F32) + recv_ref[k].astype(F32)
-        send_ref[k] = (keep_ref[half + k].astype(F32) + recv_ref[half + k].astype(F32)).astype(BF16)
+    kept_ref[0] = keep_ref[0].astype(F32) + recv_ref[0].astype(F32)
+    for k, send_ref in enumerate(send_refs, 1):
+        send_ref[0] = (keep_ref[k].astype(F32) + recv_ref[k].astype(F32)).astype(BF16)
 
 
 def low_kernel(
@@ -200,12 +199,14 @@
     mark_ref[...] = jnp.zeros(mark_ref.shape, F32)
 
 
-def mix_kernel(place_ref, back_ref, kept_ref, recv_ref, out_ref):
+def mix_kernel(place_ref, back_ref, kept_ref, r0_ref, r1_ref, r2_ref, out_ref):
     rows = out_ref.shape[0]
     place = place_ref[0:1, :]
     select = (iota((back_ref.shape[0], rows), 0) == place).astype(F32).astype(BF16)
     delta = lax.dot_general(select, back_ref[...], TN, preferred_element_type=F32)
-    base = kept_ref[0] + recv_ref[0].astype(F32)
+    base = kept_ref[0]
+    for recv_ref in (r0_ref, r1_ref, r2_ref):
+        base = base + recv_ref[0].astype(F32)
     out_ref[...] = (base + ADAPTER_SCALE * delta).astype(BF16)
 
 
@@ -324,9 +325,10 @@
         *factors,
         handed,
     )
-    keep, out = call(halve_kernel, (blocks(2, F32), blocks(2, BF16)), mark, keep, out_recv)
-    keep, out = call(halve_kernel, (blocks(1, F32), blocks(1, BF16)), mark, keep, swap(out, 2))
-    base_recv = swap(out, 6)
+    shares = call(pair_kernel, (blocks(1, F32),) + (blocks(1, BF16),) * 3, mark, keep, out_recv)
+    shares = shares[:1] + tuple(
+        swap(share, mask) for share, mask in zip(shares[1:], (6, 2, 4), strict=True)
+    )
     back = lax.all_to_all(
         delta.reshape(n_z, cap, columns), "ad", 0, 0, axis_index_groups=along_z, tiled=True
     )
@@ -335,8 +337,7 @@
         jax.ShapeDtypeStruct((tok_rows, columns), BF16),
         place,
         back.reshape(rows, columns),
-        keep,
-        base_recv,
+        *shares,
     )
 
 

time: 92 us -> 92 us (level)
  waiting for transfers between devices: 28 us -> 23.2 us
  starting transfers between devices: 45 us -> 49.8 us
    ppermute x3 -> x4, waiting for transfers between devices: 12 us -> 3.8 us  [swap(): return lax.ppermute(array, 'tp', [(j, j ^ mask) for j in range(n_tp)])]
    ppermute x3 -> x4, starting transfers between devices: 7.47 us -> 12.3 us  [swap(): return lax.ppermute(array, 'tp', [(j, j ^ mask) for j in range(n_tp)])]
    all_to_all x1, waiting for transfers between devices: 0.63 us -> 3.96 us  [local(): lax.all_to_all(delta.reshape(n_z, cap, columns), 'ad', 0, 0, axis_index_g...]
    pallas_call x6 -> x5, Pallas kernels: 5.57 us -> 5.53 us  [call(): pl.pallas_call(kernel, out_shape=out_shape, compiler_params=pltpu.Compile...]
  transfers between devices with their start and end apart: 9 -> 10, of which waited for: 7 -> 6; matrix products, arithmetic and copies ran while one was open for 0% -> 0% of each run, Pallas kernels for 3% -> 3%
where the time goes in v6:
time: 92 us; the launch traced here: 91.4 us
  starting transfers between devices  49.8 us (54%)
  waiting for transfers between devices  23.2 us (25%)
  blocking collectives  10.4 us (11%)
  Pallas kernels  7.9 us (9%)
    all_to_all x1, starting transfers between devices, local(): lax.all_to_all(send, 'ad', 0, 0, axis_index_groups=along_z, tiled=True)  14.3 us
    ppermute x3, waiting for transfers between devices, local(): lax.ppermute(factors, 'ad', [(z * N_X + x, z * N_X + (x ^ s)) for z in ra...  12.9 us
    ppermute x4, starting transfers between devices, swap(): return lax.ppermute(array, 'tp', [(j, j ^ mask) for j in range(n_tp)])  12.3 us
    all_to_all x1, blocking collectives, local(): parts = lax.all_to_all(parts, 'tp', 0, 0, tiled=True)  10.4 us
    ppermute x3, starting transfers between devices, local(): lax.ppermute(factors, 'ad', [(z * N_X + x, z * N_X + (x ^ s)) for z in ra...  9.82 us
    all_to_all x1, starting transfers between devices, local(): lax.all_to_all(delta.reshape(n_z, cap, columns), 'ad', 0, 0, axis_index_g...  9.55 us
    pallas_call x5, Pallas kernels, call(): pl.pallas_call(kernel, out_shape=out_shape, compiler_params=pltpu.Compile...  5.53 us
    all_to_all x1, waiting for transfers between devices, local(): lax.all_to_all(delta.reshape(n_z, cap, columns), 'ad', 0, 0, axis_index_g...  3.96 us
  transfers between devices with their start and end apart: 10, of which 6 were waited for; matrix products, arithmetic and copies ran while one was open for 0% of the time, Pallas kernels for 3%

profile of v6, /device:TPU:6, one launch (start us, length us, event | category | flops | bytes accessed | tf_op | source)
XLA Modules:
  0.0 91.4 jit_solution(16674262819981435319)
XLA Ops:
  0.0 2.4 %shard_map.64 = (bf16[16,136,128]{2,1,0:T(8,128)(2,1)}, s32[8,256]{1,0:T(8,128)S(1)}, bf16[320,512]{1,0:T(8,128)(2,1)S(1)}) custom-call(s32[1,64]{1,0:T(1,128)} %refs_0_.1, s32[1,64]{1,0:T(1,128)} %bitcast.6, bf16[256,512]{1,0:T(8,128)(2,1)} %tokens_ref.1, bf16[256,512]{1,0:T(8,128)(2,1)} %bitcast.5, bf16[8,16,256]{2,1,0:T(8,128)(2,1)} %refs_4_.1), custom_call_target="tpu_custom_call" | custom-call | tf_op jit(solution)/shard_map/pallas_call | solution.py:252
  2.4 3.8 %collective-permute-start.3 = (bf16[320,512]{1,0:T(8,128)(2,1)S(1)}, bf16[320,512]{1,0:T(8,128)(2,1)S(1)}, u32[]{:S(2)}, u32[]{:S(2)}) collective-permute-start(bf16[320,512]{1,0:T(8,128)(2,1)S(1)} %get-tuple-element.20.refs_1_.refs_2_), channel_id=1, source_target_pairs={{0,4},{1,5},{2,6},{3,7},{4,8},{5,9},{6,10},{7,11},{8,12},{9,13},{1... | collective-permute-start | bytes 983048 | tf_op jit(solution)/shard_map/ppermute | solution.py:290
  6.2 14.3 %all-to-all-start = ((bf16[16,136,128]{2,1,0:T(8,128)(2,1)}), bf16[16,136,128]{2,1,0:T(8,128)(2,1)S(1)}, u32[]{:S(2)}, u32[]{:S(2)}) async-start(bf16[16,136,128]{2,1,0:T(8,128)(2,1)} %get-tuple-element.19), calls=%async_computation | async-start | bytes 1114112 | tf_op jit(solution)/shard_map/all_to_all | solution.py:282
  20.5 1.0 %collective-permute-done.3.place_ref.refs_5_.refs_6_ = bf16[320,512]{1,0:T(8,128)(2,1)S(1)} collective-permute-done((bf16[320,512]{1,0:T(8,128)(2,1)S(1)}, bf16[320,512]{1,0:T(8,128)(2,1)S(1)}, u32[]{:S(2)}, u32[]{:S(2)}) %collective-permute-start.3) | collective-permute-done | bytes 327712 | tf_op jit(solution)/shard_map/ppermute | solution.py:290
  21.5 2.4 %shard_map.65 = (bf16[4,256,256]{2,1,0:T(8,128)(2,1)S(1)}, bf16[4,256,256]{2,1,0:T(8,128)(2,1)S(1)}) custom-call(bf16[320,512]{1,0:T(8,128)(2,1)S(1)} %collective-permute-done.3.place_ref.refs_5_.refs_6_, bf16[256,512]{1,0:T(8,128)(2,1)} %tokens_ref.1, bf16[512,2048]{1,0:T(8,128)(2,1)} %weight_ref.1), custom_call_target="tpu_custom_call" | custom-call | flops 40000000000 | bytes 131072 | tf_op jit(solution)/shard_map/pallas_call | solution.py:214
  23.9 1.9 %collective-permute-start.4 = (bf16[4,256,256]{2,1,0:T(8,128)(2,1)S(1)}, bf16[4,256,256]{2,1,0:T(8,128)(2,1)S(1)}, u32[]{:S(2)}, u32[]{:S(2)}) collective-permute-start(bf16[4,256,256]{2,1,0:T(8,128)(2,1)S(1)} %get-tuple-element.21), channel_id=1, source_target_pairs={{0,64},{64,0},{128,192},{192,128},{256,320},{320,256},{384,448},{4... | collective-permute-start | bytes 1572872 | tf_op jit(solution)/shard_map/ppermute | solution.py:297
  25.8 2.4 %collective-permute-start.2 = (bf16[320,512]{1,0:T(8,128)(2,1)S(1)}, bf16[320,512]{1,0:T(8,128)(2,1)S(1)}, u32[]{:S(2)}, u32[]{:S(2)}) collective-permute-start(bf16[320,512]{1,0:T(8,128)(2,1)S(1)} %get-tuple-element.20.refs_1_.refs_2_), channel_id=1, source_target_pairs={{0,3},{1,2},{2,1},{3,0},{4,7},{5,6},{6,5},{7,4},{8,11},{9,10},{10,... | collective-permute-start | bytes 983048 | tf_op jit(solution)/shard_map/ppermute | solution.py:284
  28.2 4.3 %collective-permute-start.1 = (bf16[320,512]{1,0:T(8,128)(2,1)S(1)}, bf16[320,512]{1,0:T(8,128)(2,1)S(1)}, u32[]{:S(2)}, u32[]{:S(2)}) collective-permute-start(bf16[320,512]{1,0:T(8,128)(2,1)S(1)} %get-tuple-element.20.refs_1_.refs_2_), channel_id=1, source_target_pairs={{0,2},{1,3},{2,0},{3,1},{4,6},{5,7},{6,4},{7,5},{8,10},{9,11},{10,... | collective-permute-start | bytes 983048 | tf_op jit(solution)/shard_map/ppermute | solution.py:284
  32.6 3.1 %collective-permute-start = (bf16[320,512]{1,0:T(8,128)(2,1)S(1)}, bf16[320,512]{1,0:T(8,128)(2,1)S(1)}, u32[]{:S(2)}, u32[]{:S(2)}) collective-permute-start(bf16[320,512]{1,0:T(8,128)(2,1)S(1)} %get-tuple-element.20.refs_1_.refs_2_), channel_id=1, source_target_pairs={{0,1},{1,0},{2,3},{3,2},{4,5},{5,4},{6,7},{7,6},{8,9},{9,8},{10,11... | collective-permute-start | bytes 983048 | tf_op jit(solution)/shard_map/ppermute | solution.py:284
  35.7 10.4 %collective-permute-done.2.refs_4_.refs_5_ = bf16[320,512]{1,0:T(8,128)(2,1)S(1)} collective-permute-done((bf16[320,512]{1,0:T(8,128)(2,1)S(1)}, bf16[320,512]{1,0:T(8,128)(2,1)S(1)}, u32[]{:S(2)}, u32[]{:S(2)}) %collective-permute-start.2) | collective-permute-done | bytes 327712 | tf_op jit(solution)/shard_map/ppermute | solution.py:284
  46.1 0.0 collective-permute-done.1.refs_3_.refs_4_
  46.1 2.5 %collective-permute-done.refs_2_.refs_3_ = bf16[320,512]{1,0:T(8,128)(2,1)S(1)} collective-permute-done((bf16[320,512]{1,0:T(8,128)(2,1)S(1)}, bf16[320,512]{1,0:T(8,128)(2,1)S(1)}, u32[]{:S(2)}, u32[]{:S(2)}) %collective-permute-start) | collective-permute-done | bytes 327712 | tf_op jit(solution)/shard_map/ppermute | solution.py:284
  48.6 0.0 collective-permute-done.4.refs_6_.recv_ref
  48.6 1.5 %all-to-all-done.refs_0_ = bf16[16,136,128]{2,1,0:T(8,128)(2,1)S(1)} async-done(((bf16[16,136,128]{2,1,0:T(8,128)(2,1)}), bf16[16,136,128]{2,1,0:T(8,128)(2,1)S(1)}, u32[]{:S(2)}, u32[]{:S(2)}) %all-to-all-start) | async-done | bytes 557088 | tf_op jit(solution)/shard_map/all_to_all | solution.py:282
  50.1 0.9 %shard_map.66 = (bf16[8,16,512]{2,1,0:T(8,128)(2,1)S(1)}, f32[8,512]{1,0:T(8,128)S(1)}) custom-call(bf16[16,136,128]{2,1,0:T(8,128)(2,1)S(1)} %all-to-all-done.refs_0_, bf16[320,512]{1,0:T(8,128)(2,1)S(1)} %get-tuple-element.20.refs_1_.refs_2_, bf16[320,512]{1,0:T(8,128)(2,1)S(1)} %collective-permute-done.refs_2_.refs_3_, ...), custom_call_target="tpu_custom_call" | custom-call | tf_op jit(solution)/shard_map/pallas_call | solution.py:214
  51.1 10.4 %all_to_all.15.refs_0_ = bf16[8,16,512]{2,1,0:T(8,128)(2,1)S(1)} all-to-all(bf16[8,16,512]{2,1,0:T(8,128)(2,1)S(1)} %get-tuple-element.22), channel_id=1, replica_groups=mesh['tp'=8,'ad'=64] {'tp'}, dimensions={0} | all-to-all | bytes 262144 | tf_op jit(solution)/shard_map/all_to_all | solution.py:316
  61.5 1.1 %shard_map.67 = (bf16[512,256]{1,0:T(8,128)(2,1)}, f32[8,128]{1,0:T(8,128)S(1)}) custom-call(bf16[8,16,512]{2,1,0:T(8,128)(2,1)S(1)} %all_to_all.15.refs_0_, f32[8,512]{1,0:T(8,128)S(1)} %get-tuple-element.23.refs_1_, bf16[320,512]{1,0:T(8,128)(2,1)S(1)} %get-tuple-element.20.refs_1_.refs_2_, bf16[320,512]{1,0:T(8,128)(2,1)S(1)} %collective-permute-done.refs_2_.refs_3_, ...), custom_call_target="tpu_custom_call" | custom-call | tf_op jit(solution)/shard_map/pallas_call | solution.py:214
  62.6 9.6 %all-to-all-start.2 = ((bf16[16,32,256]{2,1,0:T(8,128)(2,1)}), bf16[16,32,256]{2,1,0:T(8,128)(2,1)S(1)}, u32[]{:S(2)}, u32[]{:S(2)}) async-start(bf16[16,32,256]{2,1,0:T(8,128)(2,1)} %bitcast.2), calls=%async_computation.2 | async-start | bytes 524288 | tf_op jit(solution)/shard_map/all_to_all | solution.py:332
  72.2 0.1 shard_map.68
  72.3 3.1 %collective-permute-start.5 = (bf16[1,256,256]{2,1,0:T(8,128)(2,1)S(1)}, bf16[1,256,256]{2,1,0:T(8,128)(2,1)S(1)}, u32[]{:S(2)}, u32[]{:S(2)}) collective-permute-start(bf16[1,256,256]{2,1,0:T(8,128)(2,1)S(1)} %get-tuple-element.28), channel_id=1, source_target_pairs={{0,384},{64,448},{128,256},{192,320},{256,128},{320,192},{384,0},{... | collective-permute-start | bytes 393224 | tf_op jit(solution)/shard_map/ppermute | solution.py:297
  75.4 1.9 %collective-permute-start.6 = (bf16[1,256,256]{2,1,0:T(8,128)(2,1)S(1)}, bf16[1,256,256]{2,1,0:T(8,128)(2,1)S(1)}, u32[]{:S(2)}, u32[]{:S(2)}) collective-permute-start(bf16[1,256,256]{2,1,0:T(8,128)(2,1)S(1)} %get-tuple-element.29), channel_id=1, source_target_pairs={{0,128},{64,192},{128,0},{192,64},{256,384},{320,448},{384,256},{4... | collective-permute-start | bytes 393224 | tf_op jit(solution)/shard_map/ppermute | solution.py:297
  77.3 5.4 %collective-permute-start.7 = (bf16[1,256,256]{2,1,0:T(8,128)(2,1)S(1)}, bf16[1,256,256]{2,1,0:T(8,128)(2,1)S(1)}, u32[]{:S(2)}, u32[]{:S(2)}) collective-permute-start(bf16[1,256,256]{2,1,0:T(8,128)(2,1)S(1)} %get-tuple-element.30), channel_id=1, source_target_pairs={{0,256},{64,320},{128,384},{192,448},{256,0},{320,64},{384,128},{4... | collective-permute-start | bytes 393224 | tf_op jit(solution)/shard_map/ppermute | solution.py:297
  82.7 0.0 collective-permute-done.5.r0_ref
  82.8 0.0 collective-permute-done.6.r1_ref
  82.8 3.8 %collective-permute-done.7.r2_ref = bf16[1,256,256]{2,1,0:T(8,128)(2,1)S(1)} collective-permute-done((bf16[1,256,256]{2,1,0:T(8,128)(2,1)S(1)}, bf16[1,256,256]{2,1,0:T(8,128)(2,1)S(1)}, u32[]{:S(2)}, u32[]{:S(2)}) %collective-permute-start.7) | collective-permute-done | bytes 131104 | tf_op jit(solution)/shard_map/ppermute | solution.py:297
  86.6 4.0 %all-to-all-done.2 = bf16[16,32,256]{2,1,0:T(8,128)(2,1)S(1)} async-done(((bf16[16,32,256]{2,1,0:T(8,128)(2,1)}), bf16[16,32,256]{2,1,0:T(8,128)(2,1)S(1)}, u32[]{:S(2)}, u32[]{:S(2)}) %all-to-all-start.2) | async-done | bytes 262176 | tf_op jit(solution)/shard_map/all_to_all | solution.py:332
  90.5 0.9 %shard_map.69 = bf16[256,256]{1,0:T(8,128)(2,1)} custom-call(s32[8,256]{1,0:T(8,128)S(1)} %get-tuple-element.18.place_ref, bf16[512,256]{1,0:T(8,128)(2,1)S(1)} %bitcast.4, f32[1,256,256]{2,1,0:T(8,128)S(1)} %get-tuple-element.27.kept_ref, bf16[1,256,256]{2,1,0:T(8,128)(2,1)S(1)} %collective-permute-done.5.r0_ref, ...), custom_call_target="tpu_custom_call" | custom-call | tf_op jit(solution)/shard_map/pallas_call | solution.py:214
Async XLA Ops:
  2.4 19.1 %collective-permute-start.3 = (bf16[320,512]{1,0:T(8,128)(2,1)S(1)}, bf16[320,512]{1,0:T(8,128)(2,1)S(1)}, u32[]{:S(2)}, u32[]{:S(2)}) collective-permute-start(bf16[320,512]{1,0:T(8,128)(2,1)S(1)} %get-tuple-element.20.refs_1_.refs_2_), channel_id=1, source_target_pairs={{0,4},{1,5},{2,6},{3,7},{4,8},{5,9},{6,10},{7,11},{8,12},{9,13},{1... | collective-permute-start | bytes 983048 | tf_op jit(solution)/shard_map/ppermute | solution.py:290
  6.2 43.9 %all-to-all-start = ((bf16[16,136,128]{2,1,0:T(8,128)(2,1)}), bf16[16,136,128]{2,1,0:T(8,128)(2,1)S(1)}, u32[]{:S(2)}, u32[]{:S(2)}) async-start(bf16[16,136,128]{2,1,0:T(8,128)(2,1)} %get-tuple-element.19), calls=%async_computation | async-start | bytes 1114112 | tf_op jit(solution)/shard_map/all_to_all | solution.py:282
  23.9 24.7 %collective-permute-start.4 = (bf16[4,256,256]{2,1,0:T(8,128)(2,1)S(1)}, bf16[4,256,256]{2,1,0:T(8,128)(2,1)S(1)}, u32[]{:S(2)}, u32[]{:S(2)}) collective-permute-start(bf16[4,256,256]{2,1,0:T(8,128)(2,1)S(1)} %get-tuple-element.21), channel_id=1, source_target_pairs={{0,64},{64,0},{128,192},{192,128},{256,320},{320,256},{384,448},{4... | collective-permute-start | bytes 1572872 | tf_op jit(solution)/shard_map/ppermute | solution.py:297
  25.8 20.2 %collective-permute-start.2 = (bf16[320,512]{1,0:T(8,128)(2,1)S(1)}, bf16[320,512]{1,0:T(8,128)(2,1)S(1)}, u32[]{:S(2)}, u32[]{:S(2)}) collective-permute-start(bf16[320,512]{1,0:T(8,128)(2,1)S(1)} %get-tuple-element.20.refs_1_.refs_2_), channel_id=1, source_target_pairs={{0,3},{1,2},{2,1},{3,0},{4,7},{5,6},{6,5},{7,4},{8,11},{9,10},{10,... | collective-permute-start | bytes 983048 | tf_op jit(solution)/shard_map/ppermute | solution.py:284
  28.2 17.9 %collective-permute-start.1 = (bf16[320,512]{1,0:T(8,128)(2,1)S(1)}, bf16[320,512]{1,0:T(8,128)(2,1)S(1)}, u32[]{:S(2)}, u32[]{:S(2)}) collective-permute-start(bf16[320,512]{1,0:T(8,128)(2,1)S(1)} %get-tuple-element.20.refs_1_.refs_2_), channel_id=1, source_target_pairs={{0,2},{1,3},{2,0},{3,1},{4,6},{5,7},{6,4},{7,5},{8,10},{9,11},{10,... | collective-permute-start | bytes 983048 | tf_op jit(solution)/shard_map/ppermute | solution.py:284
  32.6 16.0 %collective-permute-start = (bf16[320,512]{1,0:T(8,128)(2,1)S(1)}, bf16[320,512]{1,0:T(8,128)(2,1)S(1)}, u32[]{:S(2)}, u32[]{:S(2)}) collective-permute-start(bf16[320,512]{1,0:T(8,128)(2,1)S(1)} %get-tuple-element.20.refs_1_.refs_2_), channel_id=1, source_target_pairs={{0,1},{1,0},{2,3},{3,2},{4,5},{5,4},{6,7},{7,6},{8,9},{9,8},{10,11... | collective-permute-start | bytes 983048 | tf_op jit(solution)/shard_map/ppermute | solution.py:284
  62.6 27.9 %all-to-all-start.2 = ((bf16[16,32,256]{2,1,0:T(8,128)(2,1)}), bf16[16,32,256]{2,1,0:T(8,128)(2,1)S(1)}, u32[]{:S(2)}, u32[]{:S(2)}) async-start(bf16[16,32,256]{2,1,0:T(8,128)(2,1)} %bitcast.2), calls=%async_computation.2 | async-start | bytes 524288 | tf_op jit(solution)/shard_map/all_to_all | solution.py:332
  72.3 10.5 %collective-permute-start.5 = (bf16[1,256,256]{2,1,0:T(8,128)(2,1)S(1)}, bf16[1,256,256]{2,1,0:T(8,128)(2,1)S(1)}, u32[]{:S(2)}, u32[]{:S(2)}) collective-permute-start(bf16[1,256,256]{2,1,0:T(8,128)(2,1)S(1)} %get-tuple-element.28), channel_id=1, source_target_pairs={{0,384},{64,448},{128,256},{192,320},{256,128},{320,192},{384,0},{... | collective-permute-start | bytes 393224 | tf_op jit(solution)/shard_map/ppermute | solution.py:297
  75.4 7.4 %collective-permute-start.6 = (bf16[1,256,256]{2,1,0:T(8,128)(2,1)S(1)}, bf16[1,256,256]{2,1,0:T(8,128)(2,1)S(1)}, u32[]{:S(2)}, u32[]{:S(2)}) collective-permute-start(bf16[1,256,256]{2,1,0:T(8,128)(2,1)S(1)} %get-tuple-element.29), channel_id=1, source_target_pairs={{0,128},{64,192},{128,0},{192,64},{256,384},{320,448},{384,256},{4... | collective-permute-start | bytes 393224 | tf_op jit(solution)/shard_map/ppermute | solution.py:297
  77.3 9.2 %collective-permute-start.7 = (bf16[1,256,256]{2,1,0:T(8,128)(2,1)S(1)}, bf16[1,256,256]{2,1,0:T(8,128)(2,1)S(1)}, u32[]{:S(2)}, u32[]{:S(2)}) collective-permute-start(bf16[1,256,256]{2,1,0:T(8,128)(2,1)S(1)} %get-tuple-element.30), channel_id=1, source_target_pairs={{0,256},{64,320},{128,384},{192,448},{256,0},{320,64},{384,128},{4... | collective-permute-start | bytes 393224 | tf_op jit(solution)/shard_map/ppermute | solution.py:297

commit v7 on v6

--- a/solution.py
+++ b/solution.py
@@ -199,15 +199,19 @@
     mark_ref[...] = jnp.zeros(mark_ref.shape, F32)
 
 
-def mix_kernel(place_ref, back_ref, kept_ref, r0_ref, r1_ref, r2_ref, out_ref):
-    rows = out_ref.shape[0]
-    place = place_ref[0:1, :]
-    select = (iota((back_ref.shape[0], rows), 0) == place).astype(F32).astype(BF16)
-    delta = lax.dot_general(select, back_ref[...], TN, preferred_element_type=F32)
+def ready_kernel(place_ref, kept_ref, r0_ref, r1_ref, r2_ref, base_ref, select_ref):
     base = kept_ref[0]
     for recv_ref in (r0_ref, r1_ref, r2_ref):
         base = base + recv_ref[0].astype(F32)
-    out_ref[...] = (base + ADAPTER_SCALE * delta).astype(BF16)
+    base_ref[...] = base
+    places, rows = select_ref.shape[1], select_ref.shape[0]
+    select = (iota((places, rows), 0) == place_ref[0:1, :]).astype(F32)
+    select_ref[...] = select.T.astype(BF16)
+
+
+def mix_kernel(back_ref, base_ref, select_ref, out_ref):
+    delta = jnp.dot(select_ref[...], back_ref[...], preferred_element_type=F32)
+    out_ref[...] = (base_ref[...] + ADAPTER_SCALE * delta).astype(BF16)
 
 
 def call(kernel, out_shape, *args, cost=None):
@@ -332,12 +336,22 @@
     back = lax.all_to_all(
         delta.reshape(n_z, cap, columns), "ad", 0, 0, axis_index_groups=along_z, tiled=True
     )
+    base, select = call(
+        ready_kernel,
+        (
+            jax.ShapeDtypeStruct((tok_rows, columns), F32),
+            jax.ShapeDtypeStruct((tok_rows, rows), BF16),
+        ),
+        place,
+        *shares,
+        cost=pl.CostEstimate(flops=10**9, bytes_accessed=tokens.size, transcendentals=0),
+    )
     return call(
         mix_kernel,
         jax.ShapeDtypeStruct((tok_rows, columns), BF16),
-        place,
         back.reshape(rows, columns),
-        *shares,
+        base,
+        select,
     )
 
 

time: 92 us -> 92 us (level)
    pallas_call x5 -> x6, Pallas kernels: 5.53 us -> 5.65 us  [call(): pl.pallas_call(kernel, out_shape=out_shape, compiler_params=pltpu.Compile...]
where the time goes in v7:
time: 92 us; the launch traced here: 91.4 us
  starting transfers between devices  49.9 us (54%)
  waiting for transfers between devices  23 us (25%)
  blocking collectives  10.4 us (11%)
  Pallas kernels  8.01 us (9%)
    all_to_all x1, starting transfers between devices, local(): lax.all_to_all(send, 'ad', 0, 0, axis_index_groups=along_z, tiled=True)  14.3 us
    ppermute x3, waiting for transfers between devices, local(): lax.ppermute(factors, 'ad', [(z * N_X + x, z * N_X + (x ^ s)) for z in ra...  12.9 us
    ppermute x4, starting transfers between devices, swap(): return lax.ppermute(array, 'tp', [(j, j ^ mask) for j in range(n_tp)])  12.3 us
    all_to_all x1, blocking collectives, local(): parts = lax.all_to_all(parts, 'tp', 0, 0, tiled=True)  10.4 us
    ppermute x3, starting transfers between devices, local(): lax.ppermute(factors, 'ad', [(z * N_X + x, z * N_X + (x ^ s)) for z in ra...  9.82 us
    all_to_all x1, starting transfers between devices, local(): lax.all_to_all(delta.reshape(n_z, cap, columns), 'ad', 0, 0, axis_index_g...  9.56 us
    pallas_call x6, Pallas kernels, call(): pl.pallas_call(kernel, out_shape=out_shape, compiler_params=pltpu.Compile...  5.65 us
    ppermute x1, starting transfers between devices, local(): lax.ppermute(factors[0], 'ad', [(z * N_X + x, (z + CHAIN) % n_z * N_X + x...  3.82 us
  transfers between devices with their start and end apart: 10, of which 6 were waited for; matrix products, arithmetic and copies ran while one was open for 0% of the time, Pallas kernels for 3%

profile of v7, /device:TPU:6, one launch (start us, length us, event | category | flops | bytes accessed | tf_op | source)
XLA Modules:
  0.0 91.4 jit_solution(6417149685851941120)
XLA Ops:
  0.0 2.4 %shard_map.64 = (bf16[16,136,128]{2,1,0:T(8,128)(2,1)}, s32[8,256]{1,0:T(8,128)S(1)}, bf16[320,512]{1,0:T(8,128)(2,1)S(1)}) custom-call(s32[1,64]{1,0:T(1,128)} %refs_0_.1, s32[1,64]{1,0:T(1,128)} %bitcast.6, bf16[256,512]{1,0:T(8,128)(2,1)} %tokens_ref.1, bf16[256,512]{1,0:T(8,128)(2,1)} %bitcast.5, bf16[8,16,256]{2,1,0:T(8,128)(2,1)} %refs_4_.1), custom_call_target="tpu_custom_call" | custom-call | tf_op jit(solution)/shard_map/pallas_call | solution.py:256
  2.4 3.8 %collective-permute-start.3 = (bf16[320,512]{1,0:T(8,128)(2,1)S(1)}, bf16[320,512]{1,0:T(8,128)(2,1)S(1)}, u32[]{:S(2)}, u32[]{:S(2)}) collective-permute-start(bf16[320,512]{1,0:T(8,128)(2,1)S(1)} %get-tuple-element.21.refs_1_.refs_2_), channel_id=1, source_target_pairs={{0,4},{1,5},{2,6},{3,7},{4,8},{5,9},{6,10},{7,11},{8,12},{9,13},{1... | collective-permute-start | bytes 983048 | tf_op jit(solution)/shard_map/ppermute | solution.py:294
  6.2 14.3 %all-to-all-start = ((bf16[16,136,128]{2,1,0:T(8,128)(2,1)}), bf16[16,136,128]{2,1,0:T(8,128)(2,1)S(1)}, u32[]{:S(2)}, u32[]{:S(2)}) async-start(bf16[16,136,128]{2,1,0:T(8,128)(2,1)} %get-tuple-element.20), calls=%async_computation | async-start | bytes 1114112 | tf_op jit(solution)/shard_map/all_to_all | solution.py:286
  20.5 1.0 %collective-permute-done.3.place_ref.refs_5_.refs_6_ = bf16[320,512]{1,0:T(8,128)(2,1)S(1)} collective-permute-done((bf16[320,512]{1,0:T(8,128)(2,1)S(1)}, bf16[320,512]{1,0:T(8,128)(2,1)S(1)}, u32[]{:S(2)}, u32[]{:S(2)}) %collective-permute-start.3) | collective-permute-done | bytes 327712 | tf_op jit(solution)/shard_map/ppermute | solution.py:294
  21.5 2.4 %shard_map.65 = (bf16[4,256,256]{2,1,0:T(8,128)(2,1)S(1)}, bf16[4,256,256]{2,1,0:T(8,128)(2,1)S(1)}) custom-call(bf16[320,512]{1,0:T(8,128)(2,1)S(1)} %collective-permute-done.3.place_ref.refs_5_.refs_6_, bf16[256,512]{1,0:T(8,128)(2,1)} %tokens_ref.1, bf16[512,2048]{1,0:T(8,128)(2,1)} %weight_ref.1), custom_call_target="tpu_custom_call" | custom-call | flops 40000000000 | bytes 131072 | tf_op jit(solution)/shard_map/pallas_call | solution.py:218
  23.9 1.9 %collective-permute-start.4 = (bf16[4,256,256]{2,1,0:T(8,128)(2,1)S(1)}, bf16[4,256,256]{2,1,0:T(8,128)(2,1)S(1)}, u32[]{:S(2)}, u32[]{:S(2)}) collective-permute-start(bf16[4,256,256]{2,1,0:T(8,128)(2,1)S(1)} %get-tuple-element.22), channel_id=1, source_target_pairs={{0,64},{64,0},{128,192},{192,128},{256,320},{320,256},{384,448},{4... | collective-permute-start | bytes 1572872 | tf_op jit(solution)/shard_map/ppermute | solution.py:301
  25.8 2.4 %collective-permute-start.2 = (bf16[320,512]{1,0:T(8,128)(2,1)S(1)}, bf16[320,512]{1,0:T(8,128)(2,1)S(1)}, u32[]{:S(2)}, u32[]{:S(2)}) collective-permute-start(bf16[320,512]{1,0:T(8,128)(2,1)S(1)} %get-tuple-element.21.refs_1_.refs_2_), channel_id=1, source_target_pairs={{0,3},{1,2},{2,1},{3,0},{4,7},{5,6},{6,5},{7,4},{8,11},{9,10},{10,... | collective-permute-start | bytes 983048 | tf_op jit(solution)/shard_map/ppermute | solution.py:288
  28.2 4.3 %collective-permute-start.1 = (bf16[320,512]{1,0:T(8,128)(2,1)S(1)}, bf16[320,512]{1,0:T(8,128)(2,1)S(1)}, u32[]{:S(2)}, u32[]{:S(2)}) collective-permute-start(bf16[320,512]{1,0:T(8,128)(2,1)S(1)} %get-tuple-element.21.refs_1_.refs_2_), channel_id=1, source_target_pairs={{0,2},{1,3},{2,0},{3,1},{4,6},{5,7},{6,4},{7,5},{8,10},{9,11},{10,... | collective-permute-start | bytes 983048 | tf_op jit(solution)/shard_map/ppermute | solution.py:288
  32.6 3.1 %collective-permute-start = (bf16[320,512]{1,0:T(8,128)(2,1)S(1)}, bf16[320,512]{1,0:T(8,128)(2,1)S(1)}, u32[]{:S(2)}, u32[]{:S(2)}) collective-permute-start(bf16[320,512]{1,0:T(8,128)(2,1)S(1)} %get-tuple-element.21.refs_1_.refs_2_), channel_id=1, source_target_pairs={{0,1},{1,0},{2,3},{3,2},{4,5},{5,4},{6,7},{7,6},{8,9},{9,8},{10,11... | collective-permute-start | bytes 983048 | tf_op jit(solution)/shard_map/ppermute | solution.py:288
  35.7 10.4 %collective-permute-done.2.refs_4_.refs_5_ = bf16[320,512]{1,0:T(8,128)(2,1)S(1)} collective-permute-done((bf16[320,512]{1,0:T(8,128)(2,1)S(1)}, bf16[320,512]{1,0:T(8,128)(2,1)S(1)}, u32[]{:S(2)}, u32[]{:S(2)}) %collective-permute-start.2) | collective-permute-done | bytes 327712 | tf_op jit(solution)/shard_map/ppermute | solution.py:288
  46.1 0.0 collective-permute-done.1.refs_3_.refs_4_
  46.1 2.5 %collective-permute-done.refs_2_.refs_3_ = bf16[320,512]{1,0:T(8,128)(2,1)S(1)} collective-permute-done((bf16[320,512]{1,0:T(8,128)(2,1)S(1)}, bf16[320,512]{1,0:T(8,128)(2,1)S(1)}, u32[]{:S(2)}, u32[]{:S(2)}) %collective-permute-start) | collective-permute-done | bytes 327712 | tf_op jit(solution)/shard_map/ppermute | solution.py:288
  48.6 0.0 collective-permute-done.4.refs_6_.recv_ref
  48.6 1.5 %all-to-all-done.refs_0_ = bf16[16,136,128]{2,1,0:T(8,128)(2,1)S(1)} async-done(((bf16[16,136,128]{2,1,0:T(8,128)(2,1)}), bf16[16,136,128]{2,1,0:T(8,128)(2,1)S(1)}, u32[]{:S(2)}, u32[]{:S(2)}) %all-to-all-start) | async-done | bytes 557088 | tf_op jit(solution)/shard_map/all_to_all | solution.py:286
  50.1 0.9 %shard_map.66 = (bf16[8,16,512]{2,1,0:T(8,128)(2,1)S(1)}, f32[8,512]{1,0:T(8,128)S(1)}) custom-call(bf16[16,136,128]{2,1,0:T(8,128)(2,1)S(1)} %all-to-all-done.refs_0_, bf16[320,512]{1,0:T(8,128)(2,1)S(1)} %get-tuple-element.21.refs_1_.refs_2_, bf16[320,512]{1,0:T(8,128)(2,1)S(1)} %collective-permute-done.refs_2_.refs_3_, ...), custom_call_target="tpu_custom_call" | custom-call | tf_op jit(solution)/shard_map/pallas_call | solution.py:218
  51.1 10.4 %all_to_all.15.refs_0_ = bf16[8,16,512]{2,1,0:T(8,128)(2,1)S(1)} all-to-all(bf16[8,16,512]{2,1,0:T(8,128)(2,1)S(1)} %get-tuple-element.23), channel_id=1, replica_groups=mesh['tp'=8,'ad'=64] {'tp'}, dimensions={0} | all-to-all | bytes 262144 | tf_op jit(solution)/shard_map/all_to_all | solution.py:320
  61.5 1.1 %shard_map.67 = (bf16[512,256]{1,0:T(8,128)(2,1)}, f32[8,128]{1,0:T(8,128)S(1)}) custom-call(bf16[8,16,512]{2,1,0:T(8,128)(2,1)S(1)} %all_to_all.15.refs_0_, f32[8,512]{1,0:T(8,128)S(1)} %get-tuple-element.24.refs_1_, bf16[320,512]{1,0:T(8,128)(2,1)S(1)} %get-tuple-element.21.refs_1_.refs_2_, bf16[320,512]{1,0:T(8,128)(2,1)S(1)} %collective-permute-done.refs_2_.refs_3_, ...), custom_call_target="tpu_custom_call" | custom-call | tf_op jit(solution)/shard_map/pallas_call | solution.py:218
  62.6 9.6 %all-to-all-start.2 = ((bf16[16,32,256]{2,1,0:T(8,128)(2,1)}), bf16[16,32,256]{2,1,0:T(8,128)(2,1)S(1)}, u32[]{:S(2)}, u32[]{:S(2)}) async-start(bf16[16,32,256]{2,1,0:T(8,128)(2,1)} %bitcast.2), calls=%async_computation.2 | async-start | bytes 524288 | tf_op jit(solution)/shard_map/all_to_all | solution.py:336
  72.2 0.1 shard_map.68
  72.3 3.1 %collective-permute-start.5 = (bf16[1,256,256]{2,1,0:T(8,128)(2,1)S(1)}, bf16[1,256,256]{2,1,0:T(8,128)(2,1)S(1)}, u32[]{:S(2)}, u32[]{:S(2)}) collective-permute-start(bf16[1,256,256]{2,1,0:T(8,128)(2,1)S(1)} %get-tuple-element.30), channel_id=1, source_target_pairs={{0,384},{64,448},{128,256},{192,320},{256,128},{320,192},{384,0},{... | collective-permute-start | bytes 393224 | tf_op jit(solution)/shard_map/ppermute | solution.py:301
  75.4 1.9 %collective-permute-start.6 = (bf16[1,256,256]{2,1,0:T(8,128)(2,1)S(1)}, bf16[1,256,256]{2,1,0:T(8,128)(2,1)S(1)}, u32[]{:S(2)}, u32[]{:S(2)}) collective-permute-start(bf16[1,256,256]{2,1,0:T(8,128)(2,1)S(1)} %get-tuple-element.31), channel_id=1, source_target_pairs={{0,128},{64,192},{128,0},{192,64},{256,384},{320,448},{384,256},{4... | collective-permute-start | bytes 393224 | tf_op jit(solution)/shard_map/ppermute | solution.py:301
  77.3 5.4 %collective-permute-start.7 = (bf16[1,256,256]{2,1,0:T(8,128)(2,1)S(1)}, bf16[1,256,256]{2,1,0:T(8,128)(2,1)S(1)}, u32[]{:S(2)}, u32[]{:S(2)}) collective-permute-start(bf16[1,256,256]{2,1,0:T(8,128)(2,1)S(1)} %get-tuple-element.32), channel_id=1, source_target_pairs={{0,256},{64,320},{128,384},{192,448},{256,0},{320,64},{384,128},{4... | collective-permute-start | bytes 393224 | tf_op jit(solution)/shard_map/ppermute | solution.py:301
  82.7 0.0 collective-permute-done.5.r0_ref
  82.7 0.0 collective-permute-done.6.r1_ref
  82.8 3.8 %collective-permute-done.7.r2_ref = bf16[1,256,256]{2,1,0:T(8,128)(2,1)S(1)} collective-permute-done((bf16[1,256,256]{2,1,0:T(8,128)(2,1)S(1)}, bf16[1,256,256]{2,1,0:T(8,128)(2,1)S(1)}, u32[]{:S(2)}, u32[]{:S(2)}) %collective-permute-start.7) | collective-permute-done | bytes 131104 | tf_op jit(solution)/shard_map/ppermute | solution.py:301
  86.5 0.2 shard_map.69
  86.7 3.8 %all-to-all-done.2 = bf16[16,32,256]{2,1,0:T(8,128)(2,1)S(1)} async-done(((bf16[16,32,256]{2,1,0:T(8,128)(2,1)}), bf16[16,32,256]{2,1,0:T(8,128)(2,1)S(1)}, u32[]{:S(2)}, u32[]{:S(2)}) %all-to-all-start.2) | async-done | bytes 262176 | tf_op jit(solution)/shard_map/all_to_all | solution.py:336
  90.5 0.9 shard_map.70
Async XLA Ops:
  2.4 19.1 %collective-permute-start.3 = (bf16[320,512]{1,0:T(8,128)(2,1)S(1)}, bf16[320,512]{1,0:T(8,128)(2,1)S(1)}, u32[]{:S(2)}, u32[]{:S(2)}) collective-permute-start(bf16[320,512]{1,0:T(8,128)(2,1)S(1)} %get-tuple-element.21.refs_1_.refs_2_), channel_id=1, source_target_pairs={{0,4},{1,5},{2,6},{3,7},{4,8},{5,9},{6,10},{7,11},{8,12},{9,13},{1... | collective-permute-start | bytes 983048 | tf_op jit(solution)/shard_map/ppermute | solution.py:294
  6.2 43.9 %all-to-all-start = ((bf16[16,136,128]{2,1,0:T(8,128)(2,1)}), bf16[16,136,128]{2,1,0:T(8,128)(2,1)S(1)}, u32[]{:S(2)}, u32[]{:S(2)}) async-start(bf16[16,136,128]{2,1,0:T(8,128)(2,1)} %get-tuple-element.20), calls=%async_computation | async-start | bytes 1114112 | tf_op jit(solution)/shard_map/all_to_all | solution.py:286
  23.9 24.7 %collective-permute-start.4 = (bf16[4,256,256]{2,1,0:T(8,128)(2,1)S(1)}, bf16[4,256,256]{2,1,0:T(8,128)(2,1)S(1)}, u32[]{:S(2)}, u32[]{:S(2)}) collective-permute-start(bf16[4,256,256]{2,1,0:T(8,128)(2,1)S(1)} %get-tuple-element.22), channel_id=1, source_target_pairs={{0,64},{64,0},{128,192},{192,128},{256,320},{320,256},{384,448},{4... | collective-permute-start | bytes 1572872 | tf_op jit(solution)/shard_map/ppermute | solution.py:301
  25.8 20.2 %collective-permute-start.2 = (bf16[320,512]{1,0:T(8,128)(2,1)S(1)}, bf16[320,512]{1,0:T(8,128)(2,1)S(1)}, u32[]{:S(2)}, u32[]{:S(2)}) collective-permute-start(bf16[320,512]{1,0:T(8,128)(2,1)S(1)} %get-tuple-element.21.refs_1_.refs_2_), channel_id=1, source_target_pairs={{0,3},{1,2},{2,1},{3,0},{4,7},{5,6},{6,5},{7,4},{8,11},{9,10},{10,... | collective-permute-start | bytes 983048 | tf_op jit(solution)/shard_map/ppermute | solution.py:288
  28.2 17.9 %collective-permute-start.1 = (bf16[320,512]{1,0:T(8,128)(2,1)S(1)}, bf16[320,512]{1,0:T(8,128)(2,1)S(1)}, u32[]{:S(2)}, u32[]{:S(2)}) collective-permute-start(bf16[320,512]{1,0:T(8,128)(2,1)S(1)} %get-tuple-element.21.refs_1_.refs_2_), channel_id=1, source_target_pairs={{0,2},{1,3},{2,0},{3,1},{4,6},{5,7},{6,4},{7,5},{8,10},{9,11},{10,... | collective-permute-start | bytes 983048 | tf_op jit(solution)/shard_map/ppermute | solution.py:288
  32.6 16.0 %collective-permute-start = (bf16[320,512]{1,0:T(8,128)(2,1)S(1)}, bf16[320,512]{1,0:T(8,128)(2,1)S(1)}, u32[]{:S(2)}, u32[]{:S(2)}) collective-permute-start(bf16[320,512]{1,0:T(8,128)(2,1)S(1)} %get-tuple-element.21.refs_1_.refs_2_), channel_id=1, source_target_pairs={{0,1},{1,0},{2,3},{3,2},{4,5},{5,4},{6,7},{7,6},{8,9},{9,8},{10,11... | collective-permute-start | bytes 983048 | tf_op jit(solution)/shard_map/ppermute | solution.py:288
  62.6 27.9 %all-to-all-start.2 = ((bf16[16,32,256]{2,1,0:T(8,128)(2,1)}), bf16[16,32,256]{2,1,0:T(8,128)(2,1)S(1)}, u32[]{:S(2)}, u32[]{:S(2)}) async-start(bf16[16,32,256]{2,1,0:T(8,128)(2,1)} %bitcast.2), calls=%async_computation.2 | async-start | bytes 524288 | tf_op jit(solution)/shard_map/all_to_all | solution.py:336
  72.3 10.5 %collective-permute-start.5 = (bf16[1,256,256]{2,1,0:T(8,128)(2,1)S(1)}, bf16[1,256,256]{2,1,0:T(8,128)(2,1)S(1)}, u32[]{:S(2)}, u32[]{:S(2)}) collective-permute-start(bf16[1,256,256]{2,1,0:T(8,128)(2,1)S(1)} %get-tuple-element.30), channel_id=1, source_target_pairs={{0,384},{64,448},{128,256},{192,320},{256,128},{320,192},{384,0},{... | collective-permute-start | bytes 393224 | tf_op jit(solution)/shard_map/ppermute | solution.py:301
  75.4 7.4 %collective-permute-start.6 = (bf16[1,256,256]{2,1,0:T(8,128)(2,1)S(1)}, bf16[1,256,256]{2,1,0:T(8,128)(2,1)S(1)}, u32[]{:S(2)}, u32[]{:S(2)}) collective-permute-start(bf16[1,256,256]{2,1,0:T(8,128)(2,1)S(1)} %get-tuple-element.31), channel_id=1, source_target_pairs={{0,128},{64,192},{128,0},{192,64},{256,384},{320,448},{384,256},{4... | collective-permute-start | bytes 393224 | tf_op jit(solution)/shard_map/ppermute | solution.py:301
  77.3 9.2 %collective-permute-start.7 = (bf16[1,256,256]{2,1,0:T(8,128)(2,1)S(1)}, bf16[1,256,256]{2,1,0:T(8,128)(2,1)S(1)}, u32[]{:S(2)}, u32[]{:S(2)}) collective-permute-start(bf16[1,256,256]{2,1,0:T(8,128)(2,1)S(1)} %get-tuple-element.32), channel_id=1, source_target_pairs={{0,256},{64,320},{128,384},{192,448},{256,0},{320,64},{384,128},{4... | collective-permute-start | bytes 393224 | tf_op jit(solution)/shard_map/ppermute | solution.py:301

commit v8 on v5

--- a/solution.py
+++ b/solution.py
@@ -15,6 +15,7 @@
 NT = (((1,), (1,)), ((), ()))
 TN = (((0,), (0,)), ((), ()))
 LANES = 128
+PIECES = 4
 VMEM_LIMIT = 48 * 1024 * 1024
 
 
@@ -25,8 +26,8 @@
 def pack_kernel(
     planes, cap, stored,
     lens_hbm, index_hbm, tokens_hbm, down_hbm, up_hbm,
-    send_ref, place_ref, factors_hbm,
-    lens_ref, index_ref, tokens_ref, block_ref, up_ref, sems,
+    send_hbm, place_ref, factors_hbm,
+    lens_ref, index_ref, tokens_ref, block_ref, up_ref, send_ref, sems,
 ):
     requests = lens_ref.shape[1]
     rows, width = tokens_ref.shape
@@ -99,17 +100,28 @@
     put = copy(block_ref, factors_hbm, 5)
 
     get_tokens.wait()
-    packed = jnp.dot(select, tokens_ref[...], preferred_element_type=F32)
-    blocks = width // LANES
-    for c in range(blocks):
-        block = packed[:, c * LANES : (c + 1) * LANES].reshape(planes, cap, LANES)
-        send_ref[:, c * cap : (c + 1) * cap, :] = block.astype(BF16)
     at_rank = (iota((LANES, rows), 0).astype(F32) == rank_in).astype(F32).astype(BF16)
     ids = lax.dot_general(
         jnp.where(member, local, 0.0).astype(BF16), at_rank, NT, preferred_element_type=F32
     )
     ids = jnp.broadcast_to(ids.reshape(planes, 1, LANES), (planes, 8, LANES))
+    blocks = width // LANES
     send_ref[:, blocks * cap :, :] = ids.astype(BF16)
+    sends = []
+    part = planes // PIECES
+    for k in range(PIECES):
+        packed = jnp.dot(
+            select[k * part * cap : (k + 1) * part * cap],
+            tokens_ref[...],
+            preferred_element_type=F32,
+        )
+        for c in range(blocks):
+            block = packed[:, c * LANES : (c + 1) * LANES].reshape(part, cap, LANES)
+            send_ref[k * part : (k + 1) * part, c * cap : (c + 1) * cap, :] = block.astype(BF16)
+        piece = pl.ds(k * part, part)
+        sends.append(copy(send_ref.at[piece], send_hbm.at[piece], 6 + k))
+    for send in sends:
+        send.wait()
     put.wait()
 
 
@@ -178,7 +190,7 @@
 
 def delta_kernel(
     stored, parts_ref, lane_ids_ref, f0_ref, f1_ref, f2_ref, f3_ref,
-    handed_ref, out_ref, mark_ref
+    handed_ref, out_hbm, mark_ref, out_ref, sems
 ):
     low = parts_ref[0].astype(F32)
     for j in range(1, parts_ref.shape[0]):
@@ -193,10 +205,22 @@
             for pair in range(stored // 2):
                 a = float(x * stored + 2 * pair + side)
                 spread.append(jnp.where(ids == a, low, 0.0).astype(BF16))
-    product = lax.dot_general(
-        jnp.concatenate(spread, axis=0), jnp.concatenate(up, axis=0), TN, preferred_element_type=F32
-    )
-    out_ref[...] = product.astype(BF16)
+    spread = jnp.concatenate(spread, axis=0)
+    up = jnp.concatenate(up, axis=0)
+    part = out_ref.shape[0] // PIECES
+    puts = []
+    for k in range(PIECES):
+        piece = slice(k * part, (k + 1) * part)
+        product = lax.dot_general(spread[:, piece], up, TN, preferred_element_type=F32)
+        out_ref[piece, :] = product.astype(BF16)
+        puts.append(
+            pltpu.make_async_copy(
+                out_ref.at[pl.ds(k * part, part)], out_hbm.at[pl.ds(k * part, part)], sems.at[k]
+            )
+        )
+        puts[-1].start()
+    for put in puts:
+        put.wait()
     mark_ref[...] = jnp.zeros(mark_ref.shape, F32)
 
 
@@ -256,14 +280,15 @@
             jax.ShapeDtypeStruct((block_rows, width), BF16),
         ),
         in_specs=[hbm] * 5,
-        out_specs=(vmem, vmem, hbm),
+        out_specs=(hbm, vmem, hbm),
         scratch_shapes=[
             pltpu.VMEM((1, lengths.shape[1]), jnp.int32),
             pltpu.VMEM((1, lengths.shape[1]), jnp.int32),
             pltpu.VMEM((tok_rows, width), BF16),
             pltpu.VMEM((block_rows, width), BF16),
             pltpu.VMEM((stored, rank, columns), BF16),
-            pltpu.SemaphoreType.DMA((6,)),
+            pltpu.VMEM((n_z, width // LANES * cap + 8, LANES), BF16),
+            pltpu.SemaphoreType.DMA((6 + PIECES,)),
         ],
         compiler_params=pltpu.CompilerParams(vmem_limit_bytes=VMEM_LIMIT),
     )(
@@ -313,17 +338,20 @@
         out_recv,
     )
     parts = lax.all_to_all(parts, "tp", 0, 0, tiled=True)
-    delta, mark = call(
+    delta, mark = pl.pallas_call(
         apply_up,
-        (
+        out_shape=(
             jax.ShapeDtypeStruct((rows, columns), BF16),
             jax.ShapeDtypeStruct((8, LANES), F32),
         ),
-        parts,
-        lane_ids,
-        *factors,
-        handed,
-    )
+        in_specs=[vmem] * 7,
+        out_specs=(hbm, vmem),
+        scratch_shapes=[
+            pltpu.VMEM((rows, columns), BF16),
+            pltpu.SemaphoreType.DMA((PIECES,)),
+        ],
+        compiler_params=pltpu.CompilerParams(vmem_limit_bytes=VMEM_LIMIT),
+    )(parts, lane_ids, *factors, handed)
     keep, out = call(halve_kernel, (blocks(2, F32), blocks(2, BF16)), mark, keep, out_recv)
     keep, out = call(halve_kernel, (blocks(1, F32), blocks(1, BF16)), mark, keep, swap(out, 2))
     base_recv = swap(out, 6)

time: 92 us -> 91.9 us (level)
    pallas_call x6 -> x5, Pallas kernels: 5.57 us -> 4.44 us  [call(): pl.pallas_call(kernel, out_shape=out_shape, compiler_params=pltpu.Compile...]
    pallas_call x0 -> x1, Pallas kernels: none -> 1.09 us  [local(): pl.pallas_call(apply_up, out_shape=(jax.ShapeDtypeStruct((rows, columns),...]
where the time goes in v8:
time: 91.9 us; the launch traced here: 91.4 us
  starting transfers between devices  45 us (49%)
  waiting for transfers between devices  28 us (30%)
  blocking collectives  10.4 us (11%)
  Pallas kernels  7.84 us (9%)
    all_to_all x1, starting transfers between devices, local(): lax.all_to_all(send, 'ad', 0, 0, axis_index_groups=along_z, tiled=True)  14.3 us
    ppermute x3, waiting for transfers between devices, local(): lax.ppermute(factors, 'ad', [(z * N_X + x, z * N_X + (x ^ s)) for z in ra...  12.9 us
    ppermute x3, waiting for transfers between devices, swap(): return lax.ppermute(array, 'tp', [(j, j ^ mask) for j in range(n_tp)])  12 us
    all_to_all x1, blocking collectives, local(): parts = lax.all_to_all(parts, 'tp', 0, 0, tiled=True)  10.4 us
    ppermute x3, starting transfers between devices, local(): lax.ppermute(factors, 'ad', [(z * N_X + x, z * N_X + (x ^ s)) for z in ra...  9.82 us
    all_to_all x1, starting transfers between devices, local(): lax.all_to_all(delta.reshape(n_z, cap, columns), 'ad', 0, 0, axis_index_g...  9.57 us
    ppermute x3, starting transfers between devices, swap(): return lax.ppermute(array, 'tp', [(j, j ^ mask) for j in range(n_tp)])  7.47 us
    pallas_call x5, Pallas kernels, call(): pl.pallas_call(kernel, out_shape=out_shape, compiler_params=pltpu.Compile...  4.44 us
  transfers between devices with their start and end apart: 9, of which 7 were waited for; matrix products, arithmetic and copies ran while one was open for 0% of the time, Pallas kernels for 3%

profile of v8, /device:TPU:6, one launch (start us, length us, event | category | flops | bytes accessed | tf_op | source)
XLA Modules:
  0.0 91.4 jit_solution(1431286404820126657)
XLA Ops:
  0.0 2.3 %shard_map.64 = (bf16[16,136,128]{2,1,0:T(8,128)(2,1)}, s32[8,256]{1,0:T(8,128)S(1)}, bf16[320,512]{1,0:T(8,128)(2,1)S(1)}) custom-call(s32[1,64]{1,0:T(1,128)} %refs_0_.1, s32[1,64]{1,0:T(1,128)} %bitcast.6, bf16[256,512]{1,0:T(8,128)(2,1)} %tokens_ref.1, bf16[256,512]{1,0:T(8,128)(2,1)} %bitcast.5, bf16[8,16,256]{2,1,0:T(8,128)(2,1)} %refs_4_.1), custom_call_target="tpu_custom_call" | custom-call | tf_op jit(solution)/shard_map/pallas_call | solution.py:275
  2.3 3.8 %collective-permute-start.3 = (bf16[320,512]{1,0:T(8,128)(2,1)S(1)}, bf16[320,512]{1,0:T(8,128)(2,1)S(1)}, u32[]{:S(2)}, u32[]{:S(2)}) collective-permute-start(bf16[320,512]{1,0:T(8,128)(2,1)S(1)} %get-tuple-element.20.refs_1_.refs_2_), channel_id=1, source_target_pairs={{0,4},{1,5},{2,6},{3,7},{4,8},{5,9},{6,10},{7,11},{8,12},{9,13},{1... | collective-permute-start | bytes 983048 | tf_op jit(solution)/shard_map/ppermute | solution.py:314
  6.2 14.3 %all-to-all-start = ((bf16[16,136,128]{2,1,0:T(8,128)(2,1)}), bf16[16,136,128]{2,1,0:T(8,128)(2,1)S(1)}, u32[]{:S(2)}, u32[]{:S(2)}) async-start(bf16[16,136,128]{2,1,0:T(8,128)(2,1)} %get-tuple-element.19), calls=%async_computation | async-start | bytes 1114112 | tf_op jit(solution)/shard_map/all_to_all | solution.py:306
  20.5 1.0 %collective-permute-done.3.place_ref.refs_5_.refs_6_ = bf16[320,512]{1,0:T(8,128)(2,1)S(1)} collective-permute-done((bf16[320,512]{1,0:T(8,128)(2,1)S(1)}, bf16[320,512]{1,0:T(8,128)(2,1)S(1)}, u32[]{:S(2)}, u32[]{:S(2)}) %collective-permute-start.3) | collective-permute-done | bytes 327712 | tf_op jit(solution)/shard_map/ppermute | solution.py:314
  21.4 2.4 %shard_map.65 = (bf16[4,256,256]{2,1,0:T(8,128)(2,1)S(1)}, bf16[4,256,256]{2,1,0:T(8,128)(2,1)S(1)}) custom-call(bf16[320,512]{1,0:T(8,128)(2,1)S(1)} %collective-permute-done.3.place_ref.refs_5_.refs_6_, bf16[256,512]{1,0:T(8,128)(2,1)} %tokens_ref.1, bf16[512,2048]{1,0:T(8,128)(2,1)} %weight_ref.1), custom_call_target="tpu_custom_call" | custom-call | flops 40000000000 | bytes 131072 | tf_op jit(solution)/shard_map/pallas_call | solution.py:237
  23.9 1.9 %collective-permute-start.4 = (bf16[4,256,256]{2,1,0:T(8,128)(2,1)S(1)}, bf16[4,256,256]{2,1,0:T(8,128)(2,1)S(1)}, u32[]{:S(2)}, u32[]{:S(2)}) collective-permute-start(bf16[4,256,256]{2,1,0:T(8,128)(2,1)S(1)} %get-tuple-element.21), channel_id=1, source_target_pairs={{0,64},{64,0},{128,192},{192,128},{256,320},{320,256},{384,448},{4... | collective-permute-start | bytes 1572872 | tf_op jit(solution)/shard_map/ppermute | solution.py:321
  25.8 2.4 %collective-permute-start.2 = (bf16[320,512]{1,0:T(8,128)(2,1)S(1)}, bf16[320,512]{1,0:T(8,128)(2,1)S(1)}, u32[]{:S(2)}, u32[]{:S(2)}) collective-permute-start(bf16[320,512]{1,0:T(8,128)(2,1)S(1)} %get-tuple-element.20.refs_1_.refs_2_), channel_id=1, source_target_pairs={{0,3},{1,2},{2,1},{3,0},{4,7},{5,6},{6,5},{7,4},{8,11},{9,10},{10,... | collective-permute-start | bytes 983048 | tf_op jit(solution)/shard_map/ppermute | solution.py:308
  28.2 4.3 %collective-permute-start.1 = (bf16[320,512]{1,0:T(8,128)(2,1)S(1)}, bf16[320,512]{1,0:T(8,128)(2,1)S(1)}, u32[]{:S(2)}, u32[]{:S(2)}) collective-permute-start(bf16[320,512]{1,0:T(8,128)(2,1)S(1)} %get-tuple-element.20.refs_1_.refs_2_), channel_id=1, source_target_pairs={{0,2},{1,3},{2,0},{3,1},{4,6},{5,7},{6,4},{7,5},{8,10},{9,11},{10,... | collective-permute-start | bytes 983048 | tf_op jit(solution)/shard_map/ppermute | solution.py:308
  32.5 3.1 %collective-permute-start = (bf16[320,512]{1,0:T(8,128)(2,1)S(1)}, bf16[320,512]{1,0:T(8,128)(2,1)S(1)}, u32[]{:S(2)}, u32[]{:S(2)}) collective-permute-start(bf16[320,512]{1,0:T(8,128)(2,1)S(1)} %get-tuple-element.20.refs_1_.refs_2_), channel_id=1, source_target_pairs={{0,1},{1,0},{2,3},{3,2},{4,5},{5,4},{6,7},{7,6},{8,9},{9,8},{10,11... | collective-permute-start | bytes 983048 | tf_op jit(solution)/shard_map/ppermute | solution.py:308
  35.6 10.4 %collective-permute-done.2.refs_4_.refs_5_ = bf16[320,512]{1,0:T(8,128)(2,1)S(1)} collective-permute-done((bf16[320,512]{1,0:T(8,128)(2,1)S(1)}, bf16[320,512]{1,0:T(8,128)(2,1)S(1)}, u32[]{:S(2)}, u32[]{:S(2)}) %collective-permute-start.2) | collective-permute-done | bytes 327712 | tf_op jit(solution)/shard_map/ppermute | solution.py:308
  46.0 0.0 collective-permute-done.1.refs_3_.refs_4_
  46.0 2.5 %collective-permute-done.refs_2_.refs_3_ = bf16[320,512]{1,0:T(8,128)(2,1)S(1)} collective-permute-done((bf16[320,512]{1,0:T(8,128)(2,1)S(1)}, bf16[320,512]{1,0:T(8,128)(2,1)S(1)}, u32[]{:S(2)}, u32[]{:S(2)}) %collective-permute-start) | collective-permute-done | bytes 327712 | tf_op jit(solution)/shard_map/ppermute | solution.py:308
  48.6 0.0 collective-permute-done.4.refs_6_.recv_ref
  48.6 1.5 %all-to-all-done.refs_0_ = bf16[16,136,128]{2,1,0:T(8,128)(2,1)S(1)} async-done(((bf16[16,136,128]{2,1,0:T(8,128)(2,1)}), bf16[16,136,128]{2,1,0:T(8,128)(2,1)S(1)}, u32[]{:S(2)}, u32[]{:S(2)}) %all-to-all-start) | async-done | bytes 557088 | tf_op jit(solution)/shard_map/all_to_all | solution.py:306
  50.1 0.9 %shard_map.66 = (bf16[8,16,512]{2,1,0:T(8,128)(2,1)S(1)}, f32[8,512]{1,0:T(8,128)S(1)}) custom-call(bf16[16,136,128]{2,1,0:T(8,128)(2,1)S(1)} %all-to-all-done.refs_0_, bf16[320,512]{1,0:T(8,128)(2,1)S(1)} %get-tuple-element.20.refs_1_.refs_2_, bf16[320,512]{1,0:T(8,128)(2,1)S(1)} %collective-permute-done.refs_2_.refs_3_, ...), custom_call_target="tpu_custom_call" | custom-call | tf_op jit(solution)/shard_map/pallas_call | solution.py:237
  51.0 10.4 %all_to_all.15.refs_0_ = bf16[8,16,512]{2,1,0:T(8,128)(2,1)S(1)} all-to-all(bf16[8,16,512]{2,1,0:T(8,128)(2,1)S(1)} %get-tuple-element.22), channel_id=1, replica_groups=mesh['tp'=8,'ad'=64] {'tp'}, dimensions={0} | all-to-all | bytes 262144 | tf_op jit(solution)/shard_map/all_to_all | solution.py:340
  61.4 1.1 %shard_map.67 = (bf16[512,256]{1,0:T(8,128)(2,1)}, f32[8,128]{1,0:T(8,128)S(1)}) custom-call(bf16[8,16,512]{2,1,0:T(8,128)(2,1)S(1)} %all_to_all.15.refs_0_, f32[8,512]{1,0:T(8,128)S(1)} %get-tuple-element.23.refs_1_, bf16[320,512]{1,0:T(8,128)(2,1)S(1)} %get-tuple-element.20.refs_1_.refs_2_, bf16[320,512]{1,0:T(8,128)(2,1)S(1)} %collective-permute-done.refs_2_.refs_3_, ...), custom_call_target="tpu_custom_call" | custom-call | tf_op jit(solution)/shard_map/pallas_call | solution.py:341
  62.5 9.6 %all-to-all-start.2 = ((bf16[16,32,256]{2,1,0:T(8,128)(2,1)}), bf16[16,32,256]{2,1,0:T(8,128)(2,1)S(1)}, u32[]{:S(2)}, u32[]{:S(2)}) async-start(bf16[16,32,256]{2,1,0:T(8,128)(2,1)} %bitcast.2), calls=%async_computation.2 | async-start | bytes 524288 | tf_op jit(solution)/shard_map/all_to_all | solution.py:358
  72.1 0.1 shard_map.68
  72.2 2.5 %collective-permute-start.5 = (bf16[2,256,256]{2,1,0:T(8,128)(2,1)S(1)}, bf16[2,256,256]{2,1,0:T(8,128)(2,1)S(1)}, u32[]{:S(2)}, u32[]{:S(2)}) collective-permute-start(bf16[2,256,256]{2,1,0:T(8,128)(2,1)S(1)} %get-tuple-element.28), channel_id=1, source_target_pairs={{0,128},{64,192},{128,0},{192,64},{256,384},{320,448},{384,256},{4... | collective-permute-start | bytes 786440 | tf_op jit(solution)/shard_map/ppermute | solution.py:321
  74.7 7.0 %collective-permute-done.5.recv_ref = bf16[2,256,256]{2,1,0:T(8,128)(2,1)S(1)} collective-permute-done((bf16[2,256,256]{2,1,0:T(8,128)(2,1)S(1)}, bf16[2,256,256]{2,1,0:T(8,128)(2,1)S(1)}, u32[]{:S(2)}, u32[]{:S(2)}) %collective-permute-start.5) | collective-permute-done | bytes 262176 | tf_op jit(solution)/shard_map/ppermute | solution.py:321
  81.7 3.1 %collective-permute-start.6 = (bf16[1,256,256]{2,1,0:T(8,128)(2,1)S(1)}, bf16[1,256,256]{2,1,0:T(8,128)(2,1)S(1)}, u32[]{:S(2)}, u32[]{:S(2)}) collective-permute-start(bf16[1,256,256]{2,1,0:T(8,128)(2,1)S(1)} %get-tuple-element.30), channel_id=1, source_target_pairs={{0,384},{64,448},{128,256},{192,320},{256,128},{320,192},{384,0},{... | collective-permute-start | bytes 393224 | tf_op jit(solution)/shard_map/ppermute | solution.py:321
  84.8 5.0 %collective-permute-done.6.recv_ref = bf16[1,256,256]{2,1,0:T(8,128)(2,1)S(1)} collective-permute-done((bf16[1,256,256]{2,1,0:T(8,128)(2,1)S(1)}, bf16[1,256,256]{2,1,0:T(8,128)(2,1)S(1)}, u32[]{:S(2)}, u32[]{:S(2)}) %collective-permute-start.6) | collective-permute-done | bytes 131104 | tf_op jit(solution)/shard_map/ppermute | solution.py:321
  89.8 0.6 all-to-all-done.2
  90.4 0.9 %shard_map.70 = bf16[256,256]{1,0:T(8,128)(2,1)} custom-call(s32[8,256]{1,0:T(8,128)S(1)} %get-tuple-element.18.place_ref, bf16[512,256]{1,0:T(8,128)(2,1)S(1)} %bitcast.4, f32[1,256,256]{2,1,0:T(8,128)S(1)} %get-tuple-element.29.kept_ref, bf16[1,256,256]{2,1,0:T(8,128)(2,1)S(1)} %collective-permute-done.6.recv_ref), custom_call_target="tpu_custom_call" | custom-call | tf_op jit(solution)/shard_map/pallas_call | solution.py:237
  (1 shorter events, 0.0 us)
Async XLA Ops:
  2.3 19.1 %collective-permute-start.3 = (bf16[320,512]{1,0:T(8,128)(2,1)S(1)}, bf16[320,512]{1,0:T(8,128)(2,1)S(1)}, u32[]{:S(2)}, u32[]{:S(2)}) collective-permute-start(bf16[320,512]{1,0:T(8,128)(2,1)S(1)} %get-tuple-element.20.refs_1_.refs_2_), channel_id=1, source_target_pairs={{0,4},{1,5},{2,6},{3,7},{4,8},{5,9},{6,10},{7,11},{8,12},{9,13},{1... | collective-permute-start | bytes 983048 | tf_op jit(solution)/shard_map/ppermute | solution.py:314
  6.2 43.9 %all-to-all-start = ((bf16[16,136,128]{2,1,0:T(8,128)(2,1)}), bf16[16,136,128]{2,1,0:T(8,128)(2,1)S(1)}, u32[]{:S(2)}, u32[]{:S(2)}) async-start(bf16[16,136,128]{2,1,0:T(8,128)(2,1)} %get-tuple-element.19), calls=%async_computation | async-start | bytes 1114112 | tf_op jit(solution)/shard_map/all_to_all | solution.py:306
  23.9 24.7 %collective-permute-start.4 = (bf16[4,256,256]{2,1,0:T(8,128)(2,1)S(1)}, bf16[4,256,256]{2,1,0:T(8,128)(2,1)S(1)}, u32[]{:S(2)}, u32[]{:S(2)}) collective-permute-start(bf16[4,256,256]{2,1,0:T(8,128)(2,1)S(1)} %get-tuple-element.21), channel_id=1, source_target_pairs={{0,64},{64,0},{128,192},{192,128},{256,320},{320,256},{384,448},{4... | collective-permute-start | bytes 1572872 | tf_op jit(solution)/shard_map/ppermute | solution.py:321
  25.8 20.2 %collective-permute-start.2 = (bf16[320,512]{1,0:T(8,128)(2,1)S(1)}, bf16[320,512]{1,0:T(8,128)(2,1)S(1)}, u32[]{:S(2)}, u32[]{:S(2)}) collective-permute-start(bf16[320,512]{1,0:T(8,128)(2,1)S(1)} %get-tuple-element.20.refs_1_.refs_2_), channel_id=1, source_target_pairs={{0,3},{1,2},{2,1},{3,0},{4,7},{5,6},{6,5},{7,4},{8,11},{9,10},{10,... | collective-permute-start | bytes 983048 | tf_op jit(solution)/shard_map/ppermute | solution.py:308
  28.2 17.9 %collective-permute-start.1 = (bf16[320,512]{1,0:T(8,128)(2,1)S(1)}, bf16[320,512]{1,0:T(8,128)(2,1)S(1)}, u32[]{:S(2)}, u32[]{:S(2)}) collective-permute-start(bf16[320,512]{1,0:T(8,128)(2,1)S(1)} %get-tuple-element.20.refs_1_.refs_2_), channel_id=1, source_target_pairs={{0,2},{1,3},{2,0},{3,1},{4,6},{5,7},{6,4},{7,5},{8,10},{9,11},{10,... | collective-permute-start | bytes 983048 | tf_op jit(solution)/shard_map/ppermute | solution.py:308
  32.5 16.1 %collective-permute-start = (bf16[320,512]{1,0:T(8,128)(2,1)S(1)}, bf16[320,512]{1,0:T(8,128)(2,1)S(1)}, u32[]{:S(2)}, u32[]{:S(2)}) collective-permute-start(bf16[320,512]{1,0:T(8,128)(2,1)S(1)} %get-tuple-element.20.refs_1_.refs_2_), channel_id=1, source_target_pairs={{0,1},{1,0},{2,3},{3,2},{4,5},{5,4},{6,7},{7,6},{8,9},{9,8},{10,11... | collective-permute-start | bytes 983048 | tf_op jit(solution)/shard_map/ppermute | solution.py:308
  62.5 27.9 %all-to-all-start.2 = ((bf16[16,32,256]{2,1,0:T(8,128)(2,1)}), bf16[16,32,256]{2,1,0:T(8,128)(2,1)S(1)}, u32[]{:S(2)}, u32[]{:S(2)}) async-start(bf16[16,32,256]{2,1,0:T(8,128)(2,1)} %bitcast.2), calls=%async_computation.2 | async-start | bytes 524288 | tf_op jit(solution)/shard_map/all_to_all | solution.py:358
  72.2 9.5 %collective-permute-start.5 = (bf16[2,256,256]{2,1,0:T(8,128)(2,1)S(1)}, bf16[2,256,256]{2,1,0:T(8,128)(2,1)S(1)}, u32[]{:S(2)}, u32[]{:S(2)}) collective-permute-start(bf16[2,256,256]{2,1,0:T(8,128)(2,1)S(1)} %get-tuple-element.28), channel_id=1, source_target_pairs={{0,128},{64,192},{128,0},{192,64},{256,384},{320,448},{384,256},{4... | collective-permute-start | bytes 786440 | tf_op jit(solution)/shard_map/ppermute | solution.py:321
  81.7 8.1 %collective-permute-start.6 = (bf16[1,256,256]{2,1,0:T(8,128)(2,1)S(1)}, bf16[1,256,256]{2,1,0:T(8,128)(2,1)S(1)}, u32[]{:S(2)}, u32[]{:S(2)}) collective-permute-start(bf16[1,256,256]{2,1,0:T(8,128)(2,1)S(1)} %get-tuple-element.30), channel_id=1, source_target_pairs={{0,384},{64,448},{128,256},{192,320},{256,128},{320,192},{384,0},{... | collective-permute-start | bytes 393224 | tf_op jit(solution)/shard_map/ppermute | solution.py:321
